TPU v7x, 32 devices: a whole 2x2x4 slice. The times are simulated.
32 devices in a mesh: grp: 2 (over x), own: 16 (over z, y, core).
Axes of the slice: x: 2, y: 2, z: 4, core: 2. Of those that a mesh axis runs over, the one named last changes fastest.
Arguments:
- tokens: bfloat16 [4096, 8192], P(('grp', 'own')), parts along dimension 0, may hold values from -6 to 6
- adapter_index_rows: int32 [4096, 1], P(('grp', 'own')), parts along dimension 0, may hold values from 0 to 31; in each aligned block of 128 rows (0 to 127, 128 to 255, ...) at most 8 rows name the same one
- adapter_pool_position: int32 [64], P('grp'), parts along dimension 0, may hold values from 0 to 31, each once
- base_value_matrix: bfloat16 [8192, 512], replicated, may hold values from -0.0625 to 0.0625
- lowrank_down_weight: bfloat16 [64, 64, 8192], P(('grp', 'own')), parts along dimension 0, may hold values from -0.0625 to 0.0625
- lowrank_up_weight: bfloat16 [64, 64, 512], P(('grp', 'own')), parts along dimension 0, may hold values from -0.75 to 0.75
Outputs:
- values_out: bfloat16 [4096, 512], P(('grp', 'own')), parts along dimension 0
There are 2 independent parts, one for each index of `grp`. A program takes and returns all parts, laid end to end along the dimension named above; an argument that names none is the same for every part. Nothing has to cross between parts.
Inputs may be any that keep to these rules, and one draw needn't show every extreme that they name: `adapter_index_rows`: among the rows of one device no adapter is named by more than 8 rows; some adapter is named by exactly 8 rows of some device. `adapter_pool_position`: each slot holds one adapter; slot s lies on the device of index s // 2 along own.
All inputs are finite; a program needn't handle non-finite values.
Results may differ from a plain program's by a relative error of at most 0.0051.
Values may be sent and summed in bfloat16 or wider, within the bound.
No kernel may reach another device: no remote copies, remote signals or barrier semaphores. Data moves between devices by JAX's collectives and lax.ppermute only.
A program may use at most 64 MiB of HBM per device.

v0:
```python
import jax
import jax.numpy as jnp
from jax import lax
from jax.sharding import PartitionSpec as P


def apply_lowrank_adapters(request_block, lowrank_down_weight, lowrank_up_weight):
    reduced_rows = jnp.einsum(
        "ubzs,bis->ubzi", request_block, lowrank_down_weight, preferred_element_type=jnp.float32
    ).astype(jnp.bfloat16)
    return jnp.einsum(
        "zgpw,gwy->zgpy", reduced_rows, lowrank_up_weight, preferred_element_type=jnp.float32
    ).astype(jnp.bfloat16)


def local(
    tokens,
    adapter_index_rows,
    adapter_pool_position,
    base_value_matrix,
    lowrank_down_weight,
    lowrank_up_weight,
):
    rows, width = tokens.shape
    owners = lax.axis_size("own")
    rows_by_holder = lowrank_down_weight.shape[0]
    total = adapter_pool_position.shape[0]
    depth = max(2, 2 * rows // total)
    out_width = base_value_matrix.shape[1]
    chosen = adapter_index_rows[:, 0]
    table = jnp.arange(total, dtype=jnp.int32)
    slot = jnp.sum(
        jnp.where(chosen[:, None] == table[None, :], adapter_pool_position[None, :], 0), axis=1
    )
    places = jnp.arange(rows, dtype=jnp.int32)
    earlier = (slot[:, None] == slot[None, :]) & (places[None, :] < places[:, None])
    within = jnp.sum(earlier.astype(jnp.int32), axis=1)
    target = slot * depth + within
    outbound_rows = jnp.zeros((total * depth, width), tokens.dtype).at[target].set(tokens)
    outbound_rows = outbound_rows.reshape(owners, rows_by_holder, depth, width)
    computed = apply_lowrank_adapters(
        lax.all_to_all(outbound_rows, "own", split_axis=0, concat_axis=0, tiled=True),
        lowrank_down_weight,
        lowrank_up_weight,
    )
    returned = lax.all_to_all(computed, "own", split_axis=0, concat_axis=0, tiled=True)
    base = jnp.dot(tokens, base_value_matrix, preferred_element_type=jnp.float32)
    delta_rows = returned.reshape(total * depth, out_width)[target]
    return (base + delta_rows.astype(jnp.float32)).astype(jnp.bfloat16)


def solution(mesh):
    in_specs = (
        P(("grp", "own"), None),
        P(("grp", "own"), None),
        P("grp"),
        P(),
        P(("grp", "own"), None, None),
        P(("grp", "own"), None, None),
    )
    out_specs = P(("grp", "own"), None)
    return jax.shard_map(local, mesh=mesh, in_specs=in_specs, out_specs=out_specs, check_vma=False)
```

profile of v0, /device:TPU:0, one launch (start us, length us, event | category | flops | bytes accessed | tf_op | source)
XLA Modules:
  0.0 134.4 jit_solution(8053923143949591781)
XLA Ops:
  0.0 0.0 copy-start
  0.0 0.9 select_reduce_fusion
  0.9 0.2 convert_reduce_fusion
  1.1 7.0 %scatter_custom_fusion = bf16[256,8192]{1,0:T(8,128)(2,1)} fusion(s32[128]{0:T(128)S(1)} %fusion.23, bf16[128,8192]{1,0:T(8,128)(2,1)} %param.6, bf16[]{:T(256)} %constant.4.clone.1), kind=kCustom, calls=%fused_computation.5 | custom fusion | bytes 4194816 | tf_op jit(solution)/shard_map/scatter | solution.py:39
  8.1 0.0 copy-start.1
  8.1 99.9 %all_to_all.10 = bf16[16,2,8,8192]{3,2,1,0:T(8,128)(2,1)} all-to-all(bf16[16,2,8,8192]{3,2,1,0:T(8,128)(2,1)} %bitcast.31), channel_id=1, replica_groups=mesh['grp'=2,'own'=16] {'own'}, dimensions={0} | all-to-all | bytes 8388608 | tf_op jit(solution)/shard_map/all_to_all | solution.py:42
  108.0 0.0 copy-done
  108.0 0.0 copy-done.1
  108.0 3.6 %fusion.5 = bf16[16,2,8,512]{3,2,0,1:T(8,128)(2,1)S(1)} fusion(bf16[2,64,8192]{2,1,0:T(8,128)(2,1)S(1)} %copy-done, bf16[16,2,8,8192]{3,2,1,0:T(8,128)(2,1)} %all_to_all.10, bf16[2,64,512]{2,1,0:T(8,128)(2,1)S(1)} %copy-done.1), kind=kOutput, calls=%fused_computation.8 | convolution fusion | flops 285360128 | bytes 6684672 | tf_op jit(solution)/shard_map/zgpw,gwy->zgpy/dot_general | solution.py:11
  111.6 0.7 copy.14
  112.3 5.3 %all-to-all-start.1 = ((bf16[16,2,8,512]{3,2,1,0:T(8,128)(2,1)}), bf16[16,2,8,512]{3,2,1,0:T(8,128)(2,1)S(1)}, u32[]{:S(2)}, u32[]{:S(2)}) async-start(bf16[16,2,8,512]{3,2,1,0:T(8,128)(2,1)} %copy.14), calls=%async_computation.1 | async-start | bytes 524288 | tf_op jit(solution)/shard_map/all_to_all | solution.py:46
  117.6 10.0 %all-to-all-done.1 = bf16[16,2,8,512]{3,2,1,0:T(8,128)(2,1)S(1)} async-done(((bf16[16,2,8,512]{3,2,1,0:T(8,128)(2,1)}), bf16[16,2,8,512]{3,2,1,0:T(8,128)(2,1)S(1)}, u32[]{:S(2)}, u32[]{:S(2)}) %all-to-all-start.1) | async-done | bytes 262176 | tf_op jit(solution)/shard_map/all_to_all | solution.py:46
  127.6 0.8 gather_fusion
  128.5 5.9 %fusion.6 = bf16[128,512]{1,0:T(8,128)(2,1)} fusion(bf16[128,8192]{1,0:T(8,128)(2,1)} %param.6, bf16[8192,512]{1,0:T(8,128)(2,1)} %param.9, bf16[128,512]{1,0:T(8,128)(2,1)S(1)} %gather_fusion), kind=kOutput, calls=%fused_computation.10 | convolution fusion | flops 1073938432 | bytes 10747904 | tf_op jit(solution)/shard_map/dot_general | solution.py:47
  (2 shorter events, 0.0 us)
Async XLA Ops:
  0.0 108.0 %copy-start = (bf16[2,64,8192]{2,1,0:T(8,128)(2,1)S(1)}, bf16[2,64,8192]{2,1,0:T(8,128)(2,1)}, u32[]{:S(2)}) copy-start(bf16[2,64,8192]{2,1,0:T(8,128)(2,1)} %param.10) | copy-start | bytes 6291460
  8.1 99.9 %copy-start.1 = (bf16[2,64,512]{2,1,0:T(8,128)(2,1)S(1)}, bf16[2,64,512]{2,1,0:T(8,128)(2,1)}, u32[]{:S(2)}) copy-start(bf16[2,64,512]{2,1,0:T(8,128)(2,1)} %param.11) | copy-start | bytes 393220
  112.3 15.4 %all-to-all-start.1 = ((bf16[16,2,8,512]{3,2,1,0:T(8,128)(2,1)}), bf16[16,2,8,512]{3,2,1,0:T(8,128)(2,1)S(1)}, u32[]{:S(2)}, u32[]{:S(2)}) async-start(bf16[16,2,8,512]{3,2,1,0:T(8,128)(2,1)} %copy.14), calls=%async_computation.1 | async-start | bytes 524288 | tf_op jit(solution)/shard_map/all_to_all | solution.py:46
where the time goes:
time: 135 us; the launch traced here: 134 us
  blocking collectives  99.9 us (74%)
  waiting for transfers between devices  10 us (7%)
  matrix products  9.53 us (7%)
  local copies, waits for them, and re-layouts  8.55 us (6%)
  starting transfers between devices  5.3 us (4%)
    all_to_all x1, blocking collectives, local(): lax.all_to_all(outbound_rows, 'own', split_axis=0, concat_axis=0, tiled=T...  99.9 us
    all_to_all x1, waiting for transfers between devices, local(): lax.all_to_all(computed, 'own', split_axis=0, concat_axis=0, tiled=True)  10 us
    scatter x1, local copies, waits for them, and re-layouts, local(): jnp.zeros((total * depth, width), tokens.dtype).at[target].set(tokens)  6.98 us
    dot_general x1, matrix products, local(): jnp.dot(tokens, base_value_matrix, preferred_element_type=jnp.float32)  5.95 us
    all_to_all x1, starting transfers between devices, local(): lax.all_to_all(computed, 'own', split_axis=0, concat_axis=0, tiled=True)  5.3 us
    dot_general x1, matrix products, apply_lowrank_adapters(): jnp.einsum('zgpw,gwy->zgpy', reduced_rows, lowrank_up_weight, preferred_e...  3.59 us
  transfers between devices with their start and end apart: 1, of which 1 were waited for; matrix products, arithmetic and copies ran while one was open for 0% of the time, Pallas kernels for 0%

commit v1 on v0

v1 whole, which is shorter than its diff:
```python
import jax
import jax.numpy as jnp
from jax import lax
from jax.sharding import PartitionSpec as P

LANES = 4


def select(places, rank):
    return (places[:, None] == rank[None, :]).astype(jnp.bfloat16)


def pick(hot, values):
    return jnp.dot(hot, values, preferred_element_type=jnp.float32).astype(jnp.bfloat16)


def largest_anywhere(value, mesh_shape):
    value = jnp.full((1, 128), value, jnp.int32)
    for axis, size in mesh_shape.items():
        step = 1
        while step < size:
            pairs = [(i, i ^ step) for i in range(size)]
            value = jnp.maximum(value, lax.ppermute(value, axis, pairs))
            step *= 2
    return value[0, 0]


def make_local(mesh_shape):
    owners = mesh_shape["own"]
    planes = owners // LANES

    def by_planes(shift):
        return [
            (z * LANES + lane, (z + shift) % planes * LANES + lane)
            for z in range(planes)
            for lane in range(LANES)
        ]

    def by_lane(flip):
        return [(i, i ^ flip) for i in range(owners)]

    def send(x, shift):
        return lax.ppermute(x, "own", by_planes(shift % planes))

    def local(
        tokens,
        adapter_index_rows,
        adapter_pool_position,
        base_value_matrix,
        lowrank_down_weight,
        lowrank_up_weight,
    ):
        rows, width = tokens.shape
        held, rank, _ = lowrank_down_weight.shape
        out_width = base_value_matrix.shape[1]
        total = adapter_pool_position.shape[0]
        most = max(2, 2 * rows // total)
        cap = min(rows, LANES * held * most)
        first = cap // 2
        second = cap // 4
        third = cap - first - second
        levels = sorted({second * k // 8 for k in range(9)})
        shifts = sorted(range(1, planes), key=lambda s: -min(s, planes - s))

        me = lax.axis_index("own")
        plane, lane = me // LANES, me % LANES

        down = [lowrank_down_weight.reshape(held * rank, width)]
        up = [lowrank_up_weight.reshape(held * rank, out_width)]
        for flip in (1, 2):
            down = down + [lax.ppermute(x, "own", by_lane(flip)) for x in down]
            up = up + [lax.ppermute(x, "own", by_lane(flip)) for x in up]

        chosen = adapter_index_rows[:, 0]
        table = jnp.arange(total, dtype=jnp.int32)
        slot = jnp.sum(
            jnp.where(chosen[:, None] == table[None, :], adapter_pool_position[None, :], 0), axis=1
        )
        owner = slot // held
        shift_of = (owner // LANES - plane + planes) % planes
        column = ((owner % LANES) ^ lane) * held + slot % held
        places = jnp.arange(rows, dtype=jnp.int32)
        earlier = (shift_of[:, None] == shift_of[None, :]) & (places[None, :] < places[:, None])
        within = jnp.sum(earlier.astype(jnp.int32), axis=1)
        order = {s: jnp.where(shift_of == s, within, -1) for s in shifts}
        needed = jnp.max(jnp.where(shift_of > 0, within + 1, 0))
        needed = largest_anywhere(needed, mesh_shape)

        def hot(s, start, count):
            return select(jnp.arange(start, start + count, dtype=jnp.int32), order[s])

        arrived_column = {
            s: send(
                jnp.sum(
                    jnp.where(
                        jnp.arange(cap, dtype=jnp.int32)[:, None] == order[s][None, :],
                        column[None, :] + 1,
                        0,
                    ),
                    axis=1,
                )[None, :]
                - 1,
                s,
            )[0]
            for s in shifts
        }
        sent_first = {s: send(pick(hot(s, 0, first), tokens), s) for s in shifts}

        base = jnp.dot(tokens, base_value_matrix, preferred_element_type=jnp.float32)

        def level_branch(count):
            def branch(tokens, orders):
                out = []
                for s, o in zip(shifts, orders):
                    places = jnp.arange(first, first + count, dtype=jnp.int32)
                    if count:
                        got = send(pick(select(places, o), tokens), s)
                        out.append(jnp.pad(got, ((0, second - count), (0, 0))))
                    else:
                        out.append(jnp.zeros((second, width), tokens.dtype))
                return tuple(out)

            return branch

        level = jnp.sum((needed - first > jnp.array(levels[:-1])).astype(jnp.int32))
        sent_second = lax.switch(
            level,
            [level_branch(c) for c in levels],
            tokens,
            tuple(order[s] for s in shifts),
        )
        sent_second = dict(zip(shifts, sent_second))

        def adapters(x, columns):
            shrunk = jnp.concatenate(
                [
                    lax.dot_general(
                        x, w, (((1,), (1,)), ((), ())), preferred_element_type=jnp.float32
                    )
                    for w in down
                ],
                axis=1,
            )
            named = jnp.arange(shrunk.shape[1], dtype=jnp.int32)[None, :] // rank
            shrunk = jnp.where(named == columns[:, None], shrunk, 0).astype(jnp.bfloat16)
            return jnp.dot(
                shrunk, jnp.concatenate(up, axis=0), preferred_element_type=jnp.float32
            ).astype(jnp.bfloat16)

        both = first + second
        arrived = jnp.concatenate(
            [tokens] + [x for s in shifts for x in (sent_first[s], sent_second[s])], axis=0
        )
        arrived_columns = jnp.concatenate(
            [jnp.where(shift_of == 0, column, -1)] + [arrived_column[s][:both] for s in shifts]
        )
        computed = adapters(arrived, arrived_columns)
        own_delta = computed[:rows].astype(jnp.float32)
        returned = [
            send(computed[rows + i * both : rows + (i + 1) * both], -s)
            for i, s in enumerate(shifts)
        ]
        delta = own_delta + jnp.dot(
            jnp.concatenate([hot(s, 0, both) for s in shifts], axis=0).T,
            jnp.concatenate(returned, axis=0),
            preferred_element_type=jnp.float32,
        )

        def rest(tokens):
            sent = [send(pick(hot(s, both, third), tokens), s) for s in shifts]
            done = adapters(
                jnp.concatenate(sent, axis=0),
                jnp.concatenate([arrived_column[s][both:] for s in shifts]),
            )
            back = [send(done[i * third : (i + 1) * third], -s) for i, s in enumerate(shifts)]
            return jnp.dot(
                jnp.concatenate([hot(s, both, third) for s in shifts], axis=0).T,
                jnp.concatenate(back, axis=0),
                preferred_element_type=jnp.float32,
            )

        delta = delta + lax.cond(
            needed > both, rest, lambda x: jnp.zeros((rows, out_width), jnp.float32), tokens
        )
        return (base + delta).astype(jnp.bfloat16)

    return local


def solution(mesh):
    in_specs = (
        P(("grp", "own"), None),
        P(("grp", "own"), None),
        P("grp"),
        P(),
        P(("grp", "own"), None, None),
        P(("grp", "own"), None, None),
    )
    out_specs = P(("grp", "own"), None)
    return jax.shard_map(
        make_local(dict(mesh.shape)),
        mesh=mesh,
        in_specs=in_specs,
        out_specs=out_specs,
        check_vma=False,
    )
```

time: 135 us -> 150 us (1.11)
  blocking collectives: 99.9 us -> 0 us
  waiting for transfers between devices: 10 us -> 74 us
  starting transfers between devices: 5.3 us -> 46.9 us
  matrix products: 9.53 us -> 14.4 us
  other arithmetic: 1.09 us -> 4.68 us
    all_to_all x1 -> x0, blocking collectives: 99.9 us -> none  [local(): lax.all_to_all(outbound_rows, 'own', split_axis=0, concat_axis=0, tiled=T...]
    ppermute x0 -> x23, waiting for transfers between devices: none -> 74 us  [the longest x3 37.9 us: local(): down = down + [lax.ppermute(x, 'own', by_lane(flip)) for x in down]]
    ppermute x0 -> x23, starting transfers between devices: none -> 46.9 us  [the longest x12 31.2 us: send(): return lax.ppermute(x, 'own', by_planes(shift % planes))]
    all_to_all x1 -> x0, waiting for transfers between devices: 10 us -> none  [local(): lax.all_to_all(computed, 'own', split_axis=0, concat_axis=0, tiled=True)]
    dot_general x1 -> x12, matrix products: 3.59 us -> 13.1 us  [the longest x4 8.43 us: adapters(): lax.dot_general(x, w, (((1,), (1,)), ((), ())), preferred_element_type=jn...]
    scatter x1 -> x0, local copies, waits for them, and re-layouts: 6.98 us -> none  [local(): jnp.zeros((total * depth, width), tokens.dtype).at[target].set(tokens)]
    all_to_all x1 -> x0, starting transfers between devices: 5.3 us -> none  [local(): lax.all_to_all(computed, 'own', split_axis=0, concat_axis=0, tiled=True)]
    unnamed x4 -> x14, local copies, waits for them, and re-layouts: 0.01 us -> 4.73 us
  transfers between devices with their start and end apart: 1 -> 23, of which waited for: 1 -> 11; matrix products, arithmetic and copies ran while one was open for 0% -> 14% of each run, Pallas kernels for 0% -> 0%
where the time goes in v1:
time: 150 us
  waiting for transfers between devices  74 us (49%)
  starting transfers between devices  46.9 us (31%)
  matrix products  14.4 us (10%)
  local copies, waits for them, and re-layouts  8.56 us (6%)
  other arithmetic  4.68 us (3%)
    ppermute x3, waiting for transfers between devices, local(): down = down + [lax.ppermute(x, 'own', by_lane(flip)) for x in down]  37.9 us
    ppermute x12, waiting for transfers between devices, send(): return lax.ppermute(x, 'own', by_planes(shift % planes))  32 us
    ppermute x12, starting transfers between devices, send(): return lax.ppermute(x, 'own', by_planes(shift % planes))  31.2 us
    ppermute x5, starting transfers between devices, largest_anywhere(): value = jnp.maximum(value, lax.ppermute(value, axis, pairs))  10.3 us
    dot_general x4, matrix products, adapters(): lax.dot_general(x, w, (((1,), (1,)), ((), ())), preferred_element_type=jn...  8.43 us
    unnamed x14, local copies, waits for them, and re-layouts  4.73 us
    ppermute x5, waiting for transfers between devices, largest_anywhere(): value = jnp.maximum(value, lax.ppermute(value, axis, pairs))  4.15 us
    dot_general x6, matrix products, pick(): jnp.dot(hot, values, preferred_element_type=jnp.float32)  4.05 us
  transfers between devices with their start and end apart: 23, of which 11 were waited for; matrix products, arithmetic and copies ran while one was open for 14% of the time, Pallas kernels for 0%

profile of v1, /device:TPU:0, one launch (start us, length us, event | category | flops | bytes accessed | tf_op | source)
XLA Modules:
  0.0 149.6 jit_solution(1342053502433066550)
XLA Ops:
  2.4 3.0 %collective-permute-start.34 = (s32[1,128]{1,0:T(1,128)S(1)}, s32[1,128]{1,0:T(1,128)S(1)}, u32[]{:S(2)}, u32[]{:S(2)}) collective-permute-start(s32[1,128]{1,0:T(1,128)S(1)} %broadcast_in_dim.56), channel_id=1, source_target_pairs={{0,16},{16,0},{1,17},{17,1},{2,18},{18,2},{3,19},{19,3},{4,20},{20... | collective-permute-start | bytes 1544 | tf_op jit(solution)/shard_map/ppermute | solution.py:23
  5.4 1.5 %collective-permute-done.34 = s32[1,128]{1,0:T(1,128)S(1)} collective-permute-done((s32[1,128]{1,0:T(1,128)S(1)}, s32[1,128]{1,0:T(1,128)S(1)}, u32[]{:S(2)}, u32[]{:S(2)}) %collective-permute-start.34) | collective-permute-done | bytes 544 | tf_op jit(solution)/shard_map/ppermute | solution.py:23
  9.4 2.1 %collective-permute-start.36 = (s32[1,128]{1,0:T(1,128)S(1)}, s32[1,128]{1,0:T(1,128)S(1)}, u32[]{:S(2)}, u32[]{:S(2)}) collective-permute-start(s32[1,128]{1,0:T(1,128)S(1)} %fusion.204), channel_id=1, source_target_pairs={{0,2},{1,3},{2,0},{3,1},{4,6},{5,7},{6,4},{7,5},{8,10},{9,11},{10,... | collective-permute-start | bytes 1544 | tf_op jit(solution)/shard_map/ppermute | solution.py:23
  11.6 1.5 %collective-permute-done.36 = s32[1,128]{1,0:T(1,128)S(1)} collective-permute-done((s32[1,128]{1,0:T(1,128)S(1)}, s32[1,128]{1,0:T(1,128)S(1)}, u32[]{:S(2)}, u32[]{:S(2)}) %collective-permute-start.36) | collective-permute-done | bytes 544 | tf_op jit(solution)/shard_map/ppermute | solution.py:23
  13.1 2.1 %collective-permute-start.37 = (s32[1,128]{1,0:T(1,128)S(1)}, s32[1,128]{1,0:T(1,128)S(1)}, u32[]{:S(2)}, u32[]{:S(2)}) collective-permute-start(s32[1,128]{1,0:T(1,128)S(1)} %max.17), channel_id=1, source_target_pairs={{0,4},{1,5},{2,6},{3,7},{4,0},{5,1},{6,2},{7,3},{8,12},{9,13},{10,... | collective-permute-start | bytes 1544 | tf_op jit(solution)/shard_map/ppermute | solution.py:23
  15.2 1.5 %collective-permute-start.42 = (bf16[128,8192]{1,0:T(8,128)(2,1)}, bf16[128,8192]{1,0:T(8,128)(2,1)}, u32[]{:S(2)}, u32[]{:S(2)}) collective-permute-start(bf16[128,8192]{1,0:T(8,128)(2,1)} %bitcast.73), channel_id=1, source_target_pairs={{0,2},{1,3},{2,0},{3,1},{4,6},{5,7},{6,4},{7,5},{8,10},{9,11},{10,... | collective-permute-start | bytes 6291464 | tf_op jit(solution)/shard_map/ppermute | solution.py:71
  16.7 3.0 %collective-permute-start.38 = (s32[1,128]{1,0:T(1,128)S(1)}, s32[1,128]{1,0:T(1,128)S(1)}, u32[]{:S(2)}, u32[]{:S(2)}) collective-permute-start(s32[1,128]{1,0:T(1,128)S(1)} %max.18), channel_id=1, source_target_pairs={{0,8},{1,9},{2,10},{3,11},{4,12},{5,13},{6,14},{7,15},{8,0},{9,1},... | collective-permute-start | bytes 1544 | tf_op jit(solution)/shard_map/ppermute | solution.py:23
  19.7 2.0 %convolution_convert_fusion.30 = bf16[32,8192]{1,0:T(8,128)(2,1)S(1)} fusion(bf16[128,8192]{1,0:T(8,128)(2,1)} %param.18, s32[128]{0:T(128)S(1)} %get-tuple-element.178), kind=kOutput, calls=%fused_computation.156 | convolution fusion | flops 67375104 | bytes 2621952 | tf_op jit(solution)/shard_map/dot_general | solution.py:14
  22.9 14.2 %conditional.2 = (bf16[16,8192]{1,0:T(8,128)(2,1)}, bf16[16,8192]{1,0:T(8,128)(2,1)}, bf16[16,8192]{1,0:T(8,128)(2,1)}) conditional(s32[]{:T(128)} %clamp.3, () %tuple.47, (s32[128]{0:T(128)S(1)}, bf16[128,8192]{1,0:T(8,128)(2,1)S(1)}, s32[128]{0:T(128)S(1)}, s32[128]{0:T(128)S(1)}) %tuple.77, (s32[128]{0:T(128)S(1)}, ...), branch_computations={%region_7.8_spmd, %region_8.9_spmd, %region_9.10_spmd, %region_10.... | conditional | flops 101062672 | bytes 11208566 | solution.py:126
  23.4 2.5 %collective-permute-start.9 = (bf16[8,8192]{1,0:T(8,128)(2,1)S(1)}, bf16[8,8192]{1,0:T(8,128)(2,1)S(1)}, u32[]{:S(2)}, u32[]{:S(2)}) collective-permute-start(bf16[8,8192]{1,0:T(8,128)(2,1)S(1)} %convolution_convert_fusion.11), channel_id=1, source_target_pairs={{0,8},{1,9},{2,10},{3,11},{4,12},{5,13},{6,14},{7,15},{8,0},{9,1},... | collective-permute-start | bytes 393224 | tf_op jit(solution)/shard_map/cond/branch_4_fun/ppermute | solution.py:43
  26.3 1.6 %collective-permute-start.10 = (bf16[8,8192]{1,0:T(8,128)(2,1)S(1)}, bf16[8,8192]{1,0:T(8,128)(2,1)S(1)}, u32[]{:S(2)}, u32[]{:S(2)}) collective-permute-start(bf16[8,8192]{1,0:T(8,128)(2,1)S(1)} %convolution_convert_fusion.10), channel_id=1, source_target_pairs={{0,4},{1,5},{2,6},{3,7},{4,8},{5,9},{6,10},{7,11},{8,12},{9,13},{1... | collective-permute-start | bytes 393224 | tf_op jit(solution)/shard_map/cond/branch_4_fun/ppermute | solution.py:43
  28.3 2.3 %collective-permute-start.11 = (bf16[8,8192]{1,0:T(8,128)(2,1)S(1)}, bf16[8,8192]{1,0:T(8,128)(2,1)S(1)}, u32[]{:S(2)}, u32[]{:S(2)}) collective-permute-start(bf16[8,8192]{1,0:T(8,128)(2,1)S(1)} %convolution_convert_fusion.9), channel_id=1, source_target_pairs={{0,12},{1,13},{2,14},{3,15},{4,0},{5,1},{6,2},{7,3},{8,4},{9,5},{1... | collective-permute-start | bytes 393224 | tf_op jit(solution)/shard_map/cond/branch_4_fun/ppermute | solution.py:43
  30.6 4.3 %collective-permute-done.9 = bf16[8,8192]{1,0:T(8,128)(2,1)S(1)} collective-permute-done((bf16[8,8192]{1,0:T(8,128)(2,1)S(1)}, bf16[8,8192]{1,0:T(8,128)(2,1)S(1)}, u32[]{:S(2)}, u32[]{:S(2)}) %collective-permute-start.9) | collective-permute-done | bytes 131104 | tf_op jit(solution)/shard_map/cond/branch_4_fun/ppermute | solution.py:43
  37.1 2.6 %collective-permute-start.33 = (bf16[32,8192]{1,0:T(8,128)(2,1)S(1)}, bf16[32,8192]{1,0:T(8,128)(2,1)S(1)}, u32[]{:S(2)}, u32[]{:S(2)}) collective-permute-start(bf16[32,8192]{1,0:T(8,128)(2,1)S(1)} %convolution_convert_fusion.30), channel_id=1, source_target_pairs={{0,8},{1,9},{2,10},{3,11},{4,12},{5,13},{6,14},{7,15},{8,0},{9,1},... | collective-permute-start | bytes 1572872 | tf_op jit(solution)/shard_map/ppermute | solution.py:43
  39.8 1.6 %collective-permute-start.32 = (s32[1,64]{1,0:T(1,128)S(1)}, s32[1,64]{1,0:T(1,128)S(1)}, u32[]{:S(2)}, u32[]{:S(2)}) collective-permute-start(s32[1,64]{1,0:T(1,128)S(1)} %add_bitcast_fusion), channel_id=1, source_target_pairs={{0,12},{1,13},{2,14},{3,15},{4,0},{5,1},{6,2},{7,3},{8,4},{9,5},{1... | collective-permute-start | bytes 776 | tf_op jit(solution)/shard_map/ppermute | solution.py:43
  42.9 2.4 %copy-done.1 = bf16[8192,512]{1,0:T(8,128)(2,1)S(1)} copy-done((bf16[8192,512]{1,0:T(8,128)(2,1)S(1)}, bf16[8192,512]{1,0:T(8,128)(2,1)}, u32[]{:S(2)}) %copy-start.1) | copy-done | bytes 8388632
  45.3 1.4 fusion.151
  46.7 2.5 %collective-permute-done.32 = s32[1,64]{1,0:T(1,128)S(1)} collective-permute-done((s32[1,64]{1,0:T(1,128)S(1)}, s32[1,64]{1,0:T(1,128)S(1)}, u32[]{:S(2)}, u32[]{:S(2)}) %collective-permute-start.32) | collective-permute-done | bytes 288 | tf_op jit(solution)/shard_map/ppermute | solution.py:43
  49.2 13.2 %collective-permute-start.30 = (s32[1,64]{1,0:T(1,128)S(1)}, s32[1,64]{1,0:T(1,128)S(1)}, u32[]{:S(2)}, u32[]{:S(2)}) collective-permute-start(s32[1,64]{1,0:T(1,128)S(1)} %add_bitcast_fusion.2), channel_id=1, source_target_pairs={{0,8},{1,9},{2,10},{3,11},{4,12},{5,13},{6,14},{7,15},{8,0},{9,1},... | collective-permute-start | bytes 776 | tf_op jit(solution)/shard_map/ppermute | solution.py:43
  62.5 1.4 collective-permute-done.30
  64.1 3.9 %collective-permute-start.39 = (bf16[32,8192]{1,0:T(8,128)(2,1)S(1)}, bf16[32,8192]{1,0:T(8,128)(2,1)S(1)}, u32[]{:S(2)}, u32[]{:S(2)}) collective-permute-start(bf16[32,8192]{1,0:T(8,128)(2,1)S(1)} %convolution_convert_fusion.29), channel_id=1, source_target_pairs={{0,4},{1,5},{2,6},{3,7},{4,8},{5,9},{6,10},{7,11},{8,12},{9,13},{1... | collective-permute-start | bytes 1572872 | tf_op jit(solution)/shard_map/ppermute | solution.py:43
  69.3 11.6 %collective-permute-done.39 = bf16[32,8192]{1,0:T(8,128)(2,1)S(1)} collective-permute-done((bf16[32,8192]{1,0:T(8,128)(2,1)S(1)}, bf16[32,8192]{1,0:T(8,128)(2,1)S(1)}, u32[]{:S(2)}, u32[]{:S(2)}) %collective-permute-start.39) | collective-permute-done | bytes 524320 | tf_op jit(solution)/shard_map/ppermute | solution.py:43
  80.9 2.0 %collective-permute-start.46 = (bf16[128,512]{1,0:T(8,128)(2,1)S(1)}, bf16[128,512]{1,0:T(8,128)(2,1)S(1)}, u32[]{:S(2)}, u32[]{:S(2)}) collective-permute-start(bf16[128,512]{1,0:T(8,128)(2,1)S(1)} %collective-permute-done.44), channel_id=1, source_target_pairs={{0,2},{1,3},{2,0},{3,1},{4,6},{5,7},{6,4},{7,5},{8,10},{9,11},{10,... | collective-permute-start | bytes 393224 | tf_op jit(solution)/shard_map/ppermute | solution.py:72
  83.9 6.2 %collective-permute-done.40 = bf16[32,8192]{1,0:T(8,128)(2,1)S(1)} collective-permute-done((bf16[32,8192]{1,0:T(8,128)(2,1)S(1)}, bf16[32,8192]{1,0:T(8,128)(2,1)S(1)}, u32[]{:S(2)}, u32[]{:S(2)}) %collective-permute-start.40) | collective-permute-done | bytes 524320 | tf_op jit(solution)/shard_map/ppermute | solution.py:43
  90.2 1.8 %collective-permute-start.43 = (bf16[128,8192]{1,0:T(8,128)(2,1)}, bf16[128,8192]{1,0:T(8,128)(2,1)S(1)}, u32[]{:S(2)}, u32[]{:S(2)}) collective-permute-start(bf16[128,8192]{1,0:T(8,128)(2,1)} %collective-permute-done.41), channel_id=1, source_target_pairs={{0,2},{1,3},{2,0},{3,1},{4,6},{5,7},{6,4},{7,5},{8,10},{9,11},{10,... | collective-permute-start | bytes 6291464 | tf_op jit(solution)/shard_map/ppermute | solution.py:71
  92.9 1.3 fusion.152
  94.3 2.9 %fusion.153 = bf16[272,128]{1,0:T(8,128)(2,1)S(1)} fusion(bf16[272,8192]{1,0:T(8,128)(2,1)S(1)} %constant_dynamic-update-slice_fusion.3, bf16[128,8192]{1,0:T(8,128)(2,1)} %collective-permute-done.41), kind=kOutput, calls=%fused_computation.263 | convolution fusion | flops 570425344 | bytes 6623232 | tf_op jit(solution)/shard_map/dot_general | solution.py:137
  97.2 2.9 %fusion.154 = bf16[272,128]{1,0:T(8,128)(2,1)S(1)} fusion(bf16[272,8192]{1,0:T(8,128)(2,1)S(1)} %constant_dynamic-update-slice_fusion.3, bf16[128,8192]{1,0:T(8,128)(2,1)} %collective-permute-done.42), kind=kOutput, calls=%fused_computation.264 | convolution fusion | flops 570425344 | bytes 6623232 | tf_op jit(solution)/shard_map/dot_general | solution.py:137
  100.1 37.9 %collective-permute-done.43 = bf16[128,8192]{1,0:T(8,128)(2,1)S(1)} collective-permute-done((bf16[128,8192]{1,0:T(8,128)(2,1)}, bf16[128,8192]{1,0:T(8,128)(2,1)S(1)}, u32[]{:S(2)}, u32[]{:S(2)}) %collective-permute-start.43) | collective-permute-done | bytes 2097184 | tf_op jit(solution)/shard_map/ppermute | solution.py:71
  139.8 2.9 %collective-permute-start.48 = (bf16[48,512]{1,0:T(8,128)(2,1)S(1)}, bf16[48,512]{1,0:T(8,128)(2,1)S(1)}, u32[]{:S(2)}, u32[]{:S(2)}) collective-permute-start(bf16[48,512]{1,0:T(8,128)(2,1)S(1)} %get-tuple-element.174), channel_id=1, source_target_pairs={{0,12},{1,13},{2,14},{3,15},{4,0},{5,1},{6,2},{7,3},{8,4},{9,5},{1... | collective-permute-start | bytes 147464 | tf_op jit(solution)/shard_map/ppermute | solution.py:43
  142.8 2.5 %collective-permute-done.47 = bf16[48,512]{1,0:T(8,128)(2,1)S(1)} collective-permute-done((bf16[48,512]{1,0:T(8,128)(2,1)S(1)}, bf16[48,512]{1,0:T(8,128)(2,1)S(1)}, u32[]{:S(2)}, u32[]{:S(2)}) %collective-permute-start.47) | collective-permute-done | bytes 49184 | tf_op jit(solution)/shard_map/ppermute | solution.py:43
  145.3 3.4 %collective-permute-done.49 = bf16[48,512]{1,0:T(8,128)(2,1)S(1)} collective-permute-done((bf16[48,512]{1,0:T(8,128)(2,1)S(1)}, bf16[48,512]{1,0:T(8,128)(2,1)S(1)}, u32[]{:S(2)}, u32[]{:S(2)}) %collective-permute-start.49) | collective-permute-done | bytes 49184 | tf_op jit(solution)/shard_map/ppermute | solution.py:43
  (74 shorter events, 16.8 us)
Async XLA Ops:
  0.0 22.4 %copy-start = (bf16[128,8192]{1,0:T(8,128)(2,1)S(1)}, bf16[128,8192]{1,0:T(8,128)(2,1)}, u32[]{:S(2)}) copy-start(bf16[128,8192]{1,0:T(8,128)(2,1)} %param.18) | copy-start | bytes 6291460
  2.4 4.5 %collective-permute-start.34 = (s32[1,128]{1,0:T(1,128)S(1)}, s32[1,128]{1,0:T(1,128)S(1)}, u32[]{:S(2)}, u32[]{:S(2)}) collective-permute-start(s32[1,128]{1,0:T(1,128)S(1)} %broadcast_in_dim.56), channel_id=1, source_target_pairs={{0,16},{16,0},{1,17},{17,1},{2,18},{18,2},{3,19},{19,3},{4,20},{20... | collective-permute-start | bytes 1544 | tf_op jit(solution)/shard_map/ppermute | solution.py:23
  7.6 1.2 collective-permute-start.35
  9.4 3.6 %collective-permute-start.36 = (s32[1,128]{1,0:T(1,128)S(1)}, s32[1,128]{1,0:T(1,128)S(1)}, u32[]{:S(2)}, u32[]{:S(2)}) collective-permute-start(s32[1,128]{1,0:T(1,128)S(1)} %fusion.204), channel_id=1, source_target_pairs={{0,2},{1,3},{2,0},{3,1},{4,6},{5,7},{6,4},{7,5},{8,10},{9,11},{10,... | collective-permute-start | bytes 1544 | tf_op jit(solution)/shard_map/ppermute | solution.py:23
  13.1 3.6 %collective-permute-start.37 = (s32[1,128]{1,0:T(1,128)S(1)}, s32[1,128]{1,0:T(1,128)S(1)}, u32[]{:S(2)}, u32[]{:S(2)}) collective-permute-start(s32[1,128]{1,0:T(1,128)S(1)} %max.17), channel_id=1, source_target_pairs={{0,4},{1,5},{2,6},{3,7},{4,0},{5,1},{6,2},{7,3},{8,12},{9,13},{10,... | collective-permute-start | bytes 1544 | tf_op jit(solution)/shard_map/ppermute | solution.py:23
  15.2 75.0 %collective-permute-start.41 = (bf16[128,8192]{1,0:T(8,128)(2,1)}, bf16[128,8192]{1,0:T(8,128)(2,1)}, u32[]{:S(2)}, u32[]{:S(2)}) collective-permute-start(bf16[128,8192]{1,0:T(8,128)(2,1)} %bitcast.72), channel_id=1, source_target_pairs={{0,1},{1,0},{2,3},{3,2},{4,5},{5,4},{6,7},{7,6},{8,9},{9,8},{10,11... | collective-permute-start | bytes 6291464 | tf_op jit(solution)/shard_map/ppermute | solution.py:71
  15.2 82.0 %collective-permute-start.42 = (bf16[128,8192]{1,0:T(8,128)(2,1)}, bf16[128,8192]{1,0:T(8,128)(2,1)}, u32[]{:S(2)}, u32[]{:S(2)}) collective-permute-start(bf16[128,8192]{1,0:T(8,128)(2,1)} %bitcast.73), channel_id=1, source_target_pairs={{0,2},{1,3},{2,0},{3,1},{4,6},{5,7},{6,4},{7,5},{8,10},{9,11},{10,... | collective-permute-start | bytes 6291464 | tf_op jit(solution)/shard_map/ppermute | solution.py:71
  16.7 5.0 %collective-permute-start.38 = (s32[1,128]{1,0:T(1,128)S(1)}, s32[1,128]{1,0:T(1,128)S(1)}, u32[]{:S(2)}, u32[]{:S(2)}) collective-permute-start(s32[1,128]{1,0:T(1,128)S(1)} %max.18), channel_id=1, source_target_pairs={{0,8},{1,9},{2,10},{3,11},{4,12},{5,13},{6,14},{7,15},{8,0},{9,1},... | collective-permute-start | bytes 1544 | tf_op jit(solution)/shard_map/ppermute | solution.py:23
  23.4 11.5 %collective-permute-start.9 = (bf16[8,8192]{1,0:T(8,128)(2,1)S(1)}, bf16[8,8192]{1,0:T(8,128)(2,1)S(1)}, u32[]{:S(2)}, u32[]{:S(2)}) collective-permute-start(bf16[8,8192]{1,0:T(8,128)(2,1)S(1)} %convolution_convert_fusion.11), channel_id=1, source_target_pairs={{0,8},{1,9},{2,10},{3,11},{4,12},{5,13},{6,14},{7,15},{8,0},{9,1},... | collective-permute-start | bytes 393224 | tf_op jit(solution)/shard_map/cond/branch_4_fun/ppermute | solution.py:43
  26.3 9.4 %collective-permute-start.10 = (bf16[8,8192]{1,0:T(8,128)(2,1)S(1)}, bf16[8,8192]{1,0:T(8,128)(2,1)S(1)}, u32[]{:S(2)}, u32[]{:S(2)}) collective-permute-start(bf16[8,8192]{1,0:T(8,128)(2,1)S(1)} %convolution_convert_fusion.10), channel_id=1, source_target_pairs={{0,4},{1,5},{2,6},{3,7},{4,8},{5,9},{6,10},{7,11},{8,12},{9,13},{1... | collective-permute-start | bytes 393224 | tf_op jit(solution)/shard_map/cond/branch_4_fun/ppermute | solution.py:43
  28.3 8.1 %collective-permute-start.11 = (bf16[8,8192]{1,0:T(8,128)(2,1)S(1)}, bf16[8,8192]{1,0:T(8,128)(2,1)S(1)}, u32[]{:S(2)}, u32[]{:S(2)}) collective-permute-start(bf16[8,8192]{1,0:T(8,128)(2,1)S(1)} %convolution_convert_fusion.9), channel_id=1, source_target_pairs={{0,12},{1,13},{2,14},{3,15},{4,0},{5,1},{6,2},{7,3},{8,4},{9,5},{1... | collective-permute-start | bytes 393224 | tf_op jit(solution)/shard_map/cond/branch_4_fun/ppermute | solution.py:43
  37.1 27.0 %collective-permute-start.33 = (bf16[32,8192]{1,0:T(8,128)(2,1)S(1)}, bf16[32,8192]{1,0:T(8,128)(2,1)S(1)}, u32[]{:S(2)}, u32[]{:S(2)}) collective-permute-start(bf16[32,8192]{1,0:T(8,128)(2,1)S(1)} %convolution_convert_fusion.30), channel_id=1, source_target_pairs={{0,8},{1,9},{2,10},{3,11},{4,12},{5,13},{6,14},{7,15},{8,0},{9,1},... | collective-permute-start | bytes 1572872 | tf_op jit(solution)/shard_map/ppermute | solution.py:43
  39.8 9.4 %collective-permute-start.32 = (s32[1,64]{1,0:T(1,128)S(1)}, s32[1,64]{1,0:T(1,128)S(1)}, u32[]{:S(2)}, u32[]{:S(2)}) collective-permute-start(s32[1,64]{1,0:T(1,128)S(1)} %add_bitcast_fusion), channel_id=1, source_target_pairs={{0,12},{1,13},{2,14},{3,15},{4,0},{5,1},{6,2},{7,3},{8,4},{9,5},{1... | collective-permute-start | bytes 776 | tf_op jit(solution)/shard_map/ppermute | solution.py:43
  41.4 21.0 %collective-permute-start.31 = (s32[1,64]{1,0:T(1,128)S(1)}, s32[1,64]{1,0:T(1,128)S(1)}, u32[]{:S(2)}, u32[]{:S(2)}) collective-permute-start(s32[1,64]{1,0:T(1,128)S(1)} %add_bitcast_fusion.1), channel_id=1, source_target_pairs={{0,4},{1,5},{2,6},{3,7},{4,8},{5,9},{6,10},{7,11},{8,12},{9,13},{1... | collective-permute-start | bytes 776 | tf_op jit(solution)/shard_map/ppermute | solution.py:43
  41.9 3.4 %copy-start.1 = (bf16[8192,512]{1,0:T(8,128)(2,1)S(1)}, bf16[8192,512]{1,0:T(8,128)(2,1)}, u32[]{:S(2)}) copy-start(bf16[8192,512]{1,0:T(8,128)(2,1)} %param.21) | copy-start | bytes 25165828
  45.3 17.2 %copy-start.3 = (bf16[2,64,512]{2,1,0:T(8,128)(2,1)S(1)}, bf16[2,64,512]{2,1,0:T(8,128)(2,1)}, u32[]{:S(2)}) copy-start(bf16[2,64,512]{2,1,0:T(8,128)(2,1)} %param.23) | copy-start | bytes 393220
  49.2 14.7 %collective-permute-start.30 = (s32[1,64]{1,0:T(1,128)S(1)}, s32[1,64]{1,0:T(1,128)S(1)}, u32[]{:S(2)}, u32[]{:S(2)}) collective-permute-start(s32[1,64]{1,0:T(1,128)S(1)} %add_bitcast_fusion.2), channel_id=1, source_target_pairs={{0,8},{1,9},{2,10},{3,11},{4,12},{5,13},{6,14},{7,15},{8,0},{9,1},... | collective-permute-start | bytes 776 | tf_op jit(solution)/shard_map/ppermute | solution.py:43
  62.5 6.8 %collective-permute-start.44 = (bf16[128,512]{1,0:T(8,128)(2,1)S(1)}, bf16[128,512]{1,0:T(8,128)(2,1)S(1)}, u32[]{:S(2)}, u32[]{:S(2)}) collective-permute-start(bf16[128,512]{1,0:T(8,128)(2,1)S(1)} %bitcast.76), channel_id=1, source_target_pairs={{0,1},{1,0},{2,3},{3,2},{4,5},{5,4},{6,7},{7,6},{8,9},{9,8},{10,11... | collective-permute-start | bytes 393224 | tf_op jit(solution)/shard_map/ppermute | solution.py:72
  64.0 75.3 %collective-permute-start.45 = (bf16[128,512]{1,0:T(8,128)(2,1)S(1)}, bf16[128,512]{1,0:T(8,128)(2,1)S(1)}, u32[]{:S(2)}, u32[]{:S(2)}) collective-permute-start(bf16[128,512]{1,0:T(8,128)(2,1)S(1)} %bitcast.77), channel_id=1, source_target_pairs={{0,2},{1,3},{2,0},{3,1},{4,6},{5,7},{6,4},{7,5},{8,10},{9,11},{10,... | collective-permute-start | bytes 393224 | tf_op jit(solution)/shard_map/ppermute | solution.py:72
  64.1 16.8 %collective-permute-start.39 = (bf16[32,8192]{1,0:T(8,128)(2,1)S(1)}, bf16[32,8192]{1,0:T(8,128)(2,1)S(1)}, u32[]{:S(2)}, u32[]{:S(2)}) collective-permute-start(bf16[32,8192]{1,0:T(8,128)(2,1)S(1)} %convolution_convert_fusion.29), channel_id=1, source_target_pairs={{0,4},{1,5},{2,6},{3,7},{4,8},{5,9},{6,10},{7,11},{8,12},{9,13},{1... | collective-permute-start | bytes 1572872 | tf_op jit(solution)/shard_map/ppermute | solution.py:43
  68.1 24.9 %copy-start.2 = (bf16[2,64,8192]{2,1,0:T(8,128)(2,1)S(1)}, bf16[2,64,8192]{2,1,0:T(8,128)(2,1)}, u32[]{:S(2)}) copy-start(bf16[2,64,8192]{2,1,0:T(8,128)(2,1)} %param.22) | copy-start | bytes 6291460
  69.2 20.9 %collective-permute-start.40 = (bf16[32,8192]{1,0:T(8,128)(2,1)S(1)}, bf16[32,8192]{1,0:T(8,128)(2,1)S(1)}, u32[]{:S(2)}, u32[]{:S(2)}) collective-permute-start(bf16[32,8192]{1,0:T(8,128)(2,1)S(1)} %convolution_convert_fusion.28), channel_id=1, source_target_pairs={{0,12},{1,13},{2,14},{3,15},{4,0},{5,1},{6,2},{7,3},{8,4},{9,5},{1... | collective-permute-start | bytes 1572872 | tf_op jit(solution)/shard_map/ppermute | solution.py:43
  80.9 58.4 %collective-permute-start.46 = (bf16[128,512]{1,0:T(8,128)(2,1)S(1)}, bf16[128,512]{1,0:T(8,128)(2,1)S(1)}, u32[]{:S(2)}, u32[]{:S(2)}) collective-permute-start(bf16[128,512]{1,0:T(8,128)(2,1)S(1)} %collective-permute-done.44), channel_id=1, source_target_pairs={{0,2},{1,3},{2,0},{3,1},{4,6},{5,7},{6,4},{7,5},{8,10},{9,11},{10,... | collective-permute-start | bytes 393224 | tf_op jit(solution)/shard_map/ppermute | solution.py:72
  90.2 47.8 %collective-permute-start.43 = (bf16[128,8192]{1,0:T(8,128)(2,1)}, bf16[128,8192]{1,0:T(8,128)(2,1)S(1)}, u32[]{:S(2)}, u32[]{:S(2)}) collective-permute-start(bf16[128,8192]{1,0:T(8,128)(2,1)} %collective-permute-done.41), channel_id=1, source_target_pairs={{0,2},{1,3},{2,0},{3,1},{4,6},{5,7},{6,4},{7,5},{8,10},{9,11},{10,... | collective-permute-start | bytes 6291464 | tf_op jit(solution)/shard_map/ppermute | solution.py:71
  139.7 5.6 %collective-permute-start.47 = (bf16[48,512]{1,0:T(8,128)(2,1)S(1)}, bf16[48,512]{1,0:T(8,128)(2,1)S(1)}, u32[]{:S(2)}, u32[]{:S(2)}) collective-permute-start(bf16[48,512]{1,0:T(8,128)(2,1)S(1)} %get-tuple-element.172), channel_id=1, source_target_pairs={{0,8},{1,9},{2,10},{3,11},{4,12},{5,13},{6,14},{7,15},{8,0},{9,1},... | collective-permute-start | bytes 147464 | tf_op jit(solution)/shard_map/ppermute | solution.py:43
  139.8 5.5 %collective-permute-start.48 = (bf16[48,512]{1,0:T(8,128)(2,1)S(1)}, bf16[48,512]{1,0:T(8,128)(2,1)S(1)}, u32[]{:S(2)}, u32[]{:S(2)}) collective-permute-start(bf16[48,512]{1,0:T(8,128)(2,1)S(1)} %get-tuple-element.174), channel_id=1, source_target_pairs={{0,12},{1,13},{2,14},{3,15},{4,0},{5,1},{6,2},{7,3},{8,4},{9,5},{1... | collective-permute-start | bytes 147464 | tf_op jit(solution)/shard_map/ppermute | solution.py:43
  142.7 5.9 %collective-permute-start.49 = (bf16[48,512]{1,0:T(8,128)(2,1)S(1)}, bf16[48,512]{1,0:T(8,128)(2,1)S(1)}, u32[]{:S(2)}, u32[]{:S(2)}) collective-permute-start(bf16[48,512]{1,0:T(8,128)(2,1)S(1)} %get-tuple-element.173), channel_id=1, source_target_pairs={{0,4},{1,5},{2,6},{3,7},{4,8},{5,9},{6,10},{7,11},{8,12},{9,13},{1... | collective-permute-start | bytes 147464 | tf_op jit(solution)/shard_map/ppermute | solution.py:43

commit v2 on v0

v2 whole, which is shorter than its diff:
```python
import functools

import jax
import jax.numpy as jnp
from jax import lax
from jax.experimental import pallas as pl
from jax.experimental.pallas import tpu as pltpu
from jax.sharding import PartitionSpec as P

LANES = 4
MATMUL_T = (((1,), (1,)), ((), ()))
PARAMS = pltpu.CompilerParams(vmem_limit_bytes=40 * 1024 * 1024)


def tile_of(width):
    return next(t for t in (1024, 512, 256, 128, width) if width % t == 0)


def count_body(starts, levels, place_ref, mine_ref, mate_ref, out_ref):
    mine, mate = mine_ref[...], mate_ref[...]
    chip_rows = jnp.zeros((1, 1), jnp.int32)
    device_rows = jnp.zeros((1, 1), jnp.int32)
    for p, (low, high) in enumerate(starts):
        counts = []
        for packed in (mine, mate):
            here = (packed >= low) & (packed < high) & (place_ref[1] != p)
            counts.append(
                jnp.sum(jnp.where(here, 1.0, 0.0), axis=1, keepdims=True).astype(jnp.int32)
            )
        chip_rows = jnp.maximum(chip_rows, counts[0] + counts[1])
        device_rows = jnp.maximum(device_rows, jnp.maximum(*counts))
    level = jnp.zeros((1, 1), jnp.int32)
    for chip_cap, device_cap in levels[:-1]:
        level = level + ((chip_rows > chip_cap) | (device_rows > device_cap)).astype(jnp.int32)
    out_ref[0:1, :] = mine
    out_ref[1:2, :] = mate
    out_ref[2:3, :] = jnp.broadcast_to(level, mine.shape)


def count(place, mine, mate, starts, levels):
    return pl.pallas_call(
        functools.partial(count_body, starts, levels),
        out_shape=jax.ShapeDtypeStruct((3, mine.shape[1]), jnp.int32),
        in_specs=[
            pl.BlockSpec(memory_space=pltpu.SMEM),
            pl.BlockSpec(memory_space=pltpu.VMEM),
            pl.BlockSpec(memory_space=pltpu.VMEM),
        ],
        out_specs=pl.BlockSpec(memory_space=pltpu.VMEM),
    )(place, mine, mate)


def pack_body(shifts, planes, place_ref, goes_ref, within_ref, kept_ref, mate_ref, *outs):
    core, plane = place_ref[0], place_ref[1]
    size = outs[0].shape[0]
    spots = lax.broadcasted_iota(jnp.int32, (size, kept_ref.shape[0]), 0)
    for s, out in zip(shifts, outs):
        to = lax.rem(plane + s, planes)
        packed = jnp.zeros(out.shape, jnp.float32)
        for row, rows_ref in enumerate((kept_ref, mate_ref)):
            within = within_ref[row : row + 1, :]
            spot = jnp.where(core == row, within, size - 1 - within)
            spot = jnp.where(goes_ref[row : row + 1, :] == to, spot, -1)
            hot = jnp.where(spots == spot, 1.0, 0.0).astype(jnp.bfloat16)
            packed += jnp.dot(hot, rows_ref[...], preferred_element_type=jnp.float32)
        out[...] = packed.astype(out.dtype)


def pack(place, goes_to, within, tokens, mate, size, shifts, planes):
    rows, half = mate.shape
    tile = tile_of(half)
    steps = half // tile
    whole = lambda a: pl.BlockSpec(a.shape, lambda k, place: (0, 0))
    strip = pl.BlockSpec((rows, tile), lambda k, place: (0, k))
    return pl.pallas_call(
        functools.partial(pack_body, shifts, planes),
        grid_spec=pltpu.PrefetchScalarGridSpec(
            num_scalar_prefetch=1,
            grid=(steps,),
            in_specs=[
                whole(goes_to),
                whole(within),
                pl.BlockSpec((rows, tile), lambda k, place: (0, place[0] * steps + k)),
                strip,
            ],
            out_specs=[pl.BlockSpec((size, tile), lambda k, place: (0, k)) for _ in shifts],
        ),
        out_shape=[jax.ShapeDtypeStruct((size, half), mate.dtype) for _ in shifts],
        compiler_params=PARAMS,
        cost_estimate=pl.CostEstimate(
            flops=4 * len(shifts) * size * rows * half,
            bytes_accessed=2 * half * (2 * rows + len(shifts) * size),
            transcendentals=0,
        ),
    )(place, goes_to, within, tokens, mate)


def shrink_body(number, maps, rank, place_ref, *refs):
    xs, ws = refs[:number], refs[number : number + maps]
    column, out, total = refs[number + maps :]
    step = pl.program_id(0)
    rows = jnp.concatenate([x[...] for x in xs], axis=0)
    weights = jnp.concatenate([w[...] for w in ws], axis=0)
    part = lax.dot_general(rows, weights, MATMUL_T, preferred_element_type=jnp.float32)

    @pl.when(step == 0)
    def _():
        total[...] = part

    @pl.when(step != 0)
    def _():
        total[...] += part

    @pl.when(step == pl.num_programs(0) - 1)
    def _():
        lanes = lax.broadcasted_iota(jnp.int32, total.shape, 1)
        low = column[...] * rank
        picked = jnp.where((lanes >= low) & (lanes < low + rank), total[...], 0.0)
        folded = picked[:, :rank]
        for q in range(1, total.shape[1] // rank):
            folded = folded + picked[:, q * rank : (q + 1) * rank]
        out[...] = folded


def shrink(place, xs, ws, column, rank):
    half = min(x.shape[1] for x in xs)
    tile = tile_of(half)
    steps = half // tile
    rows, named = sum(x.shape[0] for x in xs), sum(w.shape[0] for w in ws)

    def strip(a):
        if a.shape[1] == half:
            return pl.BlockSpec((a.shape[0], tile), lambda k, place: (0, k))
        return pl.BlockSpec((a.shape[0], tile), lambda k, place: (0, place[0] * steps + k))

    return pl.pallas_call(
        functools.partial(shrink_body, len(xs), len(ws), rank),
        grid_spec=pltpu.PrefetchScalarGridSpec(
            num_scalar_prefetch=1,
            grid=(steps,),
            in_specs=[strip(x) for x in xs]
            + [strip(w) for w in ws]
            + [pl.BlockSpec(column.shape, lambda k, place: (0, 0))],
            out_specs=pl.BlockSpec((rows, rank), lambda k, place: (0, 0)),
            scratch_shapes=[pltpu.VMEM((rows, named), jnp.float32)],
        ),
        out_shape=jax.ShapeDtypeStruct((rows, rank), jnp.float32),
        compiler_params=PARAMS,
        cost_estimate=pl.CostEstimate(
            flops=2 * rows * named * half,
            bytes_accessed=2 * half * (rows + named),
            transcendentals=0,
        ),
    )(place, *xs, *ws, column)


def expand_body(chip_cap, device_cap, place_ref, one_ref, two_ref, column_ref, up_ref, *outs):
    rank, named = one_ref.shape[1], up_ref.shape[0]
    row = lax.broadcasted_iota(jnp.int32, (rank, named), 0)
    lane = lax.broadcasted_iota(jnp.int32, (rank, named), 1)
    spread = jnp.zeros((rank, named), jnp.float32)
    for q in range(named // rank):
        spread = jnp.where(lane == row + q * rank, 1.0, spread)
    spread = spread.astype(jnp.bfloat16)
    lanes = lax.broadcasted_iota(jnp.int32, (device_cap, named), 1)
    for i, out in enumerate(outs):
        front, back = i * chip_cap, (i + 1) * chip_cap - device_cap

        def window(ref):
            a, b = ref[front : front + device_cap, :], ref[back : back + device_cap, :]
            return jnp.where(place_ref[0] == 0, a, b)

        shrunk = (window(one_ref) + window(two_ref)).astype(jnp.bfloat16)
        low = window(column_ref) * rank
        wide = jnp.dot(shrunk, spread, preferred_element_type=jnp.float32)
        wide = jnp.where((lanes >= low) & (lanes < low + rank), wide, 0.0).astype(jnp.bfloat16)
        out[...] = jnp.dot(wide, up_ref[...], preferred_element_type=jnp.float32).astype(
            out.dtype
        )


def expand(place, one, two, column, up, number, device_cap):
    chip_cap = one.shape[0] // number
    return pl.pallas_call(
        functools.partial(expand_body, chip_cap, device_cap),
        in_specs=[pl.BlockSpec(memory_space=pltpu.SMEM)]
        + [pl.BlockSpec(memory_space=pltpu.VMEM) for _ in range(4)],
        out_specs=[pl.BlockSpec(memory_space=pltpu.VMEM) for _ in range(number)],
        out_shape=[jax.ShapeDtypeStruct((device_cap, up.shape[1]), up.dtype)] * number,
        compiler_params=PARAMS,
        cost_estimate=pl.CostEstimate(
            flops=2 * number * device_cap * up.shape[0] * up.shape[1],
            bytes_accessed=2 * up.size + 8 * one.size,
            transcendentals=0,
        ),
    )(place, one, two, column, up)


def make_local(mesh_shape):
    owners, groups = mesh_shape["own"], mesh_shape["grp"]
    planes = owners // LANES

    def send(x, shift):
        pairs = [
            (z * LANES + lane, (z + shift) % planes * LANES + lane)
            for z in range(planes)
            for lane in range(LANES)
        ]
        return lax.ppermute(x, "own", pairs)

    def swap(x, flip):
        return lax.ppermute(x, "own", [(i, i ^ flip) for i in range(owners)])

    def swap_group(x, group, flip):
        pairs = [
            (g * owners + i, (g + group) % groups * owners + (i ^ flip))
            for g in range(groups)
            for i in range(owners)
        ]
        return lax.ppermute(x, ("grp", "own"), pairs)

    def local(
        tokens,
        adapter_index_rows,
        adapter_pool_position,
        base_value_matrix,
        lowrank_down_weight,
        lowrank_up_weight,
    ):
        rows, width = tokens.shape
        held, rank, _ = lowrank_down_weight.shape
        out_width = base_value_matrix.shape[1]
        total = adapter_pool_position.shape[0]
        most = max(2, 2 * rows // total)
        cap = min(rows, LANES * held * most)
        levels = [(2 * cap * k // 16, cap * 3 // 4) for k in (10, 11, 12)] + [(2 * cap, cap)]
        shifts = sorted(range(1, planes), key=lambda s: -min(s, planes - s))
        half = width // 2

        me = lax.axis_index("own")
        plane, lane, core = me // LANES, me % LANES, me % 2
        place = jnp.stack([core, plane]).astype(jnp.int32)

        chosen = adapter_index_rows[:, 0]
        table = jnp.arange(total, dtype=jnp.int32)
        slot = jnp.sum(
            jnp.where(chosen[:, None] == table[None, :], adapter_pool_position[None, :], 0), axis=1
        )
        goes_to = slot // (held * LANES)
        places = jnp.arange(rows, dtype=jnp.int32)
        earlier = (goes_to[:, None] == goes_to[None, :]) & (places[None, :] < places[:, None])
        within = jnp.sum(earlier.astype(jnp.int32), axis=1)
        mine = (slot * rows + within)[None, :]
        mate = swap(mine, 1)

        mate, wide_tokens, wide_down, up = lax.optimization_barrier(
            (
                mate,
                tokens,
                lowrank_down_weight.reshape(held * rank, width),
                lowrank_up_weight.reshape(held * rank, out_width),
            )
        )
        other_half = lambda x: lax.dynamic_slice_in_dim(x, (1 - core) * half, half, axis=1)
        mate_tokens = swap(other_half(wide_tokens), 1)
        mate_down = swap(other_half(wide_down), 1)
        kept_down = lax.dynamic_slice_in_dim(wide_down, core * half, half, axis=1)
        up = jnp.concatenate([up, swap(up, 1)], axis=0)
        up = jnp.concatenate([up, swap(up, 2)], axis=0)

        span = rows * held * LANES
        starts = [(p * span, (p + 1) * span) for p in range(planes)]
        payload = count(place, mine, mate, starts, levels)
        info, level = payload[:2], payload[2:]
        infos = {s: send(payload, s) for s in shifts}
        for s in shifts:
            level = jnp.maximum(level, infos[s][2:])
        others = [
            swap_group(level, g, flip)
            for g in range(groups)
            for flip in (0, 2)
            if g or flip
        ]
        for other in others:
            level = jnp.maximum(level, other)
        level = level[0, 0]
        goes_to, within = info // span, info % rows

        def column_of(packed):
            slot = packed // rows
            return ((slot // held) % LANES ^ lane) * held + slot % held

        def at_level(chip_cap, device_cap):
            def spot_of(packed, size):
                from_front = packed % rows
                return jnp.where(
                    jnp.stack([core, 1 - core])[: packed.shape[0], None] == 0,
                    from_front,
                    size - 1 - from_front,
                )

            def branch(
                tokens, mate_tokens, info, goes_to, within, infos, kept_down, mate_down, up, matrix
            ):
                packed = pack(
                    place, goes_to, within, tokens, mate_tokens, chip_cap, shifts, planes
                )
                arrived = [send(x, s) for x, s in zip(packed, shifts)]
                down = [kept_down, mate_down]
                down = down + [swap(x, 2) for x in down]

                base = jnp.dot(tokens, matrix, preferred_element_type=jnp.float32)
                spots = jnp.arange(chip_cap, dtype=jnp.int32)
                columns = []
                for got in infos:
                    got = got[:2]
                    spot = jnp.where(got // span == plane, spot_of(got, chip_cap), -1)
                    columns.append(
                        jnp.sum(
                            jnp.where(
                                spots[:, None] == spot.reshape(1, -1),
                                column_of(got).reshape(1, -1) + 1,
                                0,
                            ),
                            axis=1,
                            keepdims=True,
                        )
                        - 1
                    )
                columns = jnp.concatenate(columns, axis=0)
                stays = jnp.where(goes_to == plane, column_of(info), -1).reshape(-1, 1)
                own = shrink(place, [tokens, mate_tokens], down, stays, rank)
                (own_delta,) = expand(
                    place, own[:rows], swap(own[rows:], 1), stays[:rows], up, 1, rows
                )
                out = base + own_delta.astype(jnp.float32)
                arrived, columns, out = lax.optimization_barrier((arrived, columns, out))

                sums = shrink(place, arrived, down, columns, rank)
                deltas = expand(place, sums, swap(sums, 1), columns, up, len(shifts), device_cap)
                home = [send(x, -s) for x, s in zip(deltas, shifts)]
                spots = jnp.arange(device_cap, dtype=jnp.int32)
                for s, back in zip(shifts, home):
                    spot = spot_of(info[:1], device_cap)
                    spot = jnp.where(goes_to[:1] == (plane + s) % planes, spot, -1)
                    hot = (spots[None, :] == spot.reshape(-1, 1)).astype(jnp.bfloat16)
                    out = out + jnp.dot(hot, back, preferred_element_type=jnp.float32)
                return out.astype(jnp.bfloat16)

            return branch

        return lax.switch(
            level,
            [at_level(*sizes) for sizes in levels],
            tokens,
            mate_tokens,
            info,
            goes_to,
            within,
            [infos[s] for s in shifts],
            kept_down,
            mate_down,
            up,
            base_value_matrix,
        )

    return local


def solution(mesh):
    in_specs = (
        P(("grp", "own"), None),
        P(("grp", "own"), None),
        P("grp"),
        P(),
        P(("grp", "own"), None, None),
        P(("grp", "own"), None, None),
    )
    out_specs = P(("grp", "own"), None)
    return jax.shard_map(
        make_local(dict(mesh.shape)),
        mesh=mesh,
        in_specs=in_specs,
        out_specs=out_specs,
        check_vma=False,
    )
```

time: 135 us -> 111 us (0.82)
  blocking collectives: 99.9 us -> 0 us
  waiting for transfers between devices: 10 us -> 51.7 us
  Pallas kernels: 0 us -> 17.4 us
  starting transfers between devices: 5.3 us -> 21.2 us
  other arithmetic: 1.09 us -> 5.46 us
  local copies, waits for them, and re-layouts: 8.55 us -> 6.52 us
  matrix products: 9.53 us -> 7.77 us
    all_to_all x1 -> x0, blocking collectives: 99.9 us -> none  [local(): lax.all_to_all(outbound_rows, 'own', split_axis=0, concat_axis=0, tiled=T...]
    ppermute x0 -> x21, waiting for transfers between devices: none -> 51.7 us  [the longest x9 41 us: swap(): return lax.ppermute(x, 'own', [(i, i ^ flip) for i in range(owners)])]
    ppermute x0 -> x21, starting transfers between devices: none -> 21.2 us  [the longest x9 12.8 us: send(): return lax.ppermute(x, 'own', pairs)]
    pallas_call x0 -> x6, Pallas kernels: none -> 17.4 us  [the longest x2 9.46 us: shrink(): pl.pallas_call(functools.partial(shrink_body, len(xs), len(ws), rank), gr...]
    all_to_all x1 -> x0, waiting for transfers between devices: 10 us -> none  [local(): lax.all_to_all(computed, 'own', split_axis=0, concat_axis=0, tiled=True)]
    scatter x1 -> x0, local copies, waits for them, and re-layouts: 6.98 us -> none  [local(): jnp.zeros((total * depth, width), tokens.dtype).at[target].set(tokens)]
    all_to_all x1 -> x0, starting transfers between devices: 5.3 us -> none  [local(): lax.all_to_all(computed, 'own', split_axis=0, concat_axis=0, tiled=True)]
    dynamic_slice x0 -> x3, local copies, waits for them, and re-layouts: none -> 4.76 us  [the longest x2 3.45 us: local(): lax.dynamic_slice_in_dim(x, (1 - core) * half, half, axis=1)]
  transfers between devices with their start and end apart: 1 -> 21, of which waited for: 1 -> 12; matrix products, arithmetic and copies ran while one was open for 0% -> 13% of each run, Pallas kernels for 0% -> 7%
where the time goes in v2:
time: 111 us
  waiting for transfers between devices  51.7 us (47%)
  starting transfers between devices  21.2 us (19%)
  Pallas kernels  17.4 us (16%)
  matrix products  7.77 us (7%)
  local copies, waits for them, and re-layouts  6.52 us (6%)
  other arithmetic  5.46 us (5%)
    ppermute x9, waiting for transfers between devices, swap(): return lax.ppermute(x, 'own', [(i, i ^ flip) for i in range(owners)])  41 us
    ppermute x9, starting transfers between devices, send(): return lax.ppermute(x, 'own', pairs)  12.8 us
    ppermute x9, waiting for transfers between devices, send(): return lax.ppermute(x, 'own', pairs)  9.73 us
    pallas_call x2, Pallas kernels, shrink(): pl.pallas_call(functools.partial(shrink_body, len(xs), len(ws), rank), gr...  9.46 us
    dot_general x1, matrix products, branch(): base = jnp.dot(tokens, matrix, preferred_element_type=jnp.float32)  6.15 us
    ppermute x9, starting transfers between devices, swap(): return lax.ppermute(x, 'own', [(i, i ^ flip) for i in range(owners)])  4.93 us
    ppermute x3, starting transfers between devices, swap_group(): return lax.ppermute(x, ('grp', 'own'), pairs)  3.49 us
    pallas_call x1, Pallas kernels, pack(): pl.pallas_call(functools.partial(pack_body, shifts, planes), grid_spec=pl...  3.46 us
  transfers between devices with their start and end apart: 21, of which 12 were waited for; matrix products, arithmetic and copies ran while one was open for 13% of the time, Pallas kernels for 7%

profile of v2, /device:TPU:0, one launch (start us, length us, event | category | flops | bytes accessed | tf_op | source)
XLA Modules:
  0.0 110.6 jit_solution(1218953821777200275)
XLA Ops:
  2.3 2.4 %constant_dynamic-slice_fusion.5 = bf16[128,4096]{1,0:T(8,128)(2,1)} fusion(bf16[128,8192]{1,0:T(8,128)(2,1)} %param.10, s32[]{:T(128)S(6)} %select_n.668), kind=kLoop, calls=%fused_computation.577 | loop fusion | bytes 2097156 | tf_op jit(solution)/shard_map/dynamic_slice | solution.py:264
  5.0 1.1 constant_dynamic-slice_fusion.4
  6.4 1.4 %shard_map.72 = s32[3,128]{1,0:T(4,128)} custom-call(s32[2]{0:T(128)S(1)} %pad_add_fusion.4.place_ref, s32[1,128]{1,0:T(1,128)} %copy-done.16, s32[1,128]{1,0:T(1,128)} %copy-done.17), custom_call_target="tpu_custom_call" | custom-call | tf_op jit(solution)/shard_map/pallas_call | solution.py:41
  7.7 4.9 %collective-permute-start.43 = (s32[3,128]{1,0:T(4,128)}, s32[3,128]{1,0:T(4,128)S(1)}, u32[]{:S(2)}, u32[]{:S(2)}) collective-permute-start(s32[3,128]{1,0:T(4,128)} %shard_map.72), channel_id=1, source_target_pairs={{0,12},{1,13},{2,14},{3,15},{4,0},{5,1},{6,2},{7,3},{8,4},{9,5},{1... | collective-permute-start | bytes 4616 | tf_op jit(solution)/shard_map/ppermute | solution.py:209
  12.6 1.0 collective-permute-start.41
  14.2 4.1 %collective-permute-done.42 = s32[3,128]{1,0:T(4,128)S(1)} collective-permute-done((s32[3,128]{1,0:T(4,128)}, s32[3,128]{1,0:T(4,128)S(1)}, u32[]{:S(2)}, u32[]{:S(2)}) %collective-permute-start.42) | collective-permute-done | bytes 1568 | tf_op jit(solution)/shard_map/ppermute | solution.py:209
  18.9 2.4 %collective-permute-start.46 = (s32[1,128]{1,0:T(1,128)S(1)}, s32[1,128]{1,0:T(1,128)S(1)}, u32[]{:S(2)}, u32[]{:S(2)}) collective-permute-start(s32[1,128]{1,0:T(1,128)S(1)} %slice_maximum_fusion), channel_id=1, source_target_pairs={{0,18},{1,19},{2,16},{3,17},{4,22},{5,23},{6,20},{7,21},{8,26},{9,... | collective-permute-start | bytes 1544 | tf_op jit(solution)/shard_map/ppermute | solution.py:220
  22.4 0.9 collective-permute-done.46
  23.4 1.5 %collective-permute-start.50 = (bf16[256,512]{1,0:T(8,128)(2,1)S(1)}, bf16[256,512]{1,0:T(8,128)(2,1)S(1)}, u32[]{:S(2)}, u32[]{:S(2)}) collective-permute-start(bf16[256,512]{1,0:T(8,128)(2,1)S(1)} %pad_maximum_fusion.1), channel_id=1, source_target_pairs={{0,2},{1,3},{2,0},{3,1},{4,6},{5,7},{6,4},{7,5},{8,10},{9,11},{10,... | collective-permute-start | bytes 786440 | tf_op jit(solution)/shard_map/ppermute | solution.py:212
  26.3 3.4 %collective-permute-done.50 = bf16[256,512]{1,0:T(8,128)(2,1)S(1)} collective-permute-done((bf16[256,512]{1,0:T(8,128)(2,1)S(1)}, bf16[256,512]{1,0:T(8,128)(2,1)S(1)}, u32[]{:S(2)}, u32[]{:S(2)}) %collective-permute-start.50) | collective-permute-done | bytes 262176 | tf_op jit(solution)/shard_map/ppermute | solution.py:212
  29.7 0.8 pad_maximum_fusion
  30.6 79.4 %conditional.3 = (bf16[128,512]{1,0:T(8,128)(2,1)S(1)}) conditional(s32[]{:T(128)} %bitcast.70, (s32[2,128]{1,0:T(2,128)S(1)}, pred[2,128]{1,0:T(4,128)(4,1)S(1)}, pred[2,128]{1,0:T(4,128)(4,1)S(1)}, s32[2,128]{1,0:T(2,128)S(1)}, s32[2]{0:T(128)S(1)}, /*index=5*/bf16[128,8192]{1,0:T(8,128)(2,1)S(1)}, ...), branch_computations={%region_2.6_spmd, %region_6.10_spmd, %region_10.14_spmd, %region_1... | conditional | flops 4757126144 | bytes 82946552
  30.7 3.5 %branch_0_fun.5 = (bf16[80,4096]{1,0:T(8,128)(2,1)}, bf16[80,4096]{1,0:T(8,128)(2,1)}, bf16[80,4096]{1,0:T(8,128)(2,1)}) custom-call(s32[2]{0:T(128)S(1)} %get-tuple-element.421.place_ref, s32[2,128]{1,0:T(2,128)S(1)} %get-tuple-element.575.goes_ref, s32[2,128]{1,0:T(2,128)S(1)} %get-tuple-element.590.within_ref, ...), custom_call_target="tpu_custom_call" | custom-call | flops 503316480 | bytes 4063232 | tf_op jit(solution)/shard_map/cond/branch_0_fun/pallas_call | solution.py:75
  34.2 3.4 %collective-permute-start.1 = (bf16[80,4096]{1,0:T(8,128)(2,1)}, bf16[80,4096]{1,0:T(8,128)(2,1)}, u32[]{:S(2)}, u32[]{:S(2)}) collective-permute-start(bf16[80,4096]{1,0:T(8,128)(2,1)} %get-tuple-element.429), channel_id=1, source_target_pairs={{0,4},{1,5},{2,6},{3,7},{4,8},{5,9},{6,10},{7,11},{8,12},{9,13},{1... | collective-permute-start | bytes 1966088 | tf_op jit(solution)/shard_map/cond/branch_0_fun/ppermute | solution.py:209
  38.1 1.3 %constant_dynamic-slice_fusion.refs_2_.refs_3_ = bf16[128,4096]{1,0:T(8,128)(2,1)S(1)} fusion(bf16[128,8192]{1,0:T(8,128)(2,1)} %get-tuple-element.439, s32[]{:T(128)S(6)} %select_n.513), kind=kLoop, calls=%fused_computation.139 | loop fusion | bytes 2097156 | tf_op jit(solution)/shard_map/dynamic_slice | solution.py:267
  39.4 1.6 %collective-permute-start.3 = (bf16[128,4096]{1,0:T(8,128)(2,1)S(1)}, bf16[128,4096]{1,0:T(8,128)(2,1)S(1)}, u32[]{:S(2)}, u32[]{:S(2)}) collective-permute-start(bf16[128,4096]{1,0:T(8,128)(2,1)S(1)} %constant_dynamic-slice_fusion.refs_2_.refs_3_), channel_id=1, source_target_pairs={{0,2},{1,3},{2,0},{3,1},{4,6},{5,7},{6,4},{7,5},{8,10},{9,11},{10,... | collective-permute-start | bytes 3145736 | tf_op jit(solution)/shard_map/cond/branch_0_fun/ppermute | solution.py:212
  42.1 6.1 %fusion.121 = f32[128,512]{1,0:T(8,128)} fusion(bf16[128,8192]{1,0:T(8,128)(2,1)} %copy-done.1, bf16[8192,512]{1,0:T(8,128)(2,1)} %get-tuple-element.566), kind=kOutput, calls=%fused_computation.582 | convolution fusion | flops 1073741824 | bytes 10747904 | tf_op jit(solution)/shard_map/cond/branch_0_fun/dot_general | solution.py:312
  48.2 17.3 %collective-permute-done.3.refs_4_.refs_5_ = bf16[128,4096]{1,0:T(8,128)(2,1)S(1)} collective-permute-done((bf16[128,4096]{1,0:T(8,128)(2,1)S(1)}, bf16[128,4096]{1,0:T(8,128)(2,1)S(1)}, u32[]{:S(2)}, u32[]{:S(2)}) %collective-permute-start.3) | collective-permute-done | bytes 1048608 | tf_op jit(solution)/shard_map/cond/branch_0_fun/ppermute | solution.py:212
  65.6 17.3 %collective-permute-done.4.refs_5_.refs_6_ = bf16[128,4096]{1,0:T(8,128)(2,1)S(1)} collective-permute-done((bf16[128,4096]{1,0:T(8,128)(2,1)}, bf16[128,4096]{1,0:T(8,128)(2,1)S(1)}, u32[]{:S(2)}, u32[]{:S(2)}) %collective-permute-start.4) | collective-permute-done | bytes 1048608 | tf_op jit(solution)/shard_map/cond/branch_0_fun/ppermute | solution.py:212
  82.8 4.6 %branch_0_fun.6 = f32[256,64]{1,0:T(8,128)S(1)} custom-call(s32[2]{0:T(128)S(1)} %get-tuple-element.421.place_ref, bf16[128,8192]{1,0:T(8,128)(2,1)S(1)} %copy-done.2, bf16[128,4096]{1,0:T(8,128)(2,1)S(1)} %copy-done.8, bf16[128,4096]{1,0:T(8,128)(2,1)S(1)} %constant_dynamic-slice_fusion.refs_2_.refs_3_, ...), custom_call_target="tpu_custom_call" | custom-call | flops 1073741824 | bytes 6291456 | tf_op jit(solution)/shard_map/cond/branch_0_fun/pallas_call | solution.py:136
  87.7 1.0 collective-permute-done.5.two_ref
  88.7 1.4 %branch_0_fun.7 = bf16[128,512]{1,0:T(8,128)(2,1)S(1)} custom-call(s32[2]{0:T(128)S(1)} %get-tuple-element.421.place_ref, f32[128,64]{1,0:T(8,128)S(1)} %get-tuple-element.589.one_ref, f32[128,64]{1,0:T(8,128)S(1)} %collective-permute-done.5.two_ref, s32[128,1]{1,0:T(8,128)S(1)} %copy.68.column_ref, bf16[512,512]{1,0:T(8,128)(2,1)} %get-tuple-element.441.up_ref), custom_call_target="tpu_custom_call" | custom-call | flops 67108864 | bytes 589824 | tf_op jit(solution)/shard_map/cond/branch_0_fun/pallas_call | solution.py:184
  90.2 1.7 %convert_add_fusion = f32[128,512]{1,0:T(8,128)} fusion(f32[128,512]{1,0:T(8,128)} %fusion.121, bf16[128,512]{1,0:T(8,128)(2,1)S(1)} %branch_0_fun.7), kind=kLoop, calls=%fused_computation.1 | loop fusion | flops 131072 | bytes 655360 | tf_op jit(solution)/shard_map/cond/branch_0_fun/add | solution.py:336
  92.0 4.9 %branch_0_fun.8.one_ref = f32[240,64]{1,0:T(8,128)S(1)} custom-call(s32[2]{0:T(128)S(1)} %get-tuple-element.421.place_ref, bf16[80,4096]{1,0:T(8,128)(2,1)} %collective-permute-done.refs_0_, bf16[80,4096]{1,0:T(8,128)(2,1)} %collective-permute-done.1.refs_1_, bf16[80,4096]{1,0:T(8,128)(2,1)} %collective-permute-done.2.refs_2_, ...), custom_call_target="tpu_custom_call" | custom-call | flops 1006632960 | bytes 6160384 | tf_op jit(solution)/shard_map/cond/branch_0_fun/pallas_call | solution.py:136
  97.2 1.1 %collective-permute-done.6.two_ref = f32[240,64]{1,0:T(8,128)S(1)} collective-permute-done((f32[240,64]{1,0:T(8,128)S(1)}, f32[240,64]{1,0:T(8,128)S(1)}, u32[]{:S(2)}, u32[]{:S(2)}) %collective-permute-start.6) | collective-permute-done | bytes 61472 | tf_op jit(solution)/shard_map/cond/branch_0_fun/ppermute | solution.py:212
  98.3 1.7 %branch_0_fun.9 = (bf16[48,512]{1,0:T(8,128)(2,1)S(1)}, bf16[48,512]{1,0:T(8,128)(2,1)S(1)}, bf16[48,512]{1,0:T(8,128)(2,1)S(1)}) custom-call(s32[2]{0:T(128)S(1)} %get-tuple-element.421.place_ref, f32[240,64]{1,0:T(8,128)S(1)} %branch_0_fun.8.one_ref, f32[240,64]{1,0:T(8,128)S(1)} %collective-permute-done.6.two_ref, s32[240,1]{1,0:T(8,128)S(1)} %copy.69.refs_7_.column_ref, ...), custom_call_target="tpu_custom_call" | custom-call | flops 75497472 | bytes 647168 | tf_op jit(solution)/shard_map/cond/branch_0_fun/pallas_call | solution.py:184
  100.1 0.9 collective-permute-start.8
  101.0 1.7 %collective-permute-start.7 = (bf16[48,512]{1,0:T(8,128)(2,1)S(1)}, bf16[48,512]{1,0:T(8,128)(2,1)S(1)}, u32[]{:S(2)}, u32[]{:S(2)}) collective-permute-start(bf16[48,512]{1,0:T(8,128)(2,1)S(1)} %get-tuple-element.447), channel_id=1, source_target_pairs={{0,8},{1,9},{2,10},{3,11},{4,12},{5,13},{6,14},{7,15},{8,0},{9,1},... | collective-permute-start | bytes 147464 | tf_op jit(solution)/shard_map/cond/branch_0_fun/ppermute | solution.py:209
  103.0 1.2 %collective-permute-done.8 = bf16[48,512]{1,0:T(8,128)(2,1)S(1)} collective-permute-done((bf16[48,512]{1,0:T(8,128)(2,1)S(1)}, bf16[48,512]{1,0:T(8,128)(2,1)S(1)}, u32[]{:S(2)}, u32[]{:S(2)}) %collective-permute-start.8) | collective-permute-done | bytes 49184 | tf_op jit(solution)/shard_map/cond/branch_0_fun/ppermute | solution.py:209
  104.4 3.0 %collective-permute-done.7 = bf16[48,512]{1,0:T(8,128)(2,1)S(1)} collective-permute-done((bf16[48,512]{1,0:T(8,128)(2,1)S(1)}, bf16[48,512]{1,0:T(8,128)(2,1)S(1)}, u32[]{:S(2)}, u32[]{:S(2)}) %collective-permute-start.7) | collective-permute-done | bytes 49184 | tf_op jit(solution)/shard_map/cond/branch_0_fun/ppermute | solution.py:209
  107.6 1.0 collective-permute-done.9
  108.6 1.2 %add_add_fusion = bf16[128,512]{1,0:T(8,128)(2,1)S(1)} fusion(f32[128,512]{1,0:T(8,128)S(1)} %fusion.1, f32[128,512]{1,0:T(8,128)} %convert_add_fusion, f32[128,512]{1,0:T(8,128)S(1)} %fusion, bf16[48,512]{1,0:T(8,128)(2,1)S(1)} %collective-permute-done.9, s32[128]{0:T(128)S(1)} %get-tuple-element.572), kind=kOutput, calls=%fused_computation | convolution fusion | flops 6559744 | bytes 967168 | tf_op jit(solution)/shard_map/cond/branch_0_fun/dot_general | solution.py:347
  (73 shorter events, 10.2 us)
Async XLA Ops:
  1.0 5.1 %copy-start.16 = (s32[1,128]{1,0:T(1,128)}, s32[1,128]{1,0:T(1,128)S(1)}, u32[]{:S(2)}) copy-start(s32[1,128]{1,0:T(1,128)S(1)} %add_bitcast_fusion.24.mine_ref) | copy-start | bytes 1540
  1.0 1.3 %collective-permute-start.40 = (s32[1,128]{1,0:T(1,128)S(1)}, s32[1,128]{1,0:T(1,128)S(1)}, u32[]{:S(2)}, u32[]{:S(2)}) collective-permute-start(s32[1,128]{1,0:T(1,128)S(1)} %add_bitcast_fusion.24.mine_ref), channel_id=1, source_target_pairs={{0,1},{1,0},{2,3},{3,2},{4,5},{5,4},{6,7},{7,6},{8,9},{9,8},{10,11... | collective-permute-start | bytes 1544 | tf_op jit(solution)/shard_map/ppermute | solution.py:212
  1.5 3.5 %copy-start.13 = (bf16[2,64,8192]{2,1,0:T(8,128)(2,1)S(1)}, bf16[2,64,8192]{2,1,0:T(8,128)(2,1)}, u32[]{:S(2)}) copy-start(bf16[2,64,8192]{2,1,0:T(8,128)(2,1)} %param.14) | copy-start | bytes 6291460
  2.3 3.8 %copy-start.17 = (s32[1,128]{1,0:T(1,128)}, s32[1,128]{1,0:T(1,128)S(1)}, u32[]{:S(2)}) copy-start(s32[1,128]{1,0:T(1,128)S(1)} %collective-permute-done.40.mate_ref) | copy-start | bytes 1540
  2.3 11.8 %copy-start.14 = (bf16[2,64,512]{2,1,0:T(8,128)(2,1)S(1)}, bf16[2,64,512]{2,1,0:T(8,128)(2,1)}, u32[]{:S(2)}) copy-start(bf16[2,64,512]{2,1,0:T(8,128)(2,1)} %param.15) | copy-start | bytes 393220
  4.7 25.9 %copy-start = (bf16[128,8192]{1,0:T(8,128)(2,1)S(1)}, bf16[128,8192]{1,0:T(8,128)(2,1)}, u32[]{:S(2)}) copy-start(bf16[128,8192]{1,0:T(8,128)(2,1)} %param.10) | copy-start | bytes 6291460
  4.7 25.9 %collective-permute-start.47 = (bf16[128,4096]{1,0:T(8,128)(2,1)}, bf16[128,4096]{1,0:T(8,128)(2,1)S(1)}, u32[]{:S(2)}, u32[]{:S(2)}) collective-permute-start(bf16[128,4096]{1,0:T(8,128)(2,1)} %constant_dynamic-slice_fusion.5), channel_id=1, source_target_pairs={{0,1},{1,0},{2,3},{3,2},{4,5},{5,4},{6,7},{7,6},{8,9},{9,8},{10,11... | collective-permute-start | bytes 3145736 | tf_op jit(solution)/shard_map/ppermute | solution.py:212
  6.1 24.5 %collective-permute-start.48 = (bf16[128,4096]{1,0:T(8,128)(2,1)}, bf16[128,4096]{1,0:T(8,128)(2,1)}, u32[]{:S(2)}, u32[]{:S(2)}) collective-permute-start(bf16[128,4096]{1,0:T(8,128)(2,1)} %constant_dynamic-slice_fusion.4), channel_id=1, source_target_pairs={{0,1},{1,0},{2,3},{3,2},{4,5},{5,4},{6,7},{7,6},{8,9},{9,8},{10,11... | collective-permute-start | bytes 3145736 | tf_op jit(solution)/shard_map/ppermute | solution.py:212
  7.7 6.4 %collective-permute-start.43 = (s32[3,128]{1,0:T(4,128)}, s32[3,128]{1,0:T(4,128)S(1)}, u32[]{:S(2)}, u32[]{:S(2)}) collective-permute-start(s32[3,128]{1,0:T(4,128)} %shard_map.72), channel_id=1, source_target_pairs={{0,12},{1,13},{2,14},{3,15},{4,0},{5,1},{6,2},{7,3},{8,4},{9,5},{1... | collective-permute-start | bytes 4616 | tf_op jit(solution)/shard_map/ppermute | solution.py:209
  12.6 5.6 %collective-permute-start.42 = (s32[3,128]{1,0:T(4,128)}, s32[3,128]{1,0:T(4,128)S(1)}, u32[]{:S(2)}, u32[]{:S(2)}) collective-permute-start(s32[3,128]{1,0:T(4,128)} %shard_map.72), channel_id=1, source_target_pairs={{0,4},{1,5},{2,6},{3,7},{4,8},{5,9},{6,10},{7,11},{8,12},{9,13},{1... | collective-permute-start | bytes 4616 | tf_op jit(solution)/shard_map/ppermute | solution.py:209
  12.6 5.6 %collective-permute-start.41 = (s32[3,128]{1,0:T(4,128)}, s32[3,128]{1,0:T(4,128)S(1)}, u32[]{:S(2)}, u32[]{:S(2)}) collective-permute-start(s32[3,128]{1,0:T(4,128)} %shard_map.72), channel_id=1, source_target_pairs={{0,8},{1,9},{2,10},{3,11},{4,12},{5,13},{6,14},{7,15},{8,0},{9,1},... | collective-permute-start | bytes 4616 | tf_op jit(solution)/shard_map/ppermute | solution.py:209
  14.1 7.8 %collective-permute-start.49 = (bf16[128,512]{1,0:T(8,128)(2,1)S(1)}, bf16[128,512]{1,0:T(8,128)(2,1)S(1)}, u32[]{:S(2)}, u32[]{:S(2)}) collective-permute-start(bf16[128,512]{1,0:T(8,128)(2,1)S(1)} %bitcast.150), channel_id=1, source_target_pairs={{0,1},{1,0},{2,3},{3,2},{4,5},{5,4},{6,7},{7,6},{8,9},{9,8},{10,11... | collective-permute-start | bytes 393224 | tf_op jit(solution)/shard_map/ppermute | solution.py:212
  18.9 4.4 %collective-permute-start.46 = (s32[1,128]{1,0:T(1,128)S(1)}, s32[1,128]{1,0:T(1,128)S(1)}, u32[]{:S(2)}, u32[]{:S(2)}) collective-permute-start(s32[1,128]{1,0:T(1,128)S(1)} %slice_maximum_fusion), channel_id=1, source_target_pairs={{0,18},{1,19},{2,16},{3,17},{4,22},{5,23},{6,20},{7,21},{8,26},{9,... | collective-permute-start | bytes 1544 | tf_op jit(solution)/shard_map/ppermute | solution.py:220
  21.4 4.9 %collective-permute-start.45 = (s32[1,128]{1,0:T(1,128)S(1)}, s32[1,128]{1,0:T(1,128)S(1)}, u32[]{:S(2)}, u32[]{:S(2)}) collective-permute-start(s32[1,128]{1,0:T(1,128)S(1)} %slice_maximum_fusion), channel_id=1, source_target_pairs={{0,16},{1,17},{2,18},{3,19},{4,20},{5,21},{6,22},{7,23},{8,24},{9,... | collective-permute-start | bytes 1544 | tf_op jit(solution)/shard_map/ppermute | solution.py:220
  21.9 4.3 %collective-permute-start.44 = (s32[1,128]{1,0:T(1,128)S(1)}, s32[1,128]{1,0:T(1,128)S(1)}, u32[]{:S(2)}, u32[]{:S(2)}) collective-permute-start(s32[1,128]{1,0:T(1,128)S(1)} %slice_maximum_fusion), channel_id=1, source_target_pairs={{0,2},{1,3},{2,0},{3,1},{4,6},{5,7},{6,4},{7,5},{8,10},{9,11},{10,... | collective-permute-start | bytes 1544 | tf_op jit(solution)/shard_map/ppermute | solution.py:220
  23.4 6.4 %collective-permute-start.50 = (bf16[256,512]{1,0:T(8,128)(2,1)S(1)}, bf16[256,512]{1,0:T(8,128)(2,1)S(1)}, u32[]{:S(2)}, u32[]{:S(2)}) collective-permute-start(bf16[256,512]{1,0:T(8,128)(2,1)S(1)} %pad_maximum_fusion.1), channel_id=1, source_target_pairs={{0,2},{1,3},{2,0},{3,1},{4,6},{5,7},{6,4},{7,5},{8,10},{9,11},{10,... | collective-permute-start | bytes 786440 | tf_op jit(solution)/shard_map/ppermute | solution.py:212
  30.6 7.5 %copy-start.1 = (bf16[128,8192]{1,0:T(8,128)(2,1)}, bf16[128,8192]{1,0:T(8,128)(2,1)S(1)}, u32[]{:S(2)}) copy-start(bf16[128,8192]{1,0:T(8,128)(2,1)S(1)} %get-tuple-element.426.kept_ref.refs_0_) | copy-start | bytes 6291460
  30.6 8.8 %copy-start.7 = (bf16[128,4096]{1,0:T(8,128)(2,1)}, bf16[128,4096]{1,0:T(8,128)(2,1)S(1)}, u32[]{:S(2)}) copy-start(bf16[128,4096]{1,0:T(8,128)(2,1)S(1)} %get-tuple-element.427.mate_ref.refs_1_) | copy-start | bytes 3145732
  34.1 57.8 %collective-permute-start = (bf16[80,4096]{1,0:T(8,128)(2,1)}, bf16[80,4096]{1,0:T(8,128)(2,1)}, u32[]{:S(2)}, u32[]{:S(2)}) collective-permute-start(bf16[80,4096]{1,0:T(8,128)(2,1)} %get-tuple-element.428), channel_id=1, source_target_pairs={{0,8},{1,9},{2,10},{3,11},{4,12},{5,13},{6,14},{7,15},{8,0},{9,1},... | collective-permute-start | bytes 1966088 | tf_op jit(solution)/shard_map/cond/branch_0_fun/ppermute | solution.py:209
  34.2 57.6 %collective-permute-start.1 = (bf16[80,4096]{1,0:T(8,128)(2,1)}, bf16[80,4096]{1,0:T(8,128)(2,1)}, u32[]{:S(2)}, u32[]{:S(2)}) collective-permute-start(bf16[80,4096]{1,0:T(8,128)(2,1)} %get-tuple-element.429), channel_id=1, source_target_pairs={{0,4},{1,5},{2,6},{3,7},{4,8},{5,9},{6,10},{7,11},{8,12},{9,13},{1... | collective-permute-start | bytes 1966088 | tf_op jit(solution)/shard_map/cond/branch_0_fun/ppermute | solution.py:209
  37.6 54.3 %collective-permute-start.2 = (bf16[80,4096]{1,0:T(8,128)(2,1)}, bf16[80,4096]{1,0:T(8,128)(2,1)}, u32[]{:S(2)}, u32[]{:S(2)}) collective-permute-start(bf16[80,4096]{1,0:T(8,128)(2,1)} %get-tuple-element.430), channel_id=1, source_target_pairs={{0,12},{1,13},{2,14},{3,15},{4,0},{5,1},{6,2},{7,3},{8,4},{9,5},{1... | collective-permute-start | bytes 1966088 | tf_op jit(solution)/shard_map/cond/branch_0_fun/ppermute | solution.py:209
  39.4 26.2 %collective-permute-start.3 = (bf16[128,4096]{1,0:T(8,128)(2,1)S(1)}, bf16[128,4096]{1,0:T(8,128)(2,1)S(1)}, u32[]{:S(2)}, u32[]{:S(2)}) collective-permute-start(bf16[128,4096]{1,0:T(8,128)(2,1)S(1)} %constant_dynamic-slice_fusion.refs_2_.refs_3_), channel_id=1, source_target_pairs={{0,2},{1,3},{2,0},{3,1},{4,6},{5,7},{6,4},{7,5},{8,10},{9,11},{10,... | collective-permute-start | bytes 3145736 | tf_op jit(solution)/shard_map/cond/branch_0_fun/ppermute | solution.py:212
  41.0 41.8 %collective-permute-start.4 = (bf16[128,4096]{1,0:T(8,128)(2,1)}, bf16[128,4096]{1,0:T(8,128)(2,1)S(1)}, u32[]{:S(2)}, u32[]{:S(2)}) collective-permute-start(bf16[128,4096]{1,0:T(8,128)(2,1)} %get-tuple-element.440.refs_3_.refs_4_), channel_id=1, source_target_pairs={{0,2},{1,3},{2,0},{3,1},{4,6},{5,7},{6,4},{7,5},{8,10},{9,11},{10,... | collective-permute-start | bytes 3145736 | tf_op jit(solution)/shard_map/cond/branch_0_fun/ppermute | solution.py:212
  42.1 40.8 %copy-start.2 = (bf16[128,8192]{1,0:T(8,128)(2,1)S(1)}, bf16[128,8192]{1,0:T(8,128)(2,1)}, u32[]{:S(2)}) copy-start(bf16[128,8192]{1,0:T(8,128)(2,1)} %copy-done.1) | copy-start | bytes 6291460
  42.1 40.7 %copy-start.8 = (bf16[128,4096]{1,0:T(8,128)(2,1)S(1)}, bf16[128,4096]{1,0:T(8,128)(2,1)}, u32[]{:S(2)}) copy-start(bf16[128,4096]{1,0:T(8,128)(2,1)} %copy-done.7) | copy-start | bytes 3145732
  87.4 1.3 %collective-permute-start.5 = (f32[128,64]{1,0:T(8,128)S(1)}, f32[128,64]{1,0:T(8,128)S(1)}, u32[]{:S(2)}, u32[]{:S(2)}) collective-permute-start(f32[128,64]{1,0:T(8,128)S(1)} %get-tuple-element.588), channel_id=1, source_target_pairs={{0,1},{1,0},{2,3},{3,2},{4,5},{5,4},{6,7},{7,6},{8,9},{9,8},{10,11... | collective-permute-start | bytes 98312 | tf_op jit(solution)/shard_map/cond/branch_0_fun/ppermute | solution.py:212
  96.9 1.4 %collective-permute-start.6 = (f32[240,64]{1,0:T(8,128)S(1)}, f32[240,64]{1,0:T(8,128)S(1)}, u32[]{:S(2)}, u32[]{:S(2)}) collective-permute-start(f32[240,64]{1,0:T(8,128)S(1)} %branch_0_fun.8.one_ref), channel_id=1, source_target_pairs={{0,1},{1,0},{2,3},{3,2},{4,5},{5,4},{6,7},{7,6},{8,9},{9,8},{10,11... | collective-permute-start | bytes 184328 | tf_op jit(solution)/shard_map/cond/branch_0_fun/ppermute | solution.py:212
  100.1 4.1 %collective-permute-start.8 = (bf16[48,512]{1,0:T(8,128)(2,1)S(1)}, bf16[48,512]{1,0:T(8,128)(2,1)S(1)}, u32[]{:S(2)}, u32[]{:S(2)}) collective-permute-start(bf16[48,512]{1,0:T(8,128)(2,1)S(1)} %get-tuple-element.448), channel_id=1, source_target_pairs={{0,12},{1,13},{2,14},{3,15},{4,0},{5,1},{6,2},{7,3},{8,4},{9,5},{1... | collective-permute-start | bytes 147464 | tf_op jit(solution)/shard_map/cond/branch_0_fun/ppermute | solution.py:209
  101.0 6.4 %collective-permute-start.7 = (bf16[48,512]{1,0:T(8,128)(2,1)S(1)}, bf16[48,512]{1,0:T(8,128)(2,1)S(1)}, u32[]{:S(2)}, u32[]{:S(2)}) collective-permute-start(bf16[48,512]{1,0:T(8,128)(2,1)S(1)} %get-tuple-element.447), channel_id=1, source_target_pairs={{0,8},{1,9},{2,10},{3,11},{4,12},{5,13},{6,14},{7,15},{8,0},{9,1},... | collective-permute-start | bytes 147464 | tf_op jit(solution)/shard_map/cond/branch_0_fun/ppermute | solution.py:209
  102.7 5.9 %collective-permute-start.9 = (bf16[48,512]{1,0:T(8,128)(2,1)S(1)}, bf16[48,512]{1,0:T(8,128)(2,1)S(1)}, u32[]{:S(2)}, u32[]{:S(2)}) collective-permute-start(bf16[48,512]{1,0:T(8,128)(2,1)S(1)} %get-tuple-element.449), channel_id=1, source_target_pairs={{0,4},{1,5},{2,6},{3,7},{4,8},{5,9},{6,10},{7,11},{8,12},{9,13},{1... | collective-permute-start | bytes 147464 | tf_op jit(solution)/shard_map/cond/branch_0_fun/ppermute | solution.py:209
  110.0 0.7 copy-start.15

commit v3 on v2

v3 whole, which is shorter than its diff:
```python
import functools

import jax
import jax.numpy as jnp
from jax import lax
from jax.experimental import pallas as pl
from jax.experimental.pallas import tpu as pltpu
from jax.sharding import PartitionSpec as P

LANES = 4
MATMUL_T = (((1,), (1,)), ((), ()))
PARAMS = pltpu.CompilerParams(vmem_limit_bytes=40 * 1024 * 1024)


def tile_of(width):
    return next(t for t in (2048, 1024, 512, 256, 128, width) if width % t == 0)


def level_body(starts, levels, first, place_ref, mine_ref, mate_ref, out_ref):
    mine, mate = mine_ref[...], mate_ref[...]
    planes = mine.shape[0]
    row = lax.broadcasted_iota(jnp.int32, (planes, 1), 0)
    source = jnp.bitwise_xor(row, place_ref[1])
    level = jnp.zeros((planes, 1), jnp.int32)
    for p, (low, high) in enumerate(starts):
        counts = []
        for packed in (mine, mate):
            here = jnp.where((packed >= low) & (packed < high), 1.0, 0.0)
            number = jnp.sum(here, axis=1, keepdims=True).astype(jnp.int32) - first
            counts.append(jnp.maximum(jnp.where(source == p, 0, number), 0))
        chip_rows, device_rows = counts[0] + counts[1], jnp.maximum(*counts)
        needed = jnp.zeros((planes, 1), jnp.int32)
        for chip_cap, device_cap in levels[:-1]:
            needed += jnp.where((chip_rows > chip_cap) | (device_rows > device_cap), 1, 0)
        level = jnp.maximum(level, needed)
    highest = level[0:1, :]
    for k in range(1, planes):
        highest = jnp.maximum(highest, level[k : k + 1, :])
    out_ref[...] = jnp.broadcast_to(highest, out_ref.shape)


def level_of(place, mine, mate, starts, levels, first):
    return pl.pallas_call(
        functools.partial(level_body, starts, levels, first),
        out_shape=jax.ShapeDtypeStruct((1, mine.shape[1]), jnp.int32),
        in_specs=[
            pl.BlockSpec(memory_space=pltpu.SMEM),
            pl.BlockSpec(memory_space=pltpu.VMEM),
            pl.BlockSpec(memory_space=pltpu.VMEM),
        ],
        out_specs=pl.BlockSpec(memory_space=pltpu.VMEM),
    )(place, mine, mate)


def pack_body(flips, number, start, place_ref, goes_ref, within_ref, *refs):
    core, plane, back = place_ref[0], place_ref[1], place_ref[2]
    values, outs, hot = refs[:number], refs[number:-1], refs[-1]
    size, rows = outs[0].shape[0], values[0].shape[0]

    @pl.when(pl.program_id(0) == 0)
    def _():
        spots = lax.broadcasted_iota(jnp.int32, (size, rows), 0)
        parts = []
        for flip in flips:
            to = jnp.bitwise_xor(plane, flip)
            sides = []
            for row in range(number):
                within = within_ref[row : row + 1, :] - start
                spot = within if number == 1 else jnp.where(core == row, within, back - 1 - within)
                named = (goes_ref[row : row + 1, :] == to) & (within >= 0) & (within < size)
                sides.append(jnp.where(spots == jnp.where(named, spot, -1), 1.0, 0.0))
            parts.append(jnp.concatenate(sides, axis=1))
        hot[...] = jnp.concatenate(parts, axis=0).astype(hot.dtype)

    rows_of_chip = jnp.concatenate([v[...] for v in values], axis=0)
    packed = jnp.dot(hot[...], rows_of_chip, preferred_element_type=jnp.float32)
    for i, out in enumerate(outs):
        out[...] = packed[i * size : (i + 1) * size, :].astype(out.dtype)


def pack(place, goes_to, within, values, start, size, flips):
    number, (rows, width) = len(values), values[0].shape
    width = width // number
    tile = tile_of(width)
    steps = width // tile
    whole = lambda a: pl.BlockSpec(a.shape, lambda k, place: (0, 0))
    strip = pl.BlockSpec(
        (rows, tile), lambda k, place: (0, k if number == 1 else place[0] * steps + k)
    )
    return pl.pallas_call(
        functools.partial(pack_body, flips, number, start),
        grid_spec=pltpu.PrefetchScalarGridSpec(
            num_scalar_prefetch=1,
            grid=(steps,),
            in_specs=[whole(goes_to), whole(within)] + [strip] * number,
            out_specs=[pl.BlockSpec((size, tile), lambda k, place: (0, k)) for _ in flips],
            scratch_shapes=[pltpu.VMEM((len(flips) * size, number * rows), values[0].dtype)],
        ),
        out_shape=[jax.ShapeDtypeStruct((size, width), values[0].dtype) for _ in flips],
        compiler_params=PARAMS,
        cost_estimate=pl.CostEstimate(
            flops=2 * len(flips) * size * number * rows * width,
            bytes_accessed=2 * width * (number * rows + len(flips) * size),
            transcendentals=0,
        ),
    )(place, goes_to, within, *values)


def shrink_body(number, maps, rank, start, place_ref, *refs):
    xs, ws = refs[:number], refs[number : number + maps]
    column, out, total = refs[number + maps :]
    step = pl.program_id(0)
    rows = jnp.concatenate([x[...] for x in xs], axis=0)
    weights = jnp.concatenate([w[...] for w in ws], axis=0)
    part = lax.dot_general(rows, weights, MATMUL_T, preferred_element_type=jnp.float32)

    @pl.when(step == 0)
    def _():
        total[...] = part

    @pl.when(step != 0)
    def _():
        total[...] += part

    @pl.when(step == pl.num_programs(0) - 1)
    def _():
        lanes = lax.broadcasted_iota(jnp.int32, total.shape, 1)
        low = (column[...] - start) * rank
        picked = jnp.where((lanes >= low) & (lanes < low + rank), total[...], 0.0)
        folded = picked[:, :rank]
        for q in range(1, total.shape[1] // rank):
            folded = folded + picked[:, q * rank : (q + 1) * rank]
        out[...] = folded


def shrink(place, xs, ws, column, rank, start=0):
    half = ws[0].shape[1]
    tile = tile_of(half)
    steps = half // tile
    rows, named = sum(x.shape[0] for x in xs), sum(w.shape[0] for w in ws)

    def strip(a):
        if a.shape[1] == half:
            return pl.BlockSpec((a.shape[0], tile), lambda k, place: (0, k))
        return pl.BlockSpec((a.shape[0], tile), lambda k, place: (0, place[0] * steps + k))

    return pl.pallas_call(
        functools.partial(shrink_body, len(xs), len(ws), rank, start),
        grid_spec=pltpu.PrefetchScalarGridSpec(
            num_scalar_prefetch=1,
            grid=(steps,),
            in_specs=[strip(x) for x in xs]
            + [strip(w) for w in ws]
            + [pl.BlockSpec(column.shape, lambda k, place: (0, 0))],
            out_specs=pl.BlockSpec((rows, rank), lambda k, place: (0, 0)),
            scratch_shapes=[pltpu.VMEM((rows, named), jnp.float32)],
        ),
        out_shape=jax.ShapeDtypeStruct((rows, rank), jnp.float32),
        compiler_params=PARAMS,
        cost_estimate=pl.CostEstimate(
            flops=2 * rows * named * half,
            bytes_accessed=2 * half * (rows + named),
            transcendentals=0,
        ),
    )(place, *xs, *ws, column)


def expand_body(chip_cap, device_cap, number, place_ref, one_ref, two_ref, column_ref, up_ref, *refs):
    given, outs = (refs[0], refs[1:]) if len(refs) > number else (None, refs)
    rank, named = one_ref.shape[1], up_ref.shape[0]
    row = lax.broadcasted_iota(jnp.int32, (rank, named), 0)
    lane = lax.broadcasted_iota(jnp.int32, (rank, named), 1)
    spread = jnp.zeros((rank, named), jnp.float32)
    for q in range(named // rank):
        spread = jnp.where(lane == row + q * rank, 1.0, spread)
    spread = spread.astype(jnp.bfloat16)

    def window(ref):
        parts = []
        for i in range(number):
            front, back = i * chip_cap, (i + 1) * chip_cap - device_cap
            a, b = ref[front : front + device_cap, :], ref[back : back + device_cap, :]
            parts.append(a if front == back else jnp.where(place_ref[0] == 0, a, b))
        return jnp.concatenate(parts, axis=0)

    shrunk = (window(one_ref) + window(two_ref)).astype(jnp.bfloat16)
    low = window(column_ref) * rank
    lanes = lax.broadcasted_iota(jnp.int32, (number * device_cap, named), 1)
    wide = jnp.dot(shrunk, spread, preferred_element_type=jnp.float32)
    wide = jnp.where((lanes >= low) & (lanes < low + rank), wide, 0.0).astype(jnp.bfloat16)
    delta = jnp.dot(wide, up_ref[...], preferred_element_type=jnp.float32)
    for i, out in enumerate(outs):
        mine = delta[i * device_cap : (i + 1) * device_cap, :].astype(out.dtype)
        if given is None:
            out[...] = mine
        else:
            first = out.shape[0] - device_cap
            out[...] = jnp.concatenate([given[i * first : (i + 1) * first, :], mine], axis=0)


def expand(place, one, two, column, up, number, device_cap, given=None):
    chip_cap = one.shape[0] // number
    rows = device_cap + (0 if given is None else given.shape[0] // number)
    operands = [place, one, two, column, up] + ([] if given is None else [given])
    return pl.pallas_call(
        functools.partial(expand_body, chip_cap, device_cap, number),
        in_specs=[pl.BlockSpec(memory_space=pltpu.SMEM)]
        + [pl.BlockSpec(memory_space=pltpu.VMEM) for _ in operands[1:]],
        out_specs=[pl.BlockSpec(memory_space=pltpu.VMEM) for _ in range(number)],
        out_shape=[jax.ShapeDtypeStruct((rows, up.shape[1]), up.dtype)] * number,
        compiler_params=PARAMS,
        cost_estimate=pl.CostEstimate(
            flops=2 * number * device_cap * up.shape[0] * up.shape[1],
            bytes_accessed=2 * up.size + 8 * one.size,
            transcendentals=0,
        ),
    )(*operands)


def make_local(mesh_shape):
    owners, groups = mesh_shape["own"], mesh_shape["grp"]
    planes = owners // LANES

    def flipped(x, axis, flip):
        size = mesh_shape[axis]
        return lax.ppermute(x, axis, [(i, i ^ flip) for i in range(size)])

    def swap(x, flip):
        return flipped(x, "own", flip)

    def send(x, flip):
        return flipped(x, "own", flip * LANES)

    def local(
        tokens,
        adapter_index_rows,
        adapter_pool_position,
        base_value_matrix,
        lowrank_down_weight,
        lowrank_up_weight,
    ):
        rows, width = tokens.shape
        held, rank, _ = lowrank_down_weight.shape
        out_width = base_value_matrix.shape[1]
        total = adapter_pool_position.shape[0]
        most = max(2, 2 * rows // total)
        cap = min(rows, LANES * held * most)
        first = cap // 4
        levels = [(2 * cap * k // 16 - 2 * first, cap * 3 // 4 - first) for k in (10, 11, 12)]
        levels = levels + [(2 * cap - 2 * first, cap - first)]
        flips = sorted(range(1, planes), key=lambda k: -k)
        half = width // 2

        me = lax.axis_index("own")
        plane, lane, core = me // LANES, me % LANES, me % 2
        place = jnp.stack([core, plane, jnp.zeros_like(core)]).astype(jnp.int32)

        chosen = adapter_index_rows[:, 0]
        table = jnp.arange(total, dtype=jnp.int32)
        slot = jnp.sum(
            jnp.where(chosen[:, None] == table[None, :], adapter_pool_position[None, :], 0), axis=1
        )
        goes_to = slot // (held * LANES)
        places = jnp.arange(rows, dtype=jnp.int32)
        earlier = (goes_to[:, None] == goes_to[None, :]) & (places[None, :] < places[:, None])
        within = jnp.sum(earlier.astype(jnp.int32), axis=1)
        mine = (slot * rows + within)[None, :]

        down = lowrank_down_weight.reshape(held * rank, width)
        up = lowrank_up_weight.reshape(held * rank, out_width)
        half_of = lambda x, c: lax.dynamic_slice_in_dim(x, c * half, half, axis=1)
        mate_tokens, mate_down, mate_up = swap(tokens, 1), swap(down, 1), swap(up, 1)
        kept_down = half_of(down, core)
        far_down = swap(kept_down, 2)

        infos, step = mine, 1
        while step < planes:
            infos = jnp.concatenate([infos, send(infos, step)], axis=0)
            step *= 2
        first_rows = pack(place, goes_to[None, :], within[None, :], [tokens], 0, first, flips)
        infos, first_rows, mate_tokens, mate_down, mate_up = lax.optimization_barrier(
            (infos, first_rows, mate_tokens, mate_down, mate_up)
        )
        first_arrived = [send(x, k) for x, k in zip(first_rows, flips)]
        mate_infos = swap(infos, 1)
        span = rows * held * LANES
        starts = [(p * span, (p + 1) * span) for p in range(planes)]
        level = level_of(place, infos, mate_infos, starts, levels, first)
        level = jnp.maximum(level, swap(level, 2))
        step = 1
        while step < groups:
            level = jnp.maximum(level, flipped(level, "grp", step))
            step *= 2
        level = level[0, 0]
        infos = jnp.stack([infos, mate_infos], axis=1)
        info = infos[0]
        goes_to, within = info // span, info % rows
        near_down = lax.optimization_barrier(half_of(mate_down, core))

        def column_of(packed):
            slot = packed // rows
            return ((slot // held) % LANES ^ lane) * held + slot % held

        def at_level(chip_cap, device_cap):
            home_core = jnp.stack([core, 1 - core])[:, None]

            def spot_of(packed, size):
                ahead = packed % rows - first
                spot = jnp.where(home_core[: packed.shape[0]] == 0, ahead, size - 1 - ahead)
                return jnp.where(ahead >= 0, spot, -1)

            def named_by(spots, spot, column):
                hot = spots[:, None] == spot.reshape(1, -1)
                return jnp.sum(jnp.where(hot, column.reshape(1, -1) + 1, 0), 1, keepdims=True) - 1

            def branch(
                tokens,
                mate_tokens,
                info,
                goes_to,
                within,
                infos,
                first_arrived,
                kept_down,
                near_down,
                far_down,
                up,
                mate_up,
                matrix,
            ):
                packed = pack(
                    jnp.stack([core, plane, jnp.full_like(core, chip_cap)]),
                    goes_to,
                    within,
                    [tokens, mate_tokens],
                    first,
                    chip_cap,
                    flips,
                )
                packed, first_arrived, up, tokens, infos = lax.optimization_barrier(
                    (packed, first_arrived, up, tokens, infos)
                )
                arrived = [send(x, k) for x, k in zip(packed, flips)]
                last_down = swap(near_down, 2)
                down = [kept_down, near_down, far_down, last_down]
                up = jnp.concatenate([up, mate_up], axis=0)
                up = jnp.concatenate([up, swap(up, 2)], axis=0)
                first_mine = jnp.concatenate(first_arrived, axis=0)
                first_mate = swap(first_mine, 1)

                base = jnp.dot(tokens, matrix, preferred_element_type=jnp.float32)
                columns, first_columns = [], [[], []]
                for k in flips:
                    got = infos[k]
                    here = got // span == plane
                    columns.append(
                        named_by(
                            jnp.arange(chip_cap, dtype=jnp.int32),
                            jnp.where(here, spot_of(got, chip_cap), -1),
                            column_of(got),
                        )
                    )
                    for row in range(2):
                        first_columns[row].append(
                            named_by(
                                jnp.arange(first, dtype=jnp.int32),
                                jnp.where(here, got % rows, -1)[row],
                                column_of(got)[row],
                            )
                        )
                columns = jnp.concatenate(columns, axis=0)
                stays = jnp.where(goes_to == plane, column_of(info), -1)[:, :, None]
                own_columns = jnp.concatenate([stays[0]] + first_columns[0], axis=0)
                mate_columns = jnp.concatenate([stays[1]] + first_columns[1], axis=0)
                held_rows = own_columns.shape[0]
                rows_here = [tokens, first_mine, mate_tokens, first_mate]
                columns_here = jnp.concatenate([own_columns, mate_columns], axis=0)
                sums = shrink(place, rows_here, down[:3], columns_here, rank)
                sums = sums + shrink(place, rows_here, down[3:], columns_here, rank, 3 * held)
                (delta,) = expand(
                    place,
                    sums[:held_rows],
                    swap(sums[held_rows:], 1),
                    own_columns,
                    up,
                    1,
                    held_rows,
                )
                out = base + delta[:rows].astype(jnp.float32)
                arrived, columns, out, first_delta = lax.optimization_barrier(
                    (arrived, columns, out, delta[rows:])
                )

                sums = shrink(place, arrived, down, columns, rank)
                deltas = expand(
                    place,
                    sums,
                    swap(sums, 1),
                    columns,
                    up,
                    len(flips),
                    device_cap,
                    first_delta,
                )
                home = [send(x, k) for x, k in zip(deltas, flips)]
                spots = jnp.arange(first + device_cap, dtype=jnp.int32)
                for k, back in zip(flips, home):
                    ahead = info[:1] % rows
                    rest = spot_of(info[:1], device_cap) + first
                    spot = jnp.where(ahead < first, ahead, rest)
                    spot = jnp.where(goes_to[:1] == plane ^ k, spot, -1)
                    hot = (spots[None, :] == spot.reshape(-1, 1)).astype(jnp.bfloat16)
                    out = out + jnp.dot(hot, back, preferred_element_type=jnp.float32)
                return out.astype(jnp.bfloat16)

            return branch

        return lax.switch(
            level,
            [at_level(*sizes) for sizes in levels],
            tokens,
            mate_tokens,
            info,
            goes_to,
            within,
            infos,
            first_arrived,
            kept_down,
            near_down,
            far_down,
            up,
            mate_up,
            base_value_matrix,
        )

    return local


def solution(mesh):
    in_specs = (
        P(("grp", "own"), None),
        P(("grp", "own"), None),
        P("grp"),
        P(),
        P(("grp", "own"), None, None),
        P(("grp", "own"), None, None),
    )
    out_specs = P(("grp", "own"), None)
    return jax.shard_map(
        make_local(dict(mesh.shape)),
        mesh=mesh,
        in_specs=in_specs,
        out_specs=out_specs,
        check_vma=False,
    )
```

time: 111 us -> 99.9 us (0.900)
  waiting for transfers between devices: 51.7 us -> 35.6 us
  matrix products: 7.77 us -> 1.93 us
  starting transfers between devices: 21.2 us -> 24.7 us
  Pallas kernels: 17.4 us -> 20.4 us
  local copies, waits for them, and re-layouts: 6.52 us -> 8.36 us
  other arithmetic: 5.46 us -> 6.73 us
    ppermute x21 -> x23, waiting for transfers between devices: 51.7 us -> 35.6 us  [flipped(): return lax.ppermute(x, axis, [(i, i ^ flip) for i in range(size)])]
    dot_general x1, matrix products: 6.15 us -> 1.26 us  [branch(): base = jnp.dot(tokens, matrix, preferred_element_type=jnp.float32)]
    ppermute x21 -> x23, starting transfers between devices: 21.2 us -> 24.7 us  [flipped(): return lax.ppermute(x, axis, [(i, i ^ flip) for i in range(size)])]
    pallas_call x6 -> x8, Pallas kernels: 17.4 us -> 20.4 us  [the longest x3 12.2 us: shrink(): pl.pallas_call(functools.partial(shrink_body, len(xs), len(ws), rank, sta...]
    another operation x1 -> x5, other arithmetic: 0.07 us -> 2.15 us  [the longest x2 1.39 us: local(): infos = jnp.stack([infos, mate_infos], axis=1)]
    add x2 -> x1, other arithmetic: 1.71 us -> 0.02 us  [branch(): sums + shrink(place, rows_here, down[3:], columns_here, rank, 3 * held)]
    unnamed x20 -> x30, local copies, waits for them, and re-layouts: 0.69 us -> 2.25 us
    concatenate x0 -> x5, local copies, waits for them, and re-layouts: none -> 1.35 us  [the longest x1 0.97 us: branch(): first_mine = jnp.concatenate(first_arrived, axis=0)]
  transfers between devices with their start and end apart: 21 -> 23, of which waited for: 12 -> 10; matrix products, arithmetic and copies ran while one was open for 13% -> 15% of each run, Pallas kernels for 7% -> 12%
where the time goes in v3:
time: 99.9 us; the launch traced here: 99 us
  waiting for transfers between devices  35.6 us (36%)
  starting transfers between devices  24.7 us (25%)
  Pallas kernels  20.4 us (20%)
  local copies, waits for them, and re-layouts  8.36 us (8%)
  other arithmetic  6.73 us (7%)
  matrix products  1.93 us (2%)
  loops' own time  1.18 us (1%)
    ppermute x23, waiting for transfers between devices, flipped(): return lax.ppermute(x, axis, [(i, i ^ flip) for i in range(size)])  35.6 us
    ppermute x23, starting transfers between devices, flipped(): return lax.ppermute(x, axis, [(i, i ^ flip) for i in range(size)])  24.7 us
    pallas_call x3, Pallas kernels, shrink(): pl.pallas_call(functools.partial(shrink_body, len(xs), len(ws), rank, sta...  12.2 us
    pallas_call x2, Pallas kernels, pack(): pl.pallas_call(functools.partial(pack_body, flips, number, start), grid_s...  4.9 us
    dynamic_slice x2, local copies, waits for them, and re-layouts, local(): half_of = lambda x, c: lax.dynamic_slice_in_dim(x, c * half, half, axis=1)  4.63 us
    unnamed x30, local copies, waits for them, and re-layouts  2.25 us
  transfers between devices with their start and end apart: 23, of which 10 were waited for; matrix products, arithmetic and copies ran while one was open for 15% of the time, Pallas kernels for 12%

profile of v3, /device:TPU:0, one launch (start us, length us, event | category | flops | bytes accessed | tf_op | source)
XLA Modules:
  0.0 99.0 jit_solution(16903013891900493909)
XLA Ops:
  1.6 3.1 %collective-permute-start.44 = (s32[1,128]{1,0:T(1,128)S(1)}, s32[1,128]{1,0:T(1,128)S(1)}, u32[]{:S(2)}, u32[]{:S(2)}) collective-permute-start(s32[1,128]{1,0:T(1,128)S(1)} %get-tuple-element.1089), channel_id=1, source_target_pairs={{0,4},{1,5},{2,6},{3,7},{4,0},{5,1},{6,2},{7,3},{8,12},{9,13},{10,... | collective-permute-start | bytes 1544 | tf_op jit(solution)/shard_map/ppermute | solution.py:226
  4.7 2.3 %constant_dynamic-slice_fusion.1 = bf16[128,4096]{1,0:T(8,128)(2,1)} fusion(bf16[128,8192]{1,0:T(8,128)(2,1)} %bitcast.779, s32[]{:T(128)S(6)} %select_n.1652), kind=kLoop, calls=%fused_computation.1074 | loop fusion | bytes 2097156 | tf_op jit(solution)/shard_map/dynamic_slice | solution.py:271
  7.0 1.5 %collective-permute-start.55 = (bf16[128,4096]{1,0:T(8,128)(2,1)}, bf16[128,4096]{1,0:T(8,128)(2,1)}, u32[]{:S(2)}, u32[]{:S(2)}) collective-permute-start(bf16[128,4096]{1,0:T(8,128)(2,1)} %constant_dynamic-slice_fusion.1), channel_id=1, source_target_pairs={{0,2},{1,3},{2,0},{3,1},{4,6},{5,7},{6,4},{7,5},{8,10},{9,11},{10,... | collective-permute-start | bytes 3145736 | tf_op jit(solution)/shard_map/ppermute | solution.py:226
  9.2 2.7 %collective-permute-start.45 = (s32[2,128]{1,0:T(2,128)S(1)}, s32[2,128]{1,0:T(2,128)S(1)}, u32[]{:S(2)}, u32[]{:S(2)}) collective-permute-start(s32[2,128]{1,0:T(2,128)S(1)} %pad_add_fusion.14), channel_id=1, source_target_pairs={{0,8},{1,9},{2,10},{3,11},{4,12},{5,13},{6,14},{7,15},{8,0},{9,1},... | collective-permute-start | bytes 3080 | tf_op jit(solution)/shard_map/ppermute | solution.py:226
  11.9 1.7 %shard_map.72 = (bf16[16,8192]{1,0:T(8,128)(2,1)S(1)}, bf16[16,8192]{1,0:T(8,128)(2,1)S(1)}, bf16[16,8192]{1,0:T(8,128)(2,1)S(1)}) custom-call(s32[3]{0:T(128)S(1)} %pad_add_fusion.15.place_ref, s32[1,128]{1,0:T(1,128)S(1)} %get-tuple-element.1088.goes_ref, s32[1,128]{1,0:T(1,128)S(1)} %bitcast.764, bf16[128,8192]{1,0:T(8,128)(2,1)S(1)} %copy-done), custom_call_target="tpu_custom_call" | custom-call | flops 100663296 | bytes 2883584 | tf_op jit(solution)/shard_map/pallas_call | solution.py:90
  13.9 2.5 %collective-permute-start.52 = (bf16[16,8192]{1,0:T(8,128)(2,1)S(1)}, bf16[16,8192]{1,0:T(8,128)(2,1)S(1)}, u32[]{:S(2)}, u32[]{:S(2)}) collective-permute-start(bf16[16,8192]{1,0:T(8,128)(2,1)S(1)} %get-tuple-element.596), channel_id=1, source_target_pairs={{0,12},{1,13},{2,14},{3,15},{4,8},{5,9},{6,10},{7,11},{8,4},{9,5},... | collective-permute-start | bytes 786440 | tf_op jit(solution)/shard_map/ppermute | solution.py:226
  16.6 1.7 %collective-permute-start.54 = (bf16[16,8192]{1,0:T(8,128)(2,1)S(1)}, bf16[16,8192]{1,0:T(8,128)(2,1)}, u32[]{:S(2)}, u32[]{:S(2)}) collective-permute-start(bf16[16,8192]{1,0:T(8,128)(2,1)S(1)} %get-tuple-element.598), channel_id=1, source_target_pairs={{0,4},{1,5},{2,6},{3,7},{4,0},{5,1},{6,2},{7,3},{8,12},{9,13},{10,... | collective-permute-start | bytes 786440 | tf_op jit(solution)/shard_map/ppermute | solution.py:226
  18.3 2.3 %constant_dynamic-slice_fusion = bf16[128,4096]{1,0:T(8,128)(2,1)} fusion(bf16[128,8192]{1,0:T(8,128)(2,1)} %collective-permute-done.47, s32[]{:T(128)S(6)} %select_n.1652), kind=kLoop, calls=%fused_computation.1073 | loop fusion | bytes 2097156 | tf_op jit(solution)/shard_map/dynamic_slice | solution.py:271
  21.2 1.5 %shard_map.73 = s32[1,128]{1,0:T(1,128)} custom-call(s32[3]{0:T(128)S(1)} %pad_add_fusion.15.place_ref, s32[4,128]{1,0:T(4,128)} %copy-done.19, s32[4,128]{1,0:T(4,128)} %copy-done.20), custom_call_target="tpu_custom_call" | custom-call | tf_op jit(solution)/shard_map/pallas_call | solution.py:43
  23.9 9.0 %collective-permute-done.50 = s32[1,128]{1,0:T(1,128)S(1)} collective-permute-done((s32[1,128]{1,0:T(1,128)}, s32[1,128]{1,0:T(1,128)S(1)}, u32[]{:S(2)}, u32[]{:S(2)}) %collective-permute-start.50) | collective-permute-done | bytes 544 | tf_op jit(solution)/shard_map/ppermute | solution.py:226
  33.6 1.5 %collective-permute-start.51 = (s32[1,128]{1,0:T(1,128)S(1)}, s32[1,128]{1,0:T(1,128)S(1)}, u32[]{:S(2)}, u32[]{:S(2)}) collective-permute-start(s32[1,128]{1,0:T(1,128)S(1)} %max.6), channel_id=1, source_target_pairs={{0,16},{16,0},{1,17},{17,1},{2,18},{18,2},{3,19},{19,3},{4,20},{20... | collective-permute-start | bytes 1544 | tf_op jit(solution)/shard_map/ppermute | solution.py:226
  35.8 1.4 %collective-permute-done.51 = s32[1,128]{1,0:T(1,128)S(1)} collective-permute-done((s32[1,128]{1,0:T(1,128)S(1)}, s32[1,128]{1,0:T(1,128)S(1)}, u32[]{:S(2)}, u32[]{:S(2)}) %collective-permute-start.51) | collective-permute-done | bytes 544 | tf_op jit(solution)/shard_map/ppermute | solution.py:226
  37.2 3.1 %collective-permute-done.53 = bf16[16,8192]{1,0:T(8,128)(2,1)S(1)} collective-permute-done((bf16[16,8192]{1,0:T(8,128)(2,1)S(1)}, bf16[16,8192]{1,0:T(8,128)(2,1)S(1)}, u32[]{:S(2)}, u32[]{:S(2)}) %collective-permute-start.53) | collective-permute-done | bytes 262176 | tf_op jit(solution)/shard_map/ppermute | solution.py:226
  40.3 58.1 %conditional.3 = (bf16[128,512]{1,0:T(8,128)(2,1)S(1)}) conditional(s32[]{:T(128)} %bitcast.151, (s32[]{:T(128)}, s32[]{:T(128)}, s32[2,128]{1,0:T(2,128)S(1)}, pred[2,128]{1,0:T(4,128)(4,1)S(1)}, pred[2,128]{1,0:T(4,128)(4,1)S(1)}, /*index=5*/s32[2,128]{1,0:T(2,128)S(1)}, bf16[128,8192]{1,0:T(8,128)(2,1)S(1)}, ...), branch_computations={%region_2.12_spmd, %region_12.22_spmd, %region_22.32_spmd, %region... | conditional | flops 4556362752 | bytes 99596880
  40.5 3.2 %branch_0_fun.6 = (bf16[48,4096]{1,0:T(8,128)(2,1)}, bf16[48,4096]{1,0:T(8,128)(2,1)}, bf16[48,4096]{1,0:T(8,128)(2,1)}) custom-call(s32[3]{0:T(128)S(1)} %pad_add_fusion.2.place_ref, s32[2,128]{1,0:T(2,128)S(1)} %get-tuple-element.919.goes_ref, s32[2,128]{1,0:T(2,128)S(1)} %get-tuple-element.946.within_ref, ...), custom_call_target="tpu_custom_call" | custom-call | flops 301989888 | bytes 3276800 | tf_op jit(solution)/shard_map/cond/branch_0_fun/pallas_call | solution.py:90
  43.7 2.7 %collective-permute-start = (bf16[48,4096]{1,0:T(8,128)(2,1)}, bf16[48,4096]{1,0:T(8,128)(2,1)}, u32[]{:S(2)}, u32[]{:S(2)}) collective-permute-start(bf16[48,4096]{1,0:T(8,128)(2,1)} %get-tuple-element.425), channel_id=1, source_target_pairs={{0,12},{1,13},{2,14},{3,15},{4,8},{5,9},{6,10},{7,11},{8,4},{9,5},... | collective-permute-start | bytes 1179656 | tf_op jit(solution)/shard_map/cond/branch_0_fun/ppermute | solution.py:226
  46.4 1.7 %collective-permute-start.2 = (bf16[48,4096]{1,0:T(8,128)(2,1)}, bf16[48,4096]{1,0:T(8,128)(2,1)}, u32[]{:S(2)}, u32[]{:S(2)}) collective-permute-start(bf16[48,4096]{1,0:T(8,128)(2,1)} %get-tuple-element.427), channel_id=1, source_target_pairs={{0,4},{1,5},{2,6},{3,7},{4,0},{5,1},{6,2},{7,3},{8,12},{9,13},{10,... | collective-permute-start | bytes 1179656 | tf_op jit(solution)/shard_map/cond/branch_0_fun/ppermute | solution.py:226
  48.2 1.0 constant_dynamic-update-slice_fusion.refs_1_
  52.2 0.9 constant_dynamic-update-slice_fusion.4
  53.1 0.9 pad_maximum_fusion
  54.0 1.6 %collective-permute-start.6 = (bf16[256,512]{1,0:T(8,128)(2,1)S(1)}, bf16[256,512]{1,0:T(8,128)(2,1)S(1)}, u32[]{:S(2)}, u32[]{:S(2)}) collective-permute-start(bf16[256,512]{1,0:T(8,128)(2,1)S(1)} %pad_maximum_fusion), channel_id=1, source_target_pairs={{0,2},{1,3},{2,0},{3,1},{4,6},{5,7},{6,4},{7,5},{8,10},{9,11},{10,... | collective-permute-start | bytes 786440 | tf_op jit(solution)/shard_map/cond/branch_0_fun/ppermute | solution.py:226
  55.6 5.0 %branch_0_fun.7 = f32[352,64]{1,0:T(8,128)S(1)} custom-call(s32[3]{0:T(128)S(1)} %get-tuple-element.434.place_ref, bf16[128,8192]{1,0:T(8,128)(2,1)} %copy-done.1, bf16[48,8192]{1,0:T(8,128)(2,1)S(1)} %constant_dynamic-update-slice_fusion.refs_1_, bf16[128,8192]{1,0:T(8,128)(2,1)} %get-tuple-element.416.refs_1_.refs_2_, ...), custom_call_target="tpu_custom_call" | custom-call | flops 1107296256 | bytes 6029312 | tf_op jit(solution)/shard_map/cond/branch_0_fun/pallas_call | solution.py:147
  60.6 14.9 %collective-permute-done.4.refs_4_.refs_6_ = bf16[128,4096]{1,0:T(8,128)(2,1)S(1)} collective-permute-done((bf16[128,4096]{1,0:T(8,128)(2,1)}, bf16[128,4096]{1,0:T(8,128)(2,1)S(1)}, u32[]{:S(2)}, u32[]{:S(2)}) %collective-permute-start.4) | collective-permute-done | bytes 1048608 | tf_op jit(solution)/shard_map/cond/branch_0_fun/ppermute | solution.py:226
  75.5 3.0 %branch_0_fun.8 = f32[352,64]{1,0:T(8,128)S(1)} custom-call(s32[3]{0:T(128)S(1)} %get-tuple-element.434.place_ref, bf16[128,8192]{1,0:T(8,128)(2,1)S(1)} %copy-done.2, bf16[48,8192]{1,0:T(8,128)(2,1)S(1)} %constant_dynamic-update-slice_fusion.refs_1_, bf16[128,8192]{1,0:T(8,128)(2,1)} %get-tuple-element.416.refs_1_.refs_2_, ...), custom_call_target="tpu_custom_call" | custom-call | flops 369098752 | bytes 3932160 | tf_op jit(solution)/shard_map/cond/branch_0_fun/pallas_call | solution.py:147
  78.7 2.0 %collective-permute-done.6 = bf16[256,512]{1,0:T(8,128)(2,1)S(1)} collective-permute-done((bf16[256,512]{1,0:T(8,128)(2,1)S(1)}, bf16[256,512]{1,0:T(8,128)(2,1)S(1)}, u32[]{:S(2)}, u32[]{:S(2)}) %collective-permute-start.6) | collective-permute-done | bytes 262176 | tf_op jit(solution)/shard_map/cond/branch_0_fun/ppermute | solution.py:226
  80.7 0.9 branch_0_fun.9
  81.7 1.3 %convert_add_fusion = f32[128,512]{1,0:T(8,128)S(1)} fusion(bf16[176,512]{1,0:T(8,128)(2,1)S(1)} %branch_0_fun.9, bf16[128,8192]{1,0:T(8,128)(2,1)S(1)} %copy-done.2, bf16[8192,512]{1,0:T(8,128)(2,1)S(1)} %bitcast.766), kind=kOutput, calls=%fused_computation.2 | convolution fusion | flops 1073872896 | bytes 10878976 | tf_op jit(solution)/shard_map/cond/branch_0_fun/dot_general | solution.py:351
  83.1 4.1 %branch_0_fun.10.one_ref = f32[144,64]{1,0:T(8,128)S(1)} custom-call(s32[3]{0:T(128)S(1)} %get-tuple-element.434.place_ref, bf16[48,4096]{1,0:T(8,128)(2,1)} %collective-permute-done.refs_0_, bf16[48,4096]{1,0:T(8,128)(2,1)} %collective-permute-done.1.refs_1_, bf16[48,4096]{1,0:T(8,128)(2,1)} %collective-permute-done.2.refs_2_, ...), custom_call_target="tpu_custom_call" | custom-call | flops 603979776 | bytes 5373952 | tf_op jit(solution)/shard_map/cond/branch_0_fun/pallas_call | solution.py:147
  87.4 1.2 %collective-permute-done.7.two_ref = f32[144,64]{1,0:T(8,128)S(1)} collective-permute-done((f32[144,64]{1,0:T(8,128)S(1)}, f32[144,64]{1,0:T(8,128)S(1)}, u32[]{:S(2)}, u32[]{:S(2)}) %collective-permute-start.7) | collective-permute-done | bytes 36896 | tf_op jit(solution)/shard_map/cond/branch_0_fun/ppermute | solution.py:226
  89.5 1.3 %collective-permute-start.9 = (bf16[48,512]{1,0:T(8,128)(2,1)S(1)}, bf16[48,512]{1,0:T(8,128)(2,1)S(1)}, u32[]{:S(2)}, u32[]{:S(2)}) collective-permute-start(bf16[48,512]{1,0:T(8,128)(2,1)S(1)} %get-tuple-element.450), channel_id=1, source_target_pairs={{0,8},{1,9},{2,10},{3,11},{4,12},{5,13},{6,14},{7,15},{8,0},{9,1},... | collective-permute-start | bytes 147464 | tf_op jit(solution)/shard_map/cond/branch_0_fun/ppermute | solution.py:226
  90.8 1.6 %collective-permute-start.8 = (bf16[48,512]{1,0:T(8,128)(2,1)S(1)}, bf16[48,512]{1,0:T(8,128)(2,1)S(1)}, u32[]{:S(2)}, u32[]{:S(2)}) collective-permute-start(bf16[48,512]{1,0:T(8,128)(2,1)S(1)} %get-tuple-element.449), channel_id=1, source_target_pairs={{0,12},{1,13},{2,14},{3,15},{4,8},{5,9},{6,10},{7,11},{8,4},{9,5},... | collective-permute-start | bytes 147464 | tf_op jit(solution)/shard_map/cond/branch_0_fun/ppermute | solution.py:226
  93.1 2.9 %collective-permute-done.9 = bf16[48,512]{1,0:T(8,128)(2,1)S(1)} collective-permute-done((bf16[48,512]{1,0:T(8,128)(2,1)S(1)}, bf16[48,512]{1,0:T(8,128)(2,1)S(1)}, u32[]{:S(2)}, u32[]{:S(2)}) %collective-permute-start.9) | collective-permute-done | bytes 49184 | tf_op jit(solution)/shard_map/cond/branch_0_fun/ppermute | solution.py:226
  (115 shorter events, 13.3 us)
Async XLA Ops:
  0.0 11.9 %copy-start = (bf16[128,8192]{1,0:T(8,128)(2,1)S(1)}, bf16[128,8192]{1,0:T(8,128)(2,1)}, u32[]{:S(2)}) copy-start(bf16[128,8192]{1,0:T(8,128)(2,1)} %refs_0_.1) | copy-start | bytes 6291460
  0.0 13.8 %collective-permute-start.46 = (bf16[128,8192]{1,0:T(8,128)(2,1)}, bf16[128,8192]{1,0:T(8,128)(2,1)}, u32[]{:S(2)}, u32[]{:S(2)}) collective-permute-start(bf16[128,8192]{1,0:T(8,128)(2,1)} %refs_0_.1), channel_id=1, source_target_pairs={{0,1},{1,0},{2,3},{3,2},{4,5},{5,4},{6,7},{7,6},{8,9},{9,8},{10,11... | collective-permute-start | bytes 6291464 | tf_op jit(solution)/shard_map/ppermute | solution.py:226
  0.5 13.4 %collective-permute-start.47 = (bf16[128,8192]{1,0:T(8,128)(2,1)}, bf16[128,8192]{1,0:T(8,128)(2,1)}, u32[]{:S(2)}, u32[]{:S(2)}) collective-permute-start(bf16[128,8192]{1,0:T(8,128)(2,1)} %bitcast.778), channel_id=1, source_target_pairs={{0,1},{1,0},{2,3},{3,2},{4,5},{5,4},{6,7},{7,6},{8,9},{9,8},{10,11... | collective-permute-start | bytes 6291464 | tf_op jit(solution)/shard_map/ppermute | solution.py:226
  1.6 7.6 %collective-permute-start.44 = (s32[1,128]{1,0:T(1,128)S(1)}, s32[1,128]{1,0:T(1,128)S(1)}, u32[]{:S(2)}, u32[]{:S(2)}) collective-permute-start(s32[1,128]{1,0:T(1,128)S(1)} %get-tuple-element.1089), channel_id=1, source_target_pairs={{0,4},{1,5},{2,6},{3,7},{4,0},{5,1},{6,2},{7,3},{8,12},{9,13},{10,... | collective-permute-start | bytes 1544 | tf_op jit(solution)/shard_map/ppermute | solution.py:226
  4.7 9.1 %collective-permute-start.48 = (bf16[128,512]{1,0:T(8,128)(2,1)}, bf16[128,512]{1,0:T(8,128)(2,1)}, u32[]{:S(2)}, u32[]{:S(2)}) collective-permute-start(bf16[128,512]{1,0:T(8,128)(2,1)} %bitcast.773), channel_id=1, source_target_pairs={{0,1},{1,0},{2,3},{3,2},{4,5},{5,4},{6,7},{7,6},{8,9},{9,8},{10,11... | collective-permute-start | bytes 393224 | tf_op jit(solution)/shard_map/ppermute | solution.py:226
  7.0 30.2 %collective-permute-start.55 = (bf16[128,4096]{1,0:T(8,128)(2,1)}, bf16[128,4096]{1,0:T(8,128)(2,1)}, u32[]{:S(2)}, u32[]{:S(2)}) collective-permute-start(bf16[128,4096]{1,0:T(8,128)(2,1)} %constant_dynamic-slice_fusion.1), channel_id=1, source_target_pairs={{0,2},{1,3},{2,0},{3,1},{4,6},{5,7},{6,4},{7,5},{8,10},{9,11},{10,... | collective-permute-start | bytes 3145736 | tf_op jit(solution)/shard_map/ppermute | solution.py:226
  9.2 4.5 %collective-permute-start.45 = (s32[2,128]{1,0:T(2,128)S(1)}, s32[2,128]{1,0:T(2,128)S(1)}, u32[]{:S(2)}, u32[]{:S(2)}) collective-permute-start(s32[2,128]{1,0:T(2,128)S(1)} %pad_add_fusion.14), channel_id=1, source_target_pairs={{0,8},{1,9},{2,10},{3,11},{4,12},{5,13},{6,14},{7,15},{8,0},{9,1},... | collective-permute-start | bytes 3080 | tf_op jit(solution)/shard_map/ppermute | solution.py:226
  11.9 28.4 %copy-start.9 = (bf16[2,64,512]{2,1,0:T(8,128)(2,1)S(1)}, bf16[2,64,512]{2,1,0:T(8,128)(2,1)}, u32[]{:S(2)}) copy-start(bf16[2,64,512]{2,1,0:T(8,128)(2,1)} %param.15) | copy-start | bytes 393220
  13.8 6.9 %copy-start.19 = (s32[4,128]{1,0:T(4,128)}, s32[4,128]{1,0:T(4,128)S(1)}, u32[]{:S(2)}) copy-start(s32[4,128]{1,0:T(4,128)S(1)} %pad_add_fusion.13.mine_ref) | copy-start | bytes 6148
  13.8 6.8 %collective-permute-start.49 = (s32[4,128]{1,0:T(4,128)S(1)}, s32[4,128]{1,0:T(4,128)S(1)}, u32[]{:S(2)}, u32[]{:S(2)}) collective-permute-start(s32[4,128]{1,0:T(4,128)S(1)} %pad_add_fusion.13.mine_ref), channel_id=1, source_target_pairs={{0,1},{1,0},{2,3},{3,2},{4,5},{5,4},{6,7},{7,6},{8,9},{9,8},{10,11... | collective-permute-start | bytes 6152 | tf_op jit(solution)/shard_map/ppermute | solution.py:226
  13.9 23.3 %collective-permute-start.52 = (bf16[16,8192]{1,0:T(8,128)(2,1)S(1)}, bf16[16,8192]{1,0:T(8,128)(2,1)S(1)}, u32[]{:S(2)}, u32[]{:S(2)}) collective-permute-start(bf16[16,8192]{1,0:T(8,128)(2,1)S(1)} %get-tuple-element.596), channel_id=1, source_target_pairs={{0,12},{1,13},{2,14},{3,15},{4,8},{5,9},{6,10},{7,11},{8,4},{9,5},... | collective-permute-start | bytes 786440 | tf_op jit(solution)/shard_map/ppermute | solution.py:226
  16.4 23.9 %collective-permute-start.53 = (bf16[16,8192]{1,0:T(8,128)(2,1)S(1)}, bf16[16,8192]{1,0:T(8,128)(2,1)S(1)}, u32[]{:S(2)}, u32[]{:S(2)}) collective-permute-start(bf16[16,8192]{1,0:T(8,128)(2,1)S(1)} %get-tuple-element.597), channel_id=1, source_target_pairs={{0,8},{1,9},{2,10},{3,11},{4,12},{5,13},{6,14},{7,15},{8,0},{9,1},... | collective-permute-start | bytes 786440 | tf_op jit(solution)/shard_map/ppermute | solution.py:226
  16.6 23.7 %collective-permute-start.54 = (bf16[16,8192]{1,0:T(8,128)(2,1)S(1)}, bf16[16,8192]{1,0:T(8,128)(2,1)}, u32[]{:S(2)}, u32[]{:S(2)}) collective-permute-start(bf16[16,8192]{1,0:T(8,128)(2,1)S(1)} %get-tuple-element.598), channel_id=1, source_target_pairs={{0,4},{1,5},{2,6},{3,7},{4,0},{5,1},{6,2},{7,3},{8,12},{9,13},{10,... | collective-permute-start | bytes 786440 | tf_op jit(solution)/shard_map/ppermute | solution.py:226
  22.7 10.2 %collective-permute-start.50 = (s32[1,128]{1,0:T(1,128)}, s32[1,128]{1,0:T(1,128)S(1)}, u32[]{:S(2)}, u32[]{:S(2)}) collective-permute-start(s32[1,128]{1,0:T(1,128)} %shard_map.73), channel_id=1, source_target_pairs={{0,2},{1,3},{2,0},{3,1},{4,6},{5,7},{6,4},{7,5},{8,10},{9,11},{10,... | collective-permute-start | bytes 1544 | tf_op jit(solution)/shard_map/ppermute | solution.py:226
  33.6 3.5 %collective-permute-start.51 = (s32[1,128]{1,0:T(1,128)S(1)}, s32[1,128]{1,0:T(1,128)S(1)}, u32[]{:S(2)}, u32[]{:S(2)}) collective-permute-start(s32[1,128]{1,0:T(1,128)S(1)} %max.6), channel_id=1, source_target_pairs={{0,16},{16,0},{1,17},{17,1},{2,18},{18,2},{3,19},{19,3},{4,20},{20... | collective-permute-start | bytes 1544 | tf_op jit(solution)/shard_map/ppermute | solution.py:226
  40.3 3.4 %copy-start.1 = (bf16[128,8192]{1,0:T(8,128)(2,1)}, bf16[128,8192]{1,0:T(8,128)(2,1)S(1)}, u32[]{:S(2)}) copy-start(bf16[128,8192]{1,0:T(8,128)(2,1)S(1)} %get-tuple-element.432.refs_0_) | copy-start | bytes 6291460
  40.5 9.3 %copy-start.25 = (s32[2]{0:T(128)S(1)}, s32[2]{0:T(128)}, u32[]{:S(2)}) copy-start(s32[2]{0:T(128)} %get-tuple-element.429) | copy-start | bytes 28
  43.7 39.3 %collective-permute-start = (bf16[48,4096]{1,0:T(8,128)(2,1)}, bf16[48,4096]{1,0:T(8,128)(2,1)}, u32[]{:S(2)}, u32[]{:S(2)}) collective-permute-start(bf16[48,4096]{1,0:T(8,128)(2,1)} %get-tuple-element.425), channel_id=1, source_target_pairs={{0,12},{1,13},{2,14},{3,15},{4,8},{5,9},{6,10},{7,11},{8,4},{9,5},... | collective-permute-start | bytes 1179656 | tf_op jit(solution)/shard_map/cond/branch_0_fun/ppermute | solution.py:226
  46.4 36.5 %collective-permute-start.1 = (bf16[48,4096]{1,0:T(8,128)(2,1)}, bf16[48,4096]{1,0:T(8,128)(2,1)}, u32[]{:S(2)}, u32[]{:S(2)}) collective-permute-start(bf16[48,4096]{1,0:T(8,128)(2,1)} %get-tuple-element.426), channel_id=1, source_target_pairs={{0,8},{1,9},{2,10},{3,11},{4,12},{5,13},{6,14},{7,15},{8,0},{9,1},... | collective-permute-start | bytes 1179656 | tf_op jit(solution)/shard_map/cond/branch_0_fun/ppermute | solution.py:226
  46.4 36.6 %collective-permute-start.2 = (bf16[48,4096]{1,0:T(8,128)(2,1)}, bf16[48,4096]{1,0:T(8,128)(2,1)}, u32[]{:S(2)}, u32[]{:S(2)}) collective-permute-start(bf16[48,4096]{1,0:T(8,128)(2,1)} %get-tuple-element.427), channel_id=1, source_target_pairs={{0,4},{1,5},{2,6},{3,7},{4,0},{5,1},{6,2},{7,3},{8,12},{9,13},{10,... | collective-permute-start | bytes 1179656 | tf_op jit(solution)/shard_map/cond/branch_0_fun/ppermute | solution.py:226
  49.2 4.8 %collective-permute-start.3 = (bf16[48,8192]{1,0:T(8,128)(2,1)S(1)}, bf16[48,8192]{1,0:T(8,128)(2,1)S(1)}, u32[]{:S(2)}, u32[]{:S(2)}) collective-permute-start(bf16[48,8192]{1,0:T(8,128)(2,1)S(1)} %constant_dynamic-update-slice_fusion.refs_1_), channel_id=1, source_target_pairs={{0,1},{1,0},{2,3},{3,2},{4,5},{5,4},{6,7},{7,6},{8,9},{9,8},{10,11... | collective-permute-start | bytes 2359304 | tf_op jit(solution)/shard_map/cond/branch_0_fun/ppermute | solution.py:226
  49.3 26.2 %collective-permute-start.4 = (bf16[128,4096]{1,0:T(8,128)(2,1)}, bf16[128,4096]{1,0:T(8,128)(2,1)S(1)}, u32[]{:S(2)}, u32[]{:S(2)}) collective-permute-start(bf16[128,4096]{1,0:T(8,128)(2,1)} %get-tuple-element.439.refs_5_.refs_4_), channel_id=1, source_target_pairs={{0,2},{1,3},{2,0},{3,1},{4,6},{5,7},{6,4},{7,5},{8,10},{9,11},{10,... | collective-permute-start | bytes 3145736 | tf_op jit(solution)/shard_map/cond/branch_0_fun/ppermute | solution.py:226
  54.0 26.6 %collective-permute-start.6 = (bf16[256,512]{1,0:T(8,128)(2,1)S(1)}, bf16[256,512]{1,0:T(8,128)(2,1)S(1)}, u32[]{:S(2)}, u32[]{:S(2)}) collective-permute-start(bf16[256,512]{1,0:T(8,128)(2,1)S(1)} %pad_maximum_fusion), channel_id=1, source_target_pairs={{0,2},{1,3},{2,0},{3,1},{4,6},{5,7},{6,4},{7,5},{8,10},{9,11},{10,... | collective-permute-start | bytes 786440 | tf_op jit(solution)/shard_map/cond/branch_0_fun/ppermute | solution.py:226
  55.6 19.9 %copy-start.2 = (bf16[128,8192]{1,0:T(8,128)(2,1)S(1)}, bf16[128,8192]{1,0:T(8,128)(2,1)}, u32[]{:S(2)}) copy-start(bf16[128,8192]{1,0:T(8,128)(2,1)} %copy-done.1) | copy-start | bytes 6291460
  55.6 26.1 %slice-start = ((s8[8388608]{0:T(1024)(128)(4,1)}), s8[4194304]{0:T(1024)(128)(4,1)S(1)}, s32[]{:S(2)}) async-start(s8[8388608]{0:T(1024)(128)(4,1)} %bitcast.765), calls=%async_computation | async-start | bytes 8388608
  60.6 21.1 %slice-start.1 = ((s8[8388608]{0:T(1024)(128)(4,1)}), s8[4194304]{0:T(1024)(128)(4,1)S(1)}, s32[]{:S(2)}) async-start(s8[8388608]{0:T(1024)(128)(4,1)} %bitcast.765), calls=%async_computation.1 | async-start | bytes 8388608
  78.6 2.1 %collective-permute-start.5 = (f32[176,64]{1,0:T(8,128)S(1)}, f32[176,64]{1,0:T(8,128)S(1)}, u32[]{:S(2)}, u32[]{:S(2)}) collective-permute-start(f32[176,64]{1,0:T(8,128)S(1)} %get-tuple-element.932), channel_id=1, source_target_pairs={{0,1},{1,0},{2,3},{3,2},{4,5},{5,4},{6,7},{7,6},{8,9},{9,8},{10,11... | collective-permute-start | bytes 135176 | tf_op jit(solution)/shard_map/cond/branch_0_fun/ppermute | solution.py:226
  83.1 4.2 %copy-start.12 = (s32[2,128]{1,0:T(2,128)S(1)}, s32[2,128]{1,0:T(2,128)}, u32[]{:S(2)}) copy-start(s32[2,128]{1,0:T(2,128)} %copy-done.11) | copy-start | bytes 3076
  87.3 1.3 %collective-permute-start.7 = (f32[144,64]{1,0:T(8,128)S(1)}, f32[144,64]{1,0:T(8,128)S(1)}, u32[]{:S(2)}, u32[]{:S(2)}) collective-permute-start(f32[144,64]{1,0:T(8,128)S(1)} %branch_0_fun.10.one_ref), channel_id=1, source_target_pairs={{0,1},{1,0},{2,3},{3,2},{4,5},{5,4},{6,7},{7,6},{8,9},{9,8},{10,11... | collective-permute-start | bytes 110600 | tf_op jit(solution)/shard_map/cond/branch_0_fun/ppermute | solution.py:226
  89.5 6.5 %collective-permute-start.9 = (bf16[48,512]{1,0:T(8,128)(2,1)S(1)}, bf16[48,512]{1,0:T(8,128)(2,1)S(1)}, u32[]{:S(2)}, u32[]{:S(2)}) collective-permute-start(bf16[48,512]{1,0:T(8,128)(2,1)S(1)} %get-tuple-element.450), channel_id=1, source_target_pairs={{0,8},{1,9},{2,10},{3,11},{4,12},{5,13},{6,14},{7,15},{8,0},{9,1},... | collective-permute-start | bytes 147464 | tf_op jit(solution)/shard_map/cond/branch_0_fun/ppermute | solution.py:226
  90.8 6.3 %collective-permute-start.8 = (bf16[48,512]{1,0:T(8,128)(2,1)S(1)}, bf16[48,512]{1,0:T(8,128)(2,1)S(1)}, u32[]{:S(2)}, u32[]{:S(2)}) collective-permute-start(bf16[48,512]{1,0:T(8,128)(2,1)S(1)} %get-tuple-element.449), channel_id=1, source_target_pairs={{0,12},{1,13},{2,14},{3,15},{4,8},{5,9},{6,10},{7,11},{8,4},{9,5},... | collective-permute-start | bytes 147464 | tf_op jit(solution)/shard_map/cond/branch_0_fun/ppermute | solution.py:226
  92.3 5.1 %collective-permute-start.10 = (bf16[48,512]{1,0:T(8,128)(2,1)S(1)}, bf16[48,512]{1,0:T(8,128)(2,1)S(1)}, u32[]{:S(2)}, u32[]{:S(2)}) collective-permute-start(bf16[48,512]{1,0:T(8,128)(2,1)S(1)} %get-tuple-element.451), channel_id=1, source_target_pairs={{0,4},{1,5},{2,6},{3,7},{4,0},{5,1},{6,2},{7,3},{8,12},{9,13},{10,... | collective-permute-start | bytes 147464 | tf_op jit(solution)/shard_map/cond/branch_0_fun/ppermute | solution.py:226
  (4 other events, 5.9 us)

commit v4 on v3

--- a/solution.py
+++ b/solution.py
@@ -9,7 +9,7 @@
 
 LANES = 4
 MATMUL_T = (((1,), (1,)), ((), ()))
-PARAMS = pltpu.CompilerParams(vmem_limit_bytes=40 * 1024 * 1024)
+PARAMS = pltpu.CompilerParams(vmem_limit_bytes=12 * 1024 * 1024)
 
 
 def tile_of(width):
@@ -246,8 +246,10 @@
         most = max(2, 2 * rows // total)
         cap = min(rows, LANES * held * most)
         first = cap // 4
-        levels = [(2 * cap * k // 16 - 2 * first, cap * 3 // 4 - first) for k in (10, 11, 12)]
-        levels = levels + [(2 * cap - 2 * first, cap - first)]
+        levels = [
+            (2 * cap * chip // 16 - 2 * first, cap * device // 8 - first)
+            for chip, device in ((10, 6), (11, 6), (12, 6), (13, 7), (16, 8))
+        ]
         flips = sorted(range(1, planes), key=lambda k: -k)
         half = width // 2
 

time: 99.9 us -> 99.9 us (level)
    unnamed x30 -> x10, local copies, waits for them, and re-layouts: 2.25 us -> 1.25 us
    another operation x2 -> x22, local copies, waits for them, and re-layouts: 0.01 us -> 1.01 us
  transfers between devices with their start and end apart: 23 -> 23, of which waited for: 10 -> 9; matrix products, arithmetic and copies ran while one was open for 15% -> 15% of each run, Pallas kernels for 12% -> 12%
where the time goes in v4:
time: 99.9 us
  waiting for transfers between devices  36.3 us (36%)
  starting transfers between devices  24.7 us (25%)
  Pallas kernels  20.6 us (21%)
  local copies, waits for them, and re-layouts  8.36 us (8%)
  other arithmetic  6.74 us (7%)
  matrix products  1.93 us (2%)
  loops' own time  1.18 us (1%)
    ppermute x23, waiting for transfers between devices, flipped(): return lax.ppermute(x, axis, [(i, i ^ flip) for i in range(size)])  36.3 us
    ppermute x23, starting transfers between devices, flipped(): return lax.ppermute(x, axis, [(i, i ^ flip) for i in range(size)])  24.7 us
    pallas_call x3, Pallas kernels, shrink(): pl.pallas_call(functools.partial(shrink_body, len(xs), len(ws), rank, sta...  12.2 us
    pallas_call x2, Pallas kernels, pack(): pl.pallas_call(functools.partial(pack_body, flips, number, start), grid_s...  5.02 us
    dynamic_slice x2, local copies, waits for them, and re-layouts, local(): half_of = lambda x, c: lax.dynamic_slice_in_dim(x, c * half, half, axis=1)  4.63 us
  transfers between devices with their start and end apart: 23, of which 9 were waited for; matrix products, arithmetic and copies ran while one was open for 15% of the time, Pallas kernels for 12%

profile of v4, /device:TPU:0, one launch (start us, length us, event | category | flops | bytes accessed | tf_op | source)
XLA Modules:
  0.0 99.9 jit_solution(17348735695892718286)
XLA Ops:
  1.6 3.1 %collective-permute-start.55 = (s32[1,128]{1,0:T(1,128)S(1)}, s32[1,128]{1,0:T(1,128)S(1)}, u32[]{:S(2)}, u32[]{:S(2)}) collective-permute-start(s32[1,128]{1,0:T(1,128)S(1)} %get-tuple-element.1404), channel_id=1, source_target_pairs={{0,4},{1,5},{2,6},{3,7},{4,0},{5,1},{6,2},{7,3},{8,12},{9,13},{10,... | collective-permute-start | bytes 1544 | tf_op jit(solution)/shard_map/ppermute | solution.py:226
  4.7 2.3 %constant_dynamic-slice_fusion.1 = bf16[128,4096]{1,0:T(8,128)(2,1)} fusion(bf16[128,8192]{1,0:T(8,128)(2,1)} %bitcast.967, s32[]{:T(128)S(6)} %select_n.2050), kind=kLoop, calls=%fused_computation.1336 | loop fusion | bytes 2097156 | tf_op jit(solution)/shard_map/dynamic_slice | solution.py:273
  7.0 1.5 %collective-permute-start.66 = (bf16[128,4096]{1,0:T(8,128)(2,1)}, bf16[128,4096]{1,0:T(8,128)(2,1)}, u32[]{:S(2)}, u32[]{:S(2)}) collective-permute-start(bf16[128,4096]{1,0:T(8,128)(2,1)} %constant_dynamic-slice_fusion.1), channel_id=1, source_target_pairs={{0,2},{1,3},{2,0},{3,1},{4,6},{5,7},{6,4},{7,5},{8,10},{9,11},{10,... | collective-permute-start | bytes 3145736 | tf_op jit(solution)/shard_map/ppermute | solution.py:226
  9.2 2.7 %collective-permute-start.56 = (s32[2,128]{1,0:T(2,128)S(1)}, s32[2,128]{1,0:T(2,128)S(1)}, u32[]{:S(2)}, u32[]{:S(2)}) collective-permute-start(s32[2,128]{1,0:T(2,128)S(1)} %pad_add_fusion.17), channel_id=1, source_target_pairs={{0,8},{1,9},{2,10},{3,11},{4,12},{5,13},{6,14},{7,15},{8,0},{9,1},... | collective-permute-start | bytes 3080 | tf_op jit(solution)/shard_map/ppermute | solution.py:226
  11.9 1.7 %shard_map.74 = (bf16[16,8192]{1,0:T(8,128)(2,1)S(1)}, bf16[16,8192]{1,0:T(8,128)(2,1)S(1)}, bf16[16,8192]{1,0:T(8,128)(2,1)S(1)}) custom-call(s32[3]{0:T(128)S(1)} %pad_add_fusion.18.place_ref, s32[1,128]{1,0:T(1,128)S(1)} %get-tuple-element.1403.goes_ref, s32[1,128]{1,0:T(1,128)S(1)} %bitcast.949, bf16[128,8192]{1,0:T(8,128)(2,1)S(1)} %copy-done), custom_call_target="tpu_custom_call" | custom-call | flops 100663296 | bytes 2883584 | tf_op jit(solution)/shard_map/pallas_call | solution.py:90
  13.9 2.5 %collective-permute-start.63 = (bf16[16,8192]{1,0:T(8,128)(2,1)S(1)}, bf16[16,8192]{1,0:T(8,128)(2,1)S(1)}, u32[]{:S(2)}, u32[]{:S(2)}) collective-permute-start(bf16[16,8192]{1,0:T(8,128)(2,1)S(1)} %get-tuple-element.732), channel_id=1, source_target_pairs={{0,12},{1,13},{2,14},{3,15},{4,8},{5,9},{6,10},{7,11},{8,4},{9,5},... | collective-permute-start | bytes 786440 | tf_op jit(solution)/shard_map/ppermute | solution.py:226
  16.6 1.7 %collective-permute-start.65 = (bf16[16,8192]{1,0:T(8,128)(2,1)S(1)}, bf16[16,8192]{1,0:T(8,128)(2,1)}, u32[]{:S(2)}, u32[]{:S(2)}) collective-permute-start(bf16[16,8192]{1,0:T(8,128)(2,1)S(1)} %get-tuple-element.734), channel_id=1, source_target_pairs={{0,4},{1,5},{2,6},{3,7},{4,0},{5,1},{6,2},{7,3},{8,12},{9,13},{10,... | collective-permute-start | bytes 786440 | tf_op jit(solution)/shard_map/ppermute | solution.py:226
  18.3 2.3 %constant_dynamic-slice_fusion = bf16[128,4096]{1,0:T(8,128)(2,1)} fusion(bf16[128,8192]{1,0:T(8,128)(2,1)} %collective-permute-done.58, s32[]{:T(128)S(6)} %select_n.2050), kind=kLoop, calls=%fused_computation.1335 | loop fusion | bytes 2097156 | tf_op jit(solution)/shard_map/dynamic_slice | solution.py:273
  21.2 1.5 %shard_map.75 = s32[1,128]{1,0:T(1,128)} custom-call(s32[3]{0:T(128)S(1)} %pad_add_fusion.18.place_ref, s32[4,128]{1,0:T(4,128)} %copy-done.23, s32[4,128]{1,0:T(4,128)} %copy-done.24), custom_call_target="tpu_custom_call" | custom-call | tf_op jit(solution)/shard_map/pallas_call | solution.py:43
  23.9 8.9 %collective-permute-done.61 = s32[1,128]{1,0:T(1,128)S(1)} collective-permute-done((s32[1,128]{1,0:T(1,128)}, s32[1,128]{1,0:T(1,128)S(1)}, u32[]{:S(2)}, u32[]{:S(2)}) %collective-permute-start.61) | collective-permute-done | bytes 544 | tf_op jit(solution)/shard_map/ppermute | solution.py:226
  33.6 1.5 %collective-permute-start.62 = (s32[1,128]{1,0:T(1,128)S(1)}, s32[1,128]{1,0:T(1,128)S(1)}, u32[]{:S(2)}, u32[]{:S(2)}) collective-permute-start(s32[1,128]{1,0:T(1,128)S(1)} %max.6), channel_id=1, source_target_pairs={{0,16},{16,0},{1,17},{17,1},{2,18},{18,2},{3,19},{19,3},{4,20},{20... | collective-permute-start | bytes 1544 | tf_op jit(solution)/shard_map/ppermute | solution.py:226
  35.8 1.4 %collective-permute-done.62 = s32[1,128]{1,0:T(1,128)S(1)} collective-permute-done((s32[1,128]{1,0:T(1,128)S(1)}, s32[1,128]{1,0:T(1,128)S(1)}, u32[]{:S(2)}, u32[]{:S(2)}) %collective-permute-start.62) | collective-permute-done | bytes 544 | tf_op jit(solution)/shard_map/ppermute | solution.py:226
  37.2 3.1 %collective-permute-done.64 = bf16[16,8192]{1,0:T(8,128)(2,1)S(1)} collective-permute-done((bf16[16,8192]{1,0:T(8,128)(2,1)S(1)}, bf16[16,8192]{1,0:T(8,128)(2,1)S(1)}, u32[]{:S(2)}, u32[]{:S(2)}) %collective-permute-start.64) | collective-permute-done | bytes 262176 | tf_op jit(solution)/shard_map/ppermute | solution.py:226
  40.3 59.0 %conditional.3 = (bf16[128,512]{1,0:T(8,128)(2,1)S(1)}) conditional(s32[]{:T(128)} %bitcast.187, (s32[]{:T(128)}, s32[]{:T(128)}, s32[2,128]{1,0:T(2,128)S(1)}, pred[2,128]{1,0:T(4,128)(4,1)S(1)}, pred[2,128]{1,0:T(4,128)(4,1)S(1)}, /*index=5*/s32[2,128]{1,0:T(2,128)S(1)}, s32[2,128]{1,0:T(2,128)S(1)}, ...), branch_computations={%region_2.12_spmd, %region_12.22_spmd, %region_22.32_spmd, %region... | conditional | flops 4556362752 | bytes 99597904
  40.7 3.3 %branch_1_fun.6 = (bf16[56,4096]{1,0:T(8,128)(2,1)}, bf16[56,4096]{1,0:T(8,128)(2,1)}, bf16[56,4096]{1,0:T(8,128)(2,1)}) custom-call(s32[3]{0:T(128)S(1)} %pad_add_fusion.5.place_ref, s32[2,128]{1,0:T(2,128)S(1)} %get-tuple-element.1195.goes_ref, s32[2,128]{1,0:T(2,128)S(1)} %get-tuple-element.1261.within_ref, ...), custom_call_target="tpu_custom_call" | custom-call | flops 352321536 | bytes 3473408 | tf_op jit(solution)/shard_map/cond/branch_1_fun/pallas_call | solution.py:90
  44.0 2.7 %collective-permute-start.11 = (bf16[56,4096]{1,0:T(8,128)(2,1)}, bf16[56,4096]{1,0:T(8,128)(2,1)}, u32[]{:S(2)}, u32[]{:S(2)}) collective-permute-start(bf16[56,4096]{1,0:T(8,128)(2,1)} %get-tuple-element.555), channel_id=1, source_target_pairs={{0,12},{1,13},{2,14},{3,15},{4,8},{5,9},{6,10},{7,11},{8,4},{9,5},... | collective-permute-start | bytes 1376264 | tf_op jit(solution)/shard_map/cond/branch_1_fun/ppermute | solution.py:226
  46.7 1.7 %collective-permute-start.13 = (bf16[56,4096]{1,0:T(8,128)(2,1)}, bf16[56,4096]{1,0:T(8,128)(2,1)}, u32[]{:S(2)}, u32[]{:S(2)}) collective-permute-start(bf16[56,4096]{1,0:T(8,128)(2,1)} %get-tuple-element.557), channel_id=1, source_target_pairs={{0,4},{1,5},{2,6},{3,7},{4,0},{5,1},{6,2},{7,3},{8,12},{9,13},{10,... | collective-permute-start | bytes 1376264 | tf_op jit(solution)/shard_map/cond/branch_1_fun/ppermute | solution.py:226
  48.5 1.0 constant_dynamic-update-slice_fusion.6.refs_1_
  53.4 0.9 pad_maximum_fusion.1
  54.3 1.6 %collective-permute-start.17 = (bf16[256,512]{1,0:T(8,128)(2,1)S(1)}, bf16[256,512]{1,0:T(8,128)(2,1)S(1)}, u32[]{:S(2)}, u32[]{:S(2)}) collective-permute-start(bf16[256,512]{1,0:T(8,128)(2,1)S(1)} %pad_maximum_fusion.1), channel_id=1, source_target_pairs={{0,2},{1,3},{2,0},{3,1},{4,6},{5,7},{6,4},{7,5},{8,10},{9,11},{10,... | collective-permute-start | bytes 786440 | tf_op jit(solution)/shard_map/cond/branch_1_fun/ppermute | solution.py:226
  55.9 5.0 %branch_1_fun.7 = f32[352,64]{1,0:T(8,128)S(1)} custom-call(s32[3]{0:T(128)S(1)} %get-tuple-element.564.place_ref, bf16[128,8192]{1,0:T(8,128)(2,1)} %copy-done.3, bf16[48,8192]{1,0:T(8,128)(2,1)S(1)} %constant_dynamic-update-slice_fusion.6.refs_1_, bf16[128,8192]{1,0:T(8,128)(2,1)} %get-tuple-element.546.refs_1_.refs_2_, ...), custom_call_target="tpu_custom_call" | custom-call | flops 1107296256 | bytes 6029312 | tf_op jit(solution)/shard_map/cond/branch_1_fun/pallas_call | solution.py:147
  60.9 14.9 %collective-permute-done.15.refs_4_.refs_6_ = bf16[128,4096]{1,0:T(8,128)(2,1)S(1)} collective-permute-done((bf16[128,4096]{1,0:T(8,128)(2,1)}, bf16[128,4096]{1,0:T(8,128)(2,1)S(1)}, u32[]{:S(2)}, u32[]{:S(2)}) %collective-permute-start.15) | collective-permute-done | bytes 1048608 | tf_op jit(solution)/shard_map/cond/branch_1_fun/ppermute | solution.py:226
  75.8 3.0 %branch_1_fun.8 = f32[352,64]{1,0:T(8,128)S(1)} custom-call(s32[3]{0:T(128)S(1)} %get-tuple-element.564.place_ref, bf16[128,8192]{1,0:T(8,128)(2,1)S(1)} %copy-done.4, bf16[48,8192]{1,0:T(8,128)(2,1)S(1)} %constant_dynamic-update-slice_fusion.6.refs_1_, bf16[128,8192]{1,0:T(8,128)(2,1)} %get-tuple-element.546.refs_1_.refs_2_, ...), custom_call_target="tpu_custom_call" | custom-call | flops 369098752 | bytes 3932160 | tf_op jit(solution)/shard_map/cond/branch_1_fun/pallas_call | solution.py:147
  79.0 2.0 %collective-permute-done.17 = bf16[256,512]{1,0:T(8,128)(2,1)S(1)} collective-permute-done((bf16[256,512]{1,0:T(8,128)(2,1)S(1)}, bf16[256,512]{1,0:T(8,128)(2,1)S(1)}, u32[]{:S(2)}, u32[]{:S(2)}) %collective-permute-start.17) | collective-permute-done | bytes 262176 | tf_op jit(solution)/shard_map/cond/branch_1_fun/ppermute | solution.py:226
  81.0 0.9 branch_1_fun.9
  82.0 1.3 %convert_add_fusion.1 = f32[128,512]{1,0:T(8,128)S(1)} fusion(bf16[176,512]{1,0:T(8,128)(2,1)S(1)} %branch_1_fun.9, bf16[128,8192]{1,0:T(8,128)(2,1)S(1)} %copy-done.4, bf16[8192,512]{1,0:T(8,128)(2,1)S(1)} %bitcast.953), kind=kOutput, calls=%fused_computation.264 | convolution fusion | flops 1073872896 | bytes 10878976 | tf_op jit(solution)/shard_map/cond/branch_1_fun/dot_general | solution.py:353
  83.3 1.8 %collective-permute-done.12.refs_1_ = bf16[56,4096]{1,0:T(8,128)(2,1)} collective-permute-done((bf16[56,4096]{1,0:T(8,128)(2,1)}, bf16[56,4096]{1,0:T(8,128)(2,1)}, u32[]{:S(2)}, u32[]{:S(2)}) %collective-permute-start.12) | collective-permute-done | bytes 458784 | tf_op jit(solution)/shard_map/cond/branch_1_fun/ppermute | solution.py:226
  85.2 4.2 %branch_1_fun.10.one_ref = f32[168,64]{1,0:T(8,128)S(1)} custom-call(s32[3]{0:T(128)S(1)} %get-tuple-element.564.place_ref, bf16[56,4096]{1,0:T(8,128)(2,1)} %collective-permute-done.11.refs_0_, bf16[56,4096]{1,0:T(8,128)(2,1)} %collective-permute-done.12.refs_1_, bf16[56,4096]{1,0:T(8,128)(2,1)} %collective-permute-done.13.refs_2_, ...), custom_call_target="tpu_custom_call" | custom-call | flops 704643072 | bytes 5570560 | tf_op jit(solution)/shard_map/cond/branch_1_fun/pallas_call | solution.py:147
  89.5 1.2 %collective-permute-done.18.two_ref = f32[168,64]{1,0:T(8,128)S(1)} collective-permute-done((f32[168,64]{1,0:T(8,128)S(1)}, f32[168,64]{1,0:T(8,128)S(1)}, u32[]{:S(2)}, u32[]{:S(2)}) %collective-permute-start.18) | collective-permute-done | bytes 43040 | tf_op jit(solution)/shard_map/cond/branch_1_fun/ppermute | solution.py:226
  91.7 1.4 %collective-permute-start.19 = (bf16[48,512]{1,0:T(8,128)(2,1)S(1)}, bf16[48,512]{1,0:T(8,128)(2,1)S(1)}, u32[]{:S(2)}, u32[]{:S(2)}) collective-permute-start(bf16[48,512]{1,0:T(8,128)(2,1)S(1)} %get-tuple-element.579), channel_id=1, source_target_pairs={{0,12},{1,13},{2,14},{3,15},{4,8},{5,9},{6,10},{7,11},{8,4},{9,5},... | collective-permute-start | bytes 147464 | tf_op jit(solution)/shard_map/cond/branch_1_fun/ppermute | solution.py:226
  93.1 2.0 %collective-permute-start.21 = (bf16[48,512]{1,0:T(8,128)(2,1)S(1)}, bf16[48,512]{1,0:T(8,128)(2,1)S(1)}, u32[]{:S(2)}, u32[]{:S(2)}) collective-permute-start(bf16[48,512]{1,0:T(8,128)(2,1)S(1)} %get-tuple-element.581), channel_id=1, source_target_pairs={{0,4},{1,5},{2,6},{3,7},{4,0},{5,1},{6,2},{7,3},{8,12},{9,13},{10,... | collective-permute-start | bytes 147464 | tf_op jit(solution)/shard_map/cond/branch_1_fun/ppermute | solution.py:226
  95.2 2.8 %collective-permute-done.20 = bf16[48,512]{1,0:T(8,128)(2,1)S(1)} collective-permute-done((bf16[48,512]{1,0:T(8,128)(2,1)S(1)}, bf16[48,512]{1,0:T(8,128)(2,1)S(1)}, u32[]{:S(2)}, u32[]{:S(2)}) %collective-permute-start.20) | collective-permute-done | bytes 49184 | tf_op jit(solution)/shard_map/cond/branch_1_fun/ppermute | solution.py:226
  (115 shorter events, 12.5 us)
Async XLA Ops:
  0.0 11.9 %copy-start = (bf16[128,8192]{1,0:T(8,128)(2,1)S(1)}, bf16[128,8192]{1,0:T(8,128)(2,1)}, u32[]{:S(2)}) copy-start(bf16[128,8192]{1,0:T(8,128)(2,1)} %refs_0_.1) | copy-start | bytes 6291460
  0.0 13.8 %collective-permute-start.57 = (bf16[128,8192]{1,0:T(8,128)(2,1)}, bf16[128,8192]{1,0:T(8,128)(2,1)}, u32[]{:S(2)}, u32[]{:S(2)}) collective-permute-start(bf16[128,8192]{1,0:T(8,128)(2,1)} %refs_0_.1), channel_id=1, source_target_pairs={{0,1},{1,0},{2,3},{3,2},{4,5},{5,4},{6,7},{7,6},{8,9},{9,8},{10,11... | collective-permute-start | bytes 6291464 | tf_op jit(solution)/shard_map/ppermute | solution.py:226
  0.5 13.3 %collective-permute-start.58 = (bf16[128,8192]{1,0:T(8,128)(2,1)}, bf16[128,8192]{1,0:T(8,128)(2,1)}, u32[]{:S(2)}, u32[]{:S(2)}) collective-permute-start(bf16[128,8192]{1,0:T(8,128)(2,1)} %bitcast.966), channel_id=1, source_target_pairs={{0,1},{1,0},{2,3},{3,2},{4,5},{5,4},{6,7},{7,6},{8,9},{9,8},{10,11... | collective-permute-start | bytes 6291464 | tf_op jit(solution)/shard_map/ppermute | solution.py:226
  1.6 7.6 %collective-permute-start.55 = (s32[1,128]{1,0:T(1,128)S(1)}, s32[1,128]{1,0:T(1,128)S(1)}, u32[]{:S(2)}, u32[]{:S(2)}) collective-permute-start(s32[1,128]{1,0:T(1,128)S(1)} %get-tuple-element.1404), channel_id=1, source_target_pairs={{0,4},{1,5},{2,6},{3,7},{4,0},{5,1},{6,2},{7,3},{8,12},{9,13},{10,... | collective-permute-start | bytes 1544 | tf_op jit(solution)/shard_map/ppermute | solution.py:226
  4.7 9.1 %collective-permute-start.59 = (bf16[128,512]{1,0:T(8,128)(2,1)}, bf16[128,512]{1,0:T(8,128)(2,1)}, u32[]{:S(2)}, u32[]{:S(2)}) collective-permute-start(bf16[128,512]{1,0:T(8,128)(2,1)} %bitcast.960), channel_id=1, source_target_pairs={{0,1},{1,0},{2,3},{3,2},{4,5},{5,4},{6,7},{7,6},{8,9},{9,8},{10,11... | collective-permute-start | bytes 393224 | tf_op jit(solution)/shard_map/ppermute | solution.py:226
  7.0 30.2 %collective-permute-start.66 = (bf16[128,4096]{1,0:T(8,128)(2,1)}, bf16[128,4096]{1,0:T(8,128)(2,1)}, u32[]{:S(2)}, u32[]{:S(2)}) collective-permute-start(bf16[128,4096]{1,0:T(8,128)(2,1)} %constant_dynamic-slice_fusion.1), channel_id=1, source_target_pairs={{0,2},{1,3},{2,0},{3,1},{4,6},{5,7},{6,4},{7,5},{8,10},{9,11},{10,... | collective-permute-start | bytes 3145736 | tf_op jit(solution)/shard_map/ppermute | solution.py:226
  9.2 4.5 %collective-permute-start.56 = (s32[2,128]{1,0:T(2,128)S(1)}, s32[2,128]{1,0:T(2,128)S(1)}, u32[]{:S(2)}, u32[]{:S(2)}) collective-permute-start(s32[2,128]{1,0:T(2,128)S(1)} %pad_add_fusion.17), channel_id=1, source_target_pairs={{0,8},{1,9},{2,10},{3,11},{4,12},{5,13},{6,14},{7,15},{8,0},{9,1},... | collective-permute-start | bytes 3080 | tf_op jit(solution)/shard_map/ppermute | solution.py:226
  11.9 28.4 %copy-start.11 = (bf16[2,64,512]{2,1,0:T(8,128)(2,1)S(1)}, bf16[2,64,512]{2,1,0:T(8,128)(2,1)}, u32[]{:S(2)}) copy-start(bf16[2,64,512]{2,1,0:T(8,128)(2,1)} %param.16) | copy-start | bytes 393220
  13.8 6.9 %copy-start.23 = (s32[4,128]{1,0:T(4,128)}, s32[4,128]{1,0:T(4,128)S(1)}, u32[]{:S(2)}) copy-start(s32[4,128]{1,0:T(4,128)S(1)} %pad_add_fusion.16.mine_ref) | copy-start | bytes 6148
  13.8 6.9 %collective-permute-start.60 = (s32[4,128]{1,0:T(4,128)S(1)}, s32[4,128]{1,0:T(4,128)S(1)}, u32[]{:S(2)}, u32[]{:S(2)}) collective-permute-start(s32[4,128]{1,0:T(4,128)S(1)} %pad_add_fusion.16.mine_ref), channel_id=1, source_target_pairs={{0,1},{1,0},{2,3},{3,2},{4,5},{5,4},{6,7},{7,6},{8,9},{9,8},{10,11... | collective-permute-start | bytes 6152 | tf_op jit(solution)/shard_map/ppermute | solution.py:226
  13.9 23.3 %collective-permute-start.63 = (bf16[16,8192]{1,0:T(8,128)(2,1)S(1)}, bf16[16,8192]{1,0:T(8,128)(2,1)S(1)}, u32[]{:S(2)}, u32[]{:S(2)}) collective-permute-start(bf16[16,8192]{1,0:T(8,128)(2,1)S(1)} %get-tuple-element.732), channel_id=1, source_target_pairs={{0,12},{1,13},{2,14},{3,15},{4,8},{5,9},{6,10},{7,11},{8,4},{9,5},... | collective-permute-start | bytes 786440 | tf_op jit(solution)/shard_map/ppermute | solution.py:226
  16.4 23.9 %collective-permute-start.64 = (bf16[16,8192]{1,0:T(8,128)(2,1)S(1)}, bf16[16,8192]{1,0:T(8,128)(2,1)S(1)}, u32[]{:S(2)}, u32[]{:S(2)}) collective-permute-start(bf16[16,8192]{1,0:T(8,128)(2,1)S(1)} %get-tuple-element.733), channel_id=1, source_target_pairs={{0,8},{1,9},{2,10},{3,11},{4,12},{5,13},{6,14},{7,15},{8,0},{9,1},... | collective-permute-start | bytes 786440 | tf_op jit(solution)/shard_map/ppermute | solution.py:226
  16.6 23.7 %collective-permute-start.65 = (bf16[16,8192]{1,0:T(8,128)(2,1)S(1)}, bf16[16,8192]{1,0:T(8,128)(2,1)}, u32[]{:S(2)}, u32[]{:S(2)}) collective-permute-start(bf16[16,8192]{1,0:T(8,128)(2,1)S(1)} %get-tuple-element.734), channel_id=1, source_target_pairs={{0,4},{1,5},{2,6},{3,7},{4,0},{5,1},{6,2},{7,3},{8,12},{9,13},{10,... | collective-permute-start | bytes 786440 | tf_op jit(solution)/shard_map/ppermute | solution.py:226
  22.7 10.2 %collective-permute-start.61 = (s32[1,128]{1,0:T(1,128)}, s32[1,128]{1,0:T(1,128)S(1)}, u32[]{:S(2)}, u32[]{:S(2)}) collective-permute-start(s32[1,128]{1,0:T(1,128)} %shard_map.75), channel_id=1, source_target_pairs={{0,2},{1,3},{2,0},{3,1},{4,6},{5,7},{6,4},{7,5},{8,10},{9,11},{10,... | collective-permute-start | bytes 1544 | tf_op jit(solution)/shard_map/ppermute | solution.py:226
  33.6 3.5 %collective-permute-start.62 = (s32[1,128]{1,0:T(1,128)S(1)}, s32[1,128]{1,0:T(1,128)S(1)}, u32[]{:S(2)}, u32[]{:S(2)}) collective-permute-start(s32[1,128]{1,0:T(1,128)S(1)} %max.6), channel_id=1, source_target_pairs={{0,16},{16,0},{1,17},{17,1},{2,18},{18,2},{3,19},{19,3},{4,20},{20... | collective-permute-start | bytes 1544 | tf_op jit(solution)/shard_map/ppermute | solution.py:226
  40.5 3.5 %copy-start.3 = (bf16[128,8192]{1,0:T(8,128)(2,1)}, bf16[128,8192]{1,0:T(8,128)(2,1)S(1)}, u32[]{:S(2)}) copy-start(bf16[128,8192]{1,0:T(8,128)(2,1)S(1)} %get-tuple-element.562.refs_0_) | copy-start | bytes 6291460 | tf_op jit(solution)/shard_map/conditional.1
  40.7 9.5 %copy-start.31 = (s32[2]{0:T(128)S(1)}, s32[2]{0:T(128)}, u32[]{:S(2)}) copy-start(s32[2]{0:T(128)} %get-tuple-element.559) | copy-start | bytes 28 | tf_op jit(solution)/shard_map/conditional.1
  44.0 39.3 %collective-permute-start.11 = (bf16[56,4096]{1,0:T(8,128)(2,1)}, bf16[56,4096]{1,0:T(8,128)(2,1)}, u32[]{:S(2)}, u32[]{:S(2)}) collective-permute-start(bf16[56,4096]{1,0:T(8,128)(2,1)} %get-tuple-element.555), channel_id=1, source_target_pairs={{0,12},{1,13},{2,14},{3,15},{4,8},{5,9},{6,10},{7,11},{8,4},{9,5},... | collective-permute-start | bytes 1376264 | tf_op jit(solution)/shard_map/cond/branch_1_fun/ppermute | solution.py:226
  46.7 38.3 %collective-permute-start.12 = (bf16[56,4096]{1,0:T(8,128)(2,1)}, bf16[56,4096]{1,0:T(8,128)(2,1)}, u32[]{:S(2)}, u32[]{:S(2)}) collective-permute-start(bf16[56,4096]{1,0:T(8,128)(2,1)} %get-tuple-element.556), channel_id=1, source_target_pairs={{0,8},{1,9},{2,10},{3,11},{4,12},{5,13},{6,14},{7,15},{8,0},{9,1},... | collective-permute-start | bytes 1376264 | tf_op jit(solution)/shard_map/cond/branch_1_fun/ppermute | solution.py:226
  46.7 38.3 %collective-permute-start.13 = (bf16[56,4096]{1,0:T(8,128)(2,1)}, bf16[56,4096]{1,0:T(8,128)(2,1)}, u32[]{:S(2)}, u32[]{:S(2)}) collective-permute-start(bf16[56,4096]{1,0:T(8,128)(2,1)} %get-tuple-element.557), channel_id=1, source_target_pairs={{0,4},{1,5},{2,6},{3,7},{4,0},{5,1},{6,2},{7,3},{8,12},{9,13},{10,... | collective-permute-start | bytes 1376264 | tf_op jit(solution)/shard_map/cond/branch_1_fun/ppermute | solution.py:226
  49.5 4.8 %collective-permute-start.14 = (bf16[48,8192]{1,0:T(8,128)(2,1)S(1)}, bf16[48,8192]{1,0:T(8,128)(2,1)S(1)}, u32[]{:S(2)}, u32[]{:S(2)}) collective-permute-start(bf16[48,8192]{1,0:T(8,128)(2,1)S(1)} %constant_dynamic-update-slice_fusion.6.refs_1_), channel_id=1, source_target_pairs={{0,1},{1,0},{2,3},{3,2},{4,5},{5,4},{6,7},{7,6},{8,9},{9,8},{10,11... | collective-permute-start | bytes 2359304 | tf_op jit(solution)/shard_map/cond/branch_1_fun/ppermute | solution.py:226
  49.6 26.2 %collective-permute-start.15 = (bf16[128,4096]{1,0:T(8,128)(2,1)}, bf16[128,4096]{1,0:T(8,128)(2,1)S(1)}, u32[]{:S(2)}, u32[]{:S(2)}) collective-permute-start(bf16[128,4096]{1,0:T(8,128)(2,1)} %get-tuple-element.569.refs_5_.refs_4_), channel_id=1, source_target_pairs={{0,2},{1,3},{2,0},{3,1},{4,6},{5,7},{6,4},{7,5},{8,10},{9,11},{10,... | collective-permute-start | bytes 3145736 | tf_op jit(solution)/shard_map/cond/branch_1_fun/ppermute | solution.py:226
  54.3 26.6 %collective-permute-start.17 = (bf16[256,512]{1,0:T(8,128)(2,1)S(1)}, bf16[256,512]{1,0:T(8,128)(2,1)S(1)}, u32[]{:S(2)}, u32[]{:S(2)}) collective-permute-start(bf16[256,512]{1,0:T(8,128)(2,1)S(1)} %pad_maximum_fusion.1), channel_id=1, source_target_pairs={{0,2},{1,3},{2,0},{3,1},{4,6},{5,7},{6,4},{7,5},{8,10},{9,11},{10,... | collective-permute-start | bytes 786440 | tf_op jit(solution)/shard_map/cond/branch_1_fun/ppermute | solution.py:226
  55.9 19.9 %copy-start.4 = (bf16[128,8192]{1,0:T(8,128)(2,1)S(1)}, bf16[128,8192]{1,0:T(8,128)(2,1)}, u32[]{:S(2)}) copy-start(bf16[128,8192]{1,0:T(8,128)(2,1)} %copy-done.3) | copy-start | bytes 6291460 | tf_op jit(solution)/shard_map/conditional.1
  55.9 26.1 %slice-start.2 = ((s8[8388608]{0:T(1024)(128)(4,1)}), s8[4194304]{0:T(1024)(128)(4,1)S(1)}, s32[]{:S(2)}) async-start(s8[8388608]{0:T(1024)(128)(4,1)} %bitcast.952), calls=%async_computation.2 | async-start | bytes 8388608 | tf_op jit(solution)/shard_map/conditional.1
  60.9 21.1 %slice-start.3 = ((s8[8388608]{0:T(1024)(128)(4,1)}), s8[4194304]{0:T(1024)(128)(4,1)S(1)}, s32[]{:S(2)}) async-start(s8[8388608]{0:T(1024)(128)(4,1)} %bitcast.952), calls=%async_computation.3 | async-start | bytes 8388608 | tf_op jit(solution)/shard_map/conditional.1
  78.9 2.1 %collective-permute-start.16 = (f32[176,64]{1,0:T(8,128)S(1)}, f32[176,64]{1,0:T(8,128)S(1)}, u32[]{:S(2)}, u32[]{:S(2)}) collective-permute-start(f32[176,64]{1,0:T(8,128)S(1)} %get-tuple-element.1247), channel_id=1, source_target_pairs={{0,1},{1,0},{2,3},{3,2},{4,5},{5,4},{6,7},{7,6},{8,9},{9,8},{10,11... | collective-permute-start | bytes 135176 | tf_op jit(solution)/shard_map/cond/branch_1_fun/ppermute | solution.py:226
  85.2 4.3 %copy-start.15 = (s32[2,128]{1,0:T(2,128)S(1)}, s32[2,128]{1,0:T(2,128)}, u32[]{:S(2)}) copy-start(s32[2,128]{1,0:T(2,128)} %copy-done.14) | copy-start | bytes 3076 | tf_op jit(solution)/shard_map/conditional.1
  89.4 1.3 %collective-permute-start.18 = (f32[168,64]{1,0:T(8,128)S(1)}, f32[168,64]{1,0:T(8,128)S(1)}, u32[]{:S(2)}, u32[]{:S(2)}) collective-permute-start(f32[168,64]{1,0:T(8,128)S(1)} %branch_1_fun.10.one_ref), channel_id=1, source_target_pairs={{0,1},{1,0},{2,3},{3,2},{4,5},{5,4},{6,7},{7,6},{8,9},{9,8},{10,11... | collective-permute-start | bytes 129032 | tf_op jit(solution)/shard_map/cond/branch_1_fun/ppermute | solution.py:226
  91.6 6.4 %collective-permute-start.20 = (bf16[48,512]{1,0:T(8,128)(2,1)S(1)}, bf16[48,512]{1,0:T(8,128)(2,1)S(1)}, u32[]{:S(2)}, u32[]{:S(2)}) collective-permute-start(bf16[48,512]{1,0:T(8,128)(2,1)S(1)} %get-tuple-element.580), channel_id=1, source_target_pairs={{0,8},{1,9},{2,10},{3,11},{4,12},{5,13},{6,14},{7,15},{8,0},{9,1},... | collective-permute-start | bytes 147464 | tf_op jit(solution)/shard_map/cond/branch_1_fun/ppermute | solution.py:226
  91.7 6.5 %collective-permute-start.19 = (bf16[48,512]{1,0:T(8,128)(2,1)S(1)}, bf16[48,512]{1,0:T(8,128)(2,1)S(1)}, u32[]{:S(2)}, u32[]{:S(2)}) collective-permute-start(bf16[48,512]{1,0:T(8,128)(2,1)S(1)} %get-tuple-element.579), channel_id=1, source_target_pairs={{0,12},{1,13},{2,14},{3,15},{4,8},{5,9},{6,10},{7,11},{8,4},{9,5},... | collective-permute-start | bytes 147464 | tf_op jit(solution)/shard_map/cond/branch_1_fun/ppermute | solution.py:226
  93.1 5.4 %collective-permute-start.21 = (bf16[48,512]{1,0:T(8,128)(2,1)S(1)}, bf16[48,512]{1,0:T(8,128)(2,1)S(1)}, u32[]{:S(2)}, u32[]{:S(2)}) collective-permute-start(bf16[48,512]{1,0:T(8,128)(2,1)S(1)} %get-tuple-element.581), channel_id=1, source_target_pairs={{0,4},{1,5},{2,6},{3,7},{4,0},{5,1},{6,2},{7,3},{8,12},{9,13},{10,... | collective-permute-start | bytes 147464 | tf_op jit(solution)/shard_map/cond/branch_1_fun/ppermute | solution.py:226
  (4 other events, 7.8 us)

commit v5 on v4

--- a/solution.py
+++ b/solution.py
@@ -350,7 +350,6 @@
                 first_mine = jnp.concatenate(first_arrived, axis=0)
                 first_mate = swap(first_mine, 1)
 
-                base = jnp.dot(tokens, matrix, preferred_element_type=jnp.float32)
                 columns, first_columns = [], [[], []]
                 for k in flips:
                     got = infos[k]
@@ -378,7 +377,10 @@
                 rows_here = [tokens, first_mine, mate_tokens, first_mate]
                 columns_here = jnp.concatenate([own_columns, mate_columns], axis=0)
                 sums = shrink(place, rows_here, down[:3], columns_here, rank)
-                sums = sums + shrink(place, rows_here, down[3:], columns_here, rank, 3 * held)
+                tokens, sums = lax.optimization_barrier((tokens, sums))
+                base = jnp.dot(tokens, matrix, preferred_element_type=jnp.float32)
+                base, last_down = lax.optimization_barrier((base, down[3]))
+                sums = sums + shrink(place, rows_here, [last_down], columns_here, rank, 3 * held)
                 (delta,) = expand(
                     place,
                     sums[:held_rows],

time: 99.9 us -> 100 us (level)
  waiting for transfers between devices: 36.3 us -> 29.3 us
  matrix products: 1.93 us -> 5.43 us
  other arithmetic: 6.74 us -> 10.2 us
    ppermute x23, waiting for transfers between devices: 36.3 us -> 29.3 us  [flipped(): return lax.ppermute(x, axis, [(i, i ^ flip) for i in range(size)])]
    dot_general x1, matrix products: 1.26 us -> 4.76 us  [branch(): base = jnp.dot(tokens, matrix, preferred_element_type=jnp.float32)]
    reduce_sum x8, other arithmetic: 0.91 us -> 2.11 us  [named_by(): jnp.sum(jnp.where(hot, column.reshape(1, -1) + 1, 0), 1, keepdims=True) - 1]
    sub x9, other arithmetic: 0.05 us -> 1.18 us  [named_by(): jnp.sum(jnp.where(hot, column.reshape(1, -1) + 1, 0), 1, keepdims=True) - 1]
  transfers between devices with their start and end apart: 23 -> 23, of which waited for: 9 -> 9; matrix products, arithmetic and copies ran while one was open for 15% -> 22% of each run, Pallas kernels for 12% -> 12%
where the time goes in v5:
time: 100 us; the launch traced here: 99.9 us
  waiting for transfers between devices  29.3 us (29%)
  starting transfers between devices  24.7 us (25%)
  Pallas kernels  20.1 us (20%)
  other arithmetic  10.2 us (10%)
  local copies, waits for them, and re-layouts  8.37 us (8%)
  matrix products  5.43 us (5%)
  loops' own time  1.68 us (2%)
    ppermute x23, waiting for transfers between devices, flipped(): return lax.ppermute(x, axis, [(i, i ^ flip) for i in range(size)])  29.3 us
    ppermute x23, starting transfers between devices, flipped(): return lax.ppermute(x, axis, [(i, i ^ flip) for i in range(size)])  24.7 us
    pallas_call x3, Pallas kernels, shrink(): pl.pallas_call(functools.partial(shrink_body, len(xs), len(ws), rank, sta...  11.9 us
    pallas_call x2, Pallas kernels, pack(): pl.pallas_call(functools.partial(pack_body, flips, number, start), grid_s...  4.99 us
    dot_general x1, matrix products, branch(): base = jnp.dot(tokens, matrix, preferred_element_type=jnp.float32)  4.76 us
    dynamic_slice x2, local copies, waits for them, and re-layouts, local(): half_of = lambda x, c: lax.dynamic_slice_in_dim(x, c * half, half, axis=1)  4.67 us
    reduce_sum x8, other arithmetic, named_by(): jnp.sum(jnp.where(hot, column.reshape(1, -1) + 1, 0), 1, keepdims=True) - 1  2.11 us
  transfers between devices with their start and end apart: 23, of which 9 were waited for; matrix products, arithmetic and copies ran while one was open for 22% of the time, Pallas kernels for 12%

profile of v5, /device:TPU:0, one launch (start us, length us, event | category | flops | bytes accessed | tf_op | source)
XLA Modules:
  0.0 99.9 jit_solution(4121030423125308306)
XLA Ops:
  1.6 3.1 %collective-permute-start.55 = (s32[1,128]{1,0:T(1,128)S(1)}, s32[1,128]{1,0:T(1,128)S(1)}, u32[]{:S(2)}, u32[]{:S(2)}) collective-permute-start(s32[1,128]{1,0:T(1,128)S(1)} %get-tuple-element.1424), channel_id=1, source_target_pairs={{0,4},{1,5},{2,6},{3,7},{4,0},{5,1},{6,2},{7,3},{8,12},{9,13},{10,... | collective-permute-start | bytes 1544 | tf_op jit(solution)/shard_map/ppermute | solution.py:226
  4.7 2.4 %constant_dynamic-slice_fusion.1 = bf16[128,4096]{1,0:T(8,128)(2,1)} fusion(bf16[128,8192]{1,0:T(8,128)(2,1)} %bitcast.957, s32[]{:T(128)S(6)} %select_n.2050), kind=kLoop, calls=%fused_computation.1336 | loop fusion | bytes 2097156 | tf_op jit(solution)/shard_map/dynamic_slice | solution.py:273
  7.0 1.5 %collective-permute-start.66 = (bf16[128,4096]{1,0:T(8,128)(2,1)}, bf16[128,4096]{1,0:T(8,128)(2,1)}, u32[]{:S(2)}, u32[]{:S(2)}) collective-permute-start(bf16[128,4096]{1,0:T(8,128)(2,1)} %constant_dynamic-slice_fusion.1), channel_id=1, source_target_pairs={{0,2},{1,3},{2,0},{3,1},{4,6},{5,7},{6,4},{7,5},{8,10},{9,11},{10,... | collective-permute-start | bytes 3145736 | tf_op jit(solution)/shard_map/ppermute | solution.py:226
  9.2 2.7 %collective-permute-start.56 = (s32[2,128]{1,0:T(2,128)S(1)}, s32[2,128]{1,0:T(2,128)S(1)}, u32[]{:S(2)}, u32[]{:S(2)}) collective-permute-start(s32[2,128]{1,0:T(2,128)S(1)} %pad_add_fusion.17), channel_id=1, source_target_pairs={{0,8},{1,9},{2,10},{3,11},{4,12},{5,13},{6,14},{7,15},{8,0},{9,1},... | collective-permute-start | bytes 3080 | tf_op jit(solution)/shard_map/ppermute | solution.py:226
  11.9 1.7 %shard_map.74 = (bf16[16,8192]{1,0:T(8,128)(2,1)S(1)}, bf16[16,8192]{1,0:T(8,128)(2,1)S(1)}, bf16[16,8192]{1,0:T(8,128)(2,1)S(1)}) custom-call(s32[3]{0:T(128)S(1)} %pad_add_fusion.18.place_ref, s32[1,128]{1,0:T(1,128)S(1)} %get-tuple-element.1423.goes_ref, s32[1,128]{1,0:T(1,128)S(1)} %bitcast.949, bf16[128,8192]{1,0:T(8,128)(2,1)S(1)} %copy-done), custom_call_target="tpu_custom_call" | custom-call | flops 100663296 | bytes 2883584 | tf_op jit(solution)/shard_map/pallas_call | solution.py:90
  13.9 2.5 %collective-permute-start.63 = (bf16[16,8192]{1,0:T(8,128)(2,1)S(1)}, bf16[16,8192]{1,0:T(8,128)(2,1)S(1)}, u32[]{:S(2)}, u32[]{:S(2)}) collective-permute-start(bf16[16,8192]{1,0:T(8,128)(2,1)S(1)} %get-tuple-element.752), channel_id=1, source_target_pairs={{0,12},{1,13},{2,14},{3,15},{4,8},{5,9},{6,10},{7,11},{8,4},{9,5},... | collective-permute-start | bytes 786440 | tf_op jit(solution)/shard_map/ppermute | solution.py:226
  16.6 1.7 %collective-permute-start.65 = (bf16[16,8192]{1,0:T(8,128)(2,1)S(1)}, bf16[16,8192]{1,0:T(8,128)(2,1)}, u32[]{:S(2)}, u32[]{:S(2)}) collective-permute-start(bf16[16,8192]{1,0:T(8,128)(2,1)S(1)} %get-tuple-element.754), channel_id=1, source_target_pairs={{0,4},{1,5},{2,6},{3,7},{4,0},{5,1},{6,2},{7,3},{8,12},{9,13},{10,... | collective-permute-start | bytes 786440 | tf_op jit(solution)/shard_map/ppermute | solution.py:226
  18.4 2.3 %constant_dynamic-slice_fusion = bf16[128,4096]{1,0:T(8,128)(2,1)} fusion(bf16[128,8192]{1,0:T(8,128)(2,1)} %collective-permute-done.58, s32[]{:T(128)S(6)} %select_n.2050), kind=kLoop, calls=%fused_computation.1335 | loop fusion | bytes 2097156 | tf_op jit(solution)/shard_map/dynamic_slice | solution.py:273
  21.2 1.4 %shard_map.75 = s32[1,128]{1,0:T(1,128)} custom-call(s32[3]{0:T(128)S(1)} %pad_add_fusion.18.place_ref, s32[4,128]{1,0:T(4,128)} %copy-done.23, s32[4,128]{1,0:T(4,128)} %copy-done.24), custom_call_target="tpu_custom_call" | custom-call | tf_op jit(solution)/shard_map/pallas_call | solution.py:43
  23.9 9.1 %collective-permute-done.61 = s32[1,128]{1,0:T(1,128)S(1)} collective-permute-done((s32[1,128]{1,0:T(1,128)}, s32[1,128]{1,0:T(1,128)S(1)}, u32[]{:S(2)}, u32[]{:S(2)}) %collective-permute-start.61) | collective-permute-done | bytes 544 | tf_op jit(solution)/shard_map/ppermute | solution.py:226
  33.6 1.5 %collective-permute-start.62 = (s32[1,128]{1,0:T(1,128)S(1)}, s32[1,128]{1,0:T(1,128)S(1)}, u32[]{:S(2)}, u32[]{:S(2)}) collective-permute-start(s32[1,128]{1,0:T(1,128)S(1)} %max.6), channel_id=1, source_target_pairs={{0,16},{16,0},{1,17},{17,1},{2,18},{18,2},{3,19},{19,3},{4,20},{20... | collective-permute-start | bytes 1544 | tf_op jit(solution)/shard_map/ppermute | solution.py:226
  35.7 1.4 %collective-permute-done.62 = s32[1,128]{1,0:T(1,128)S(1)} collective-permute-done((s32[1,128]{1,0:T(1,128)S(1)}, s32[1,128]{1,0:T(1,128)S(1)}, u32[]{:S(2)}, u32[]{:S(2)}) %collective-permute-start.62) | collective-permute-done | bytes 544 | tf_op jit(solution)/shard_map/ppermute | solution.py:226
  37.2 3.1 %collective-permute-done.64 = bf16[16,8192]{1,0:T(8,128)(2,1)S(1)} collective-permute-done((bf16[16,8192]{1,0:T(8,128)(2,1)S(1)}, bf16[16,8192]{1,0:T(8,128)(2,1)S(1)}, u32[]{:S(2)}, u32[]{:S(2)}) %collective-permute-start.64) | collective-permute-done | bytes 262176 | tf_op jit(solution)/shard_map/ppermute | solution.py:226
  40.3 58.9 %conditional.3 = (bf16[128,512]{1,0:T(8,128)(2,1)S(1)}) conditional(s32[]{:T(128)} %bitcast.187, (s32[]{:T(128)}, s32[]{:T(128)}, s32[2,128]{1,0:T(2,128)S(1)}, pred[2,128]{1,0:T(4,128)(4,1)S(1)}, pred[2,128]{1,0:T(4,128)(4,1)S(1)}, /*index=5*/s32[2,128]{1,0:T(2,128)S(1)}, s32[2,128]{1,0:T(2,128)S(1)}, ...), branch_computations={%region_2.12_spmd, %region_12.22_spmd, %region_22.32_spmd, %region... | conditional | flops 4556362752 | bytes 74956320
  40.7 3.3 %branch_1_fun.6 = (bf16[56,4096]{1,0:T(8,128)(2,1)}, bf16[56,4096]{1,0:T(8,128)(2,1)}, bf16[56,4096]{1,0:T(8,128)(2,1)}) custom-call(s32[3]{0:T(128)S(1)} %pad_add_fusion.5.place_ref, s32[2,128]{1,0:T(2,128)S(1)} %get-tuple-element.1215.goes_ref, s32[2,128]{1,0:T(2,128)S(1)} %get-tuple-element.1281.within_ref, ...), custom_call_target="tpu_custom_call" | custom-call | flops 352321536 | bytes 3473408 | tf_op jit(solution)/shard_map/cond/branch_1_fun/pallas_call | solution.py:90
  44.0 2.7 %collective-permute-start.11 = (bf16[56,4096]{1,0:T(8,128)(2,1)}, bf16[56,4096]{1,0:T(8,128)(2,1)}, u32[]{:S(2)}, u32[]{:S(2)}) collective-permute-start(bf16[56,4096]{1,0:T(8,128)(2,1)} %get-tuple-element.559), channel_id=1, source_target_pairs={{0,12},{1,13},{2,14},{3,15},{4,8},{5,9},{6,10},{7,11},{8,4},{9,5},... | collective-permute-start | bytes 1376264 | tf_op jit(solution)/shard_map/cond/branch_1_fun/ppermute | solution.py:226
  46.7 1.7 %collective-permute-start.13 = (bf16[56,4096]{1,0:T(8,128)(2,1)}, bf16[56,4096]{1,0:T(8,128)(2,1)}, u32[]{:S(2)}, u32[]{:S(2)}) collective-permute-start(bf16[56,4096]{1,0:T(8,128)(2,1)} %get-tuple-element.561), channel_id=1, source_target_pairs={{0,4},{1,5},{2,6},{3,7},{4,0},{5,1},{6,2},{7,3},{8,12},{9,13},{10,... | collective-permute-start | bytes 1376264 | tf_op jit(solution)/shard_map/cond/branch_1_fun/ppermute | solution.py:226
  48.5 1.0 constant_dynamic-update-slice_fusion.6.refs_1_
  55.2 1.3 %pad_add_fusion.3 = s32[168,1]{0,1:T(1,128)} fusion(s32[56,1]{0,1:T(1,128)} %add_bitcast_fusion.27, s32[56,1]{0,1:T(1,128)S(1)} %add_bitcast_fusion.28, s32[56,1]{0,1:T(1,128)S(1)} %add_bitcast_fusion.29), kind=kLoop, calls=%fused_computation.463 | loop fusion | flops 336 | bytes 1344 | tf_op jit(solution)/shard_map/cond/branch_1_fun/concatenate | solution.py:372
  58.3 1.6 %collective-permute-start.17 = (bf16[256,512]{1,0:T(8,128)(2,1)S(1)}, bf16[256,512]{1,0:T(8,128)(2,1)S(1)}, u32[]{:S(2)}, u32[]{:S(2)}) collective-permute-start(bf16[256,512]{1,0:T(8,128)(2,1)S(1)} %pad_maximum_fusion.1), channel_id=1, source_target_pairs={{0,2},{1,3},{2,0},{3,1},{4,6},{5,7},{6,4},{7,5},{8,10},{9,11},{10,... | collective-permute-start | bytes 786440 | tf_op jit(solution)/shard_map/cond/branch_1_fun/ppermute | solution.py:226
  59.9 4.7 %branch_1_fun.7 = f32[352,64]{1,0:T(8,128)S(1)} custom-call(s32[3]{0:T(128)S(1)} %get-tuple-element.567.place_ref, bf16[128,8192]{1,0:T(8,128)(2,1)} %copy-done.3, bf16[48,8192]{1,0:T(8,128)(2,1)S(1)} %constant_dynamic-update-slice_fusion.6.refs_1_, bf16[128,8192]{1,0:T(8,128)(2,1)} %get-tuple-element.550.refs_1_.refs_2_, ...), custom_call_target="tpu_custom_call" | custom-call | flops 1107296256 | bytes 6029312 | tf_op jit(solution)/shard_map/cond/branch_1_fun/pallas_call | solution.py:147
  64.6 4.8 %fusion.289 = f32[128,512]{1,0:T(8,128)S(1)} fusion(bf16[128,8192]{1,0:T(8,128)(2,1)S(1)} %copy-done.4, bf16[8192,512]{1,0:T(8,128)(2,1)} %get-tuple-element.794), kind=kOutput, calls=%fused_computation.1343 | convolution fusion | flops 1073741824 | bytes 10747904 | tf_op jit(solution)/shard_map/cond/branch_1_fun/dot_general | solution.py:381
  69.3 6.4 %collective-permute-done.15.refs_4_.refs_6_ = bf16[128,4096]{1,0:T(8,128)(2,1)S(1)} collective-permute-done((bf16[128,4096]{1,0:T(8,128)(2,1)}, bf16[128,4096]{1,0:T(8,128)(2,1)S(1)}, u32[]{:S(2)}, u32[]{:S(2)}) %collective-permute-start.15) | collective-permute-done | bytes 1048608 | tf_op jit(solution)/shard_map/cond/branch_1_fun/ppermute | solution.py:226
  75.8 3.0 %branch_1_fun.8 = f32[352,64]{1,0:T(8,128)S(1)} custom-call(s32[3]{0:T(128)S(1)} %get-tuple-element.567.place_ref, bf16[128,8192]{1,0:T(8,128)(2,1)S(1)} %copy-done.4, bf16[48,8192]{1,0:T(8,128)(2,1)S(1)} %constant_dynamic-update-slice_fusion.6.refs_1_, bf16[128,8192]{1,0:T(8,128)(2,1)} %get-tuple-element.550.refs_1_.refs_2_, ...), custom_call_target="tpu_custom_call" | custom-call | flops 369098752 | bytes 3932160 | tf_op jit(solution)/shard_map/cond/branch_1_fun/pallas_call | solution.py:147
  79.0 2.0 %collective-permute-done.17 = bf16[256,512]{1,0:T(8,128)(2,1)S(1)} collective-permute-done((bf16[256,512]{1,0:T(8,128)(2,1)S(1)}, bf16[256,512]{1,0:T(8,128)(2,1)S(1)}, u32[]{:S(2)}, u32[]{:S(2)}) %collective-permute-start.17) | collective-permute-done | bytes 262176 | tf_op jit(solution)/shard_map/cond/branch_1_fun/ppermute | solution.py:226
  81.0 0.9 branch_1_fun.9
  82.0 3.0 %collective-permute-done.12.refs_1_ = bf16[56,4096]{1,0:T(8,128)(2,1)} collective-permute-done((bf16[56,4096]{1,0:T(8,128)(2,1)}, bf16[56,4096]{1,0:T(8,128)(2,1)}, u32[]{:S(2)}, u32[]{:S(2)}) %collective-permute-start.12) | collective-permute-done | bytes 458784 | tf_op jit(solution)/shard_map/cond/branch_1_fun/ppermute | solution.py:226
  85.2 4.2 %branch_1_fun.10.one_ref = f32[168,64]{1,0:T(8,128)S(1)} custom-call(s32[3]{0:T(128)S(1)} %get-tuple-element.567.place_ref, bf16[56,4096]{1,0:T(8,128)(2,1)} %collective-permute-done.11.refs_0_, bf16[56,4096]{1,0:T(8,128)(2,1)} %collective-permute-done.12.refs_1_, bf16[56,4096]{1,0:T(8,128)(2,1)} %collective-permute-done.13.refs_2_, ...), custom_call_target="tpu_custom_call" | custom-call | flops 704643072 | bytes 5570560 | tf_op jit(solution)/shard_map/cond/branch_1_fun/pallas_call | solution.py:147
  89.5 1.2 %collective-permute-done.18.two_ref = f32[168,64]{1,0:T(8,128)S(1)} collective-permute-done((f32[168,64]{1,0:T(8,128)S(1)}, f32[168,64]{1,0:T(8,128)S(1)}, u32[]{:S(2)}, u32[]{:S(2)}) %collective-permute-start.18) | collective-permute-done | bytes 43040 | tf_op jit(solution)/shard_map/cond/branch_1_fun/ppermute | solution.py:226
  91.7 1.4 %collective-permute-start.19 = (bf16[48,512]{1,0:T(8,128)(2,1)S(1)}, bf16[48,512]{1,0:T(8,128)(2,1)S(1)}, u32[]{:S(2)}, u32[]{:S(2)}) collective-permute-start(bf16[48,512]{1,0:T(8,128)(2,1)S(1)} %get-tuple-element.587), channel_id=1, source_target_pairs={{0,12},{1,13},{2,14},{3,15},{4,8},{5,9},{6,10},{7,11},{8,4},{9,5},... | collective-permute-start | bytes 147464 | tf_op jit(solution)/shard_map/cond/branch_1_fun/ppermute | solution.py:226
  93.1 2.0 %collective-permute-start.21 = (bf16[48,512]{1,0:T(8,128)(2,1)S(1)}, bf16[48,512]{1,0:T(8,128)(2,1)S(1)}, u32[]{:S(2)}, u32[]{:S(2)}) collective-permute-start(bf16[48,512]{1,0:T(8,128)(2,1)S(1)} %get-tuple-element.589), channel_id=1, source_target_pairs={{0,4},{1,5},{2,6},{3,7},{4,0},{5,1},{6,2},{7,3},{8,12},{9,13},{10,... | collective-permute-start | bytes 147464 | tf_op jit(solution)/shard_map/cond/branch_1_fun/ppermute | solution.py:226
  95.2 2.8 %collective-permute-done.20 = bf16[48,512]{1,0:T(8,128)(2,1)S(1)} collective-permute-done((bf16[48,512]{1,0:T(8,128)(2,1)S(1)}, bf16[48,512]{1,0:T(8,128)(2,1)S(1)}, u32[]{:S(2)}, u32[]{:S(2)}) %collective-permute-start.20) | collective-permute-done | bytes 49184 | tf_op jit(solution)/shard_map/cond/branch_1_fun/ppermute | solution.py:226
  (111 shorter events, 15.6 us)
Async XLA Ops:
  0.0 11.9 %copy-start = (bf16[128,8192]{1,0:T(8,128)(2,1)S(1)}, bf16[128,8192]{1,0:T(8,128)(2,1)}, u32[]{:S(2)}) copy-start(bf16[128,8192]{1,0:T(8,128)(2,1)} %refs_0_.1) | copy-start | bytes 6291460
  0.0 13.8 %collective-permute-start.57 = (bf16[128,8192]{1,0:T(8,128)(2,1)}, bf16[128,8192]{1,0:T(8,128)(2,1)}, u32[]{:S(2)}, u32[]{:S(2)}) collective-permute-start(bf16[128,8192]{1,0:T(8,128)(2,1)} %refs_0_.1), channel_id=1, source_target_pairs={{0,1},{1,0},{2,3},{3,2},{4,5},{5,4},{6,7},{7,6},{8,9},{9,8},{10,11... | collective-permute-start | bytes 6291464 | tf_op jit(solution)/shard_map/ppermute | solution.py:226
  0.5 13.4 %collective-permute-start.58 = (bf16[128,8192]{1,0:T(8,128)(2,1)}, bf16[128,8192]{1,0:T(8,128)(2,1)}, u32[]{:S(2)}, u32[]{:S(2)}) collective-permute-start(bf16[128,8192]{1,0:T(8,128)(2,1)} %bitcast.956), channel_id=1, source_target_pairs={{0,1},{1,0},{2,3},{3,2},{4,5},{5,4},{6,7},{7,6},{8,9},{9,8},{10,11... | collective-permute-start | bytes 6291464 | tf_op jit(solution)/shard_map/ppermute | solution.py:226
  1.6 7.6 %collective-permute-start.55 = (s32[1,128]{1,0:T(1,128)S(1)}, s32[1,128]{1,0:T(1,128)S(1)}, u32[]{:S(2)}, u32[]{:S(2)}) collective-permute-start(s32[1,128]{1,0:T(1,128)S(1)} %get-tuple-element.1424), channel_id=1, source_target_pairs={{0,4},{1,5},{2,6},{3,7},{4,0},{5,1},{6,2},{7,3},{8,12},{9,13},{10,... | collective-permute-start | bytes 1544 | tf_op jit(solution)/shard_map/ppermute | solution.py:226
  4.7 9.1 %collective-permute-start.59 = (bf16[128,512]{1,0:T(8,128)(2,1)}, bf16[128,512]{1,0:T(8,128)(2,1)}, u32[]{:S(2)}, u32[]{:S(2)}) collective-permute-start(bf16[128,512]{1,0:T(8,128)(2,1)} %bitcast.950), channel_id=1, source_target_pairs={{0,1},{1,0},{2,3},{3,2},{4,5},{5,4},{6,7},{7,6},{8,9},{9,8},{10,11... | collective-permute-start | bytes 393224 | tf_op jit(solution)/shard_map/ppermute | solution.py:226
  7.0 30.1 %collective-permute-start.66 = (bf16[128,4096]{1,0:T(8,128)(2,1)}, bf16[128,4096]{1,0:T(8,128)(2,1)}, u32[]{:S(2)}, u32[]{:S(2)}) collective-permute-start(bf16[128,4096]{1,0:T(8,128)(2,1)} %constant_dynamic-slice_fusion.1), channel_id=1, source_target_pairs={{0,2},{1,3},{2,0},{3,1},{4,6},{5,7},{6,4},{7,5},{8,10},{9,11},{10,... | collective-permute-start | bytes 3145736 | tf_op jit(solution)/shard_map/ppermute | solution.py:226
  9.2 4.5 %collective-permute-start.56 = (s32[2,128]{1,0:T(2,128)S(1)}, s32[2,128]{1,0:T(2,128)S(1)}, u32[]{:S(2)}, u32[]{:S(2)}) collective-permute-start(s32[2,128]{1,0:T(2,128)S(1)} %pad_add_fusion.17), channel_id=1, source_target_pairs={{0,8},{1,9},{2,10},{3,11},{4,12},{5,13},{6,14},{7,15},{8,0},{9,1},... | collective-permute-start | bytes 3080 | tf_op jit(solution)/shard_map/ppermute | solution.py:226
  11.9 28.4 %copy-start.11 = (bf16[2,64,512]{2,1,0:T(8,128)(2,1)S(1)}, bf16[2,64,512]{2,1,0:T(8,128)(2,1)}, u32[]{:S(2)}) copy-start(bf16[2,64,512]{2,1,0:T(8,128)(2,1)} %param.16) | copy-start | bytes 393220
  13.8 6.9 %copy-start.23 = (s32[4,128]{1,0:T(4,128)}, s32[4,128]{1,0:T(4,128)S(1)}, u32[]{:S(2)}) copy-start(s32[4,128]{1,0:T(4,128)S(1)} %pad_add_fusion.16.mine_ref) | copy-start | bytes 6148
  13.8 6.8 %collective-permute-start.60 = (s32[4,128]{1,0:T(4,128)S(1)}, s32[4,128]{1,0:T(4,128)S(1)}, u32[]{:S(2)}, u32[]{:S(2)}) collective-permute-start(s32[4,128]{1,0:T(4,128)S(1)} %pad_add_fusion.16.mine_ref), channel_id=1, source_target_pairs={{0,1},{1,0},{2,3},{3,2},{4,5},{5,4},{6,7},{7,6},{8,9},{9,8},{10,11... | collective-permute-start | bytes 6152 | tf_op jit(solution)/shard_map/ppermute | solution.py:226
  13.9 23.3 %collective-permute-start.63 = (bf16[16,8192]{1,0:T(8,128)(2,1)S(1)}, bf16[16,8192]{1,0:T(8,128)(2,1)S(1)}, u32[]{:S(2)}, u32[]{:S(2)}) collective-permute-start(bf16[16,8192]{1,0:T(8,128)(2,1)S(1)} %get-tuple-element.752), channel_id=1, source_target_pairs={{0,12},{1,13},{2,14},{3,15},{4,8},{5,9},{6,10},{7,11},{8,4},{9,5},... | collective-permute-start | bytes 786440 | tf_op jit(solution)/shard_map/ppermute | solution.py:226
  16.4 23.9 %collective-permute-start.64 = (bf16[16,8192]{1,0:T(8,128)(2,1)S(1)}, bf16[16,8192]{1,0:T(8,128)(2,1)S(1)}, u32[]{:S(2)}, u32[]{:S(2)}) collective-permute-start(bf16[16,8192]{1,0:T(8,128)(2,1)S(1)} %get-tuple-element.753), channel_id=1, source_target_pairs={{0,8},{1,9},{2,10},{3,11},{4,12},{5,13},{6,14},{7,15},{8,0},{9,1},... | collective-permute-start | bytes 786440 | tf_op jit(solution)/shard_map/ppermute | solution.py:226
  16.6 23.7 %collective-permute-start.65 = (bf16[16,8192]{1,0:T(8,128)(2,1)S(1)}, bf16[16,8192]{1,0:T(8,128)(2,1)}, u32[]{:S(2)}, u32[]{:S(2)}) collective-permute-start(bf16[16,8192]{1,0:T(8,128)(2,1)S(1)} %get-tuple-element.754), channel_id=1, source_target_pairs={{0,4},{1,5},{2,6},{3,7},{4,0},{5,1},{6,2},{7,3},{8,12},{9,13},{10,... | collective-permute-start | bytes 786440 | tf_op jit(solution)/shard_map/ppermute | solution.py:226
  22.7 10.3 %collective-permute-start.61 = (s32[1,128]{1,0:T(1,128)}, s32[1,128]{1,0:T(1,128)S(1)}, u32[]{:S(2)}, u32[]{:S(2)}) collective-permute-start(s32[1,128]{1,0:T(1,128)} %shard_map.75), channel_id=1, source_target_pairs={{0,2},{1,3},{2,0},{3,1},{4,6},{5,7},{6,4},{7,5},{8,10},{9,11},{10,... | collective-permute-start | bytes 1544 | tf_op jit(solution)/shard_map/ppermute | solution.py:226
  33.6 3.5 %collective-permute-start.62 = (s32[1,128]{1,0:T(1,128)S(1)}, s32[1,128]{1,0:T(1,128)S(1)}, u32[]{:S(2)}, u32[]{:S(2)}) collective-permute-start(s32[1,128]{1,0:T(1,128)S(1)} %max.6), channel_id=1, source_target_pairs={{0,16},{16,0},{1,17},{17,1},{2,18},{18,2},{3,19},{19,3},{4,20},{20... | collective-permute-start | bytes 1544 | tf_op jit(solution)/shard_map/ppermute | solution.py:226
  40.5 3.5 %copy-start.3 = (bf16[128,8192]{1,0:T(8,128)(2,1)}, bf16[128,8192]{1,0:T(8,128)(2,1)S(1)}, u32[]{:S(2)}) copy-start(bf16[128,8192]{1,0:T(8,128)(2,1)S(1)} %get-tuple-element.574.refs_0_) | copy-start | bytes 6291460 | tf_op jit(solution)/shard_map/conditional.1
  40.5 3.5 %copy-start.14 = (s32[2,128]{1,0:T(2,128)}, s32[2,128]{1,0:T(2,128)S(1)}, u32[]{:S(2)}) copy-start(s32[2,128]{1,0:T(2,128)S(1)} %get-tuple-element.1193) | copy-start | bytes 3076 | tf_op jit(solution)/shard_map/conditional.1
  40.7 9.4 %copy-start.31 = (s32[2]{0:T(128)S(1)}, s32[2]{0:T(128)}, u32[]{:S(2)}) copy-start(s32[2]{0:T(128)} %get-tuple-element.563) | copy-start | bytes 28 | tf_op jit(solution)/shard_map/conditional.1
  44.0 38.0 %collective-permute-start.11 = (bf16[56,4096]{1,0:T(8,128)(2,1)}, bf16[56,4096]{1,0:T(8,128)(2,1)}, u32[]{:S(2)}, u32[]{:S(2)}) collective-permute-start(bf16[56,4096]{1,0:T(8,128)(2,1)} %get-tuple-element.559), channel_id=1, source_target_pairs={{0,12},{1,13},{2,14},{3,15},{4,8},{5,9},{6,10},{7,11},{8,4},{9,5},... | collective-permute-start | bytes 1376264 | tf_op jit(solution)/shard_map/cond/branch_1_fun/ppermute | solution.py:226
  46.7 38.3 %collective-permute-start.12 = (bf16[56,4096]{1,0:T(8,128)(2,1)}, bf16[56,4096]{1,0:T(8,128)(2,1)}, u32[]{:S(2)}, u32[]{:S(2)}) collective-permute-start(bf16[56,4096]{1,0:T(8,128)(2,1)} %get-tuple-element.560), channel_id=1, source_target_pairs={{0,8},{1,9},{2,10},{3,11},{4,12},{5,13},{6,14},{7,15},{8,0},{9,1},... | collective-permute-start | bytes 1376264 | tf_op jit(solution)/shard_map/cond/branch_1_fun/ppermute | solution.py:226
  46.7 38.3 %collective-permute-start.13 = (bf16[56,4096]{1,0:T(8,128)(2,1)}, bf16[56,4096]{1,0:T(8,128)(2,1)}, u32[]{:S(2)}, u32[]{:S(2)}) collective-permute-start(bf16[56,4096]{1,0:T(8,128)(2,1)} %get-tuple-element.561), channel_id=1, source_target_pairs={{0,4},{1,5},{2,6},{3,7},{4,0},{5,1},{6,2},{7,3},{8,12},{9,13},{10,... | collective-permute-start | bytes 1376264 | tf_op jit(solution)/shard_map/cond/branch_1_fun/ppermute | solution.py:226
  49.5 8.9 %collective-permute-start.14 = (bf16[48,8192]{1,0:T(8,128)(2,1)S(1)}, bf16[48,8192]{1,0:T(8,128)(2,1)S(1)}, u32[]{:S(2)}, u32[]{:S(2)}) collective-permute-start(bf16[48,8192]{1,0:T(8,128)(2,1)S(1)} %constant_dynamic-update-slice_fusion.6.refs_1_), channel_id=1, source_target_pairs={{0,1},{1,0},{2,3},{3,2},{4,5},{5,4},{6,7},{7,6},{8,9},{9,8},{10,11... | collective-permute-start | bytes 2359304 | tf_op jit(solution)/shard_map/cond/branch_1_fun/ppermute | solution.py:226
  49.5 26.2 %collective-permute-start.15 = (bf16[128,4096]{1,0:T(8,128)(2,1)}, bf16[128,4096]{1,0:T(8,128)(2,1)S(1)}, u32[]{:S(2)}, u32[]{:S(2)}) collective-permute-start(bf16[128,4096]{1,0:T(8,128)(2,1)} %get-tuple-element.572.refs_5_.refs_4_), channel_id=1, source_target_pairs={{0,2},{1,3},{2,0},{3,1},{4,6},{5,7},{6,4},{7,5},{8,10},{9,11},{10,... | collective-permute-start | bytes 3145736 | tf_op jit(solution)/shard_map/cond/branch_1_fun/ppermute | solution.py:226
  58.3 22.6 %collective-permute-start.17 = (bf16[256,512]{1,0:T(8,128)(2,1)S(1)}, bf16[256,512]{1,0:T(8,128)(2,1)S(1)}, u32[]{:S(2)}, u32[]{:S(2)}) collective-permute-start(bf16[256,512]{1,0:T(8,128)(2,1)S(1)} %pad_maximum_fusion.1), channel_id=1, source_target_pairs={{0,2},{1,3},{2,0},{3,1},{4,6},{5,7},{6,4},{7,5},{8,10},{9,11},{10,... | collective-permute-start | bytes 786440 | tf_op jit(solution)/shard_map/cond/branch_1_fun/ppermute | solution.py:226
  59.9 4.7 %copy-start.4 = (bf16[128,8192]{1,0:T(8,128)(2,1)S(1)}, bf16[128,8192]{1,0:T(8,128)(2,1)}, u32[]{:S(2)}) copy-start(bf16[128,8192]{1,0:T(8,128)(2,1)} %copy-done.3) | copy-start | bytes 6291460 | tf_op jit(solution)/shard_map/conditional.1
  78.8 6.2 %copy-start.27 = (s32[168,1]{0,1:T(1,128)S(1)}, s32[168,1]{0,1:T(1,128)}, u32[]{:S(2)}) copy-start(s32[168,1]{0,1:T(1,128)} %pad_add_fusion.3) | copy-start | bytes 2020 | tf_op jit(solution)/shard_map/conditional.1
  78.9 2.1 %collective-permute-start.16 = (f32[176,64]{1,0:T(8,128)S(1)}, f32[176,64]{1,0:T(8,128)S(1)}, u32[]{:S(2)}, u32[]{:S(2)}) collective-permute-start(f32[176,64]{1,0:T(8,128)S(1)} %get-tuple-element.1267), channel_id=1, source_target_pairs={{0,1},{1,0},{2,3},{3,2},{4,5},{5,4},{6,7},{7,6},{8,9},{9,8},{10,11... | collective-permute-start | bytes 135176 | tf_op jit(solution)/shard_map/cond/branch_1_fun/ppermute | solution.py:226
  85.1 4.3 %copy-start.15 = (s32[2,128]{1,0:T(2,128)S(1)}, s32[2,128]{1,0:T(2,128)}, u32[]{:S(2)}) copy-start(s32[2,128]{1,0:T(2,128)} %copy-done.14) | copy-start | bytes 3076 | tf_op jit(solution)/shard_map/conditional.1
  89.4 1.3 %collective-permute-start.18 = (f32[168,64]{1,0:T(8,128)S(1)}, f32[168,64]{1,0:T(8,128)S(1)}, u32[]{:S(2)}, u32[]{:S(2)}) collective-permute-start(f32[168,64]{1,0:T(8,128)S(1)} %branch_1_fun.10.one_ref), channel_id=1, source_target_pairs={{0,1},{1,0},{2,3},{3,2},{4,5},{5,4},{6,7},{7,6},{8,9},{9,8},{10,11... | collective-permute-start | bytes 129032 | tf_op jit(solution)/shard_map/cond/branch_1_fun/ppermute | solution.py:226
  91.6 6.4 %collective-permute-start.20 = (bf16[48,512]{1,0:T(8,128)(2,1)S(1)}, bf16[48,512]{1,0:T(8,128)(2,1)S(1)}, u32[]{:S(2)}, u32[]{:S(2)}) collective-permute-start(bf16[48,512]{1,0:T(8,128)(2,1)S(1)} %get-tuple-element.588), channel_id=1, source_target_pairs={{0,8},{1,9},{2,10},{3,11},{4,12},{5,13},{6,14},{7,15},{8,0},{9,1},... | collective-permute-start | bytes 147464 | tf_op jit(solution)/shard_map/cond/branch_1_fun/ppermute | solution.py:226
  91.7 6.5 %collective-permute-start.19 = (bf16[48,512]{1,0:T(8,128)(2,1)S(1)}, bf16[48,512]{1,0:T(8,128)(2,1)S(1)}, u32[]{:S(2)}, u32[]{:S(2)}) collective-permute-start(bf16[48,512]{1,0:T(8,128)(2,1)S(1)} %get-tuple-element.587), channel_id=1, source_target_pairs={{0,12},{1,13},{2,14},{3,15},{4,8},{5,9},{6,10},{7,11},{8,4},{9,5},... | collective-permute-start | bytes 147464 | tf_op jit(solution)/shard_map/cond/branch_1_fun/ppermute | solution.py:226
  93.1 5.4 %collective-permute-start.21 = (bf16[48,512]{1,0:T(8,128)(2,1)S(1)}, bf16[48,512]{1,0:T(8,128)(2,1)S(1)}, u32[]{:S(2)}, u32[]{:S(2)}) collective-permute-start(bf16[48,512]{1,0:T(8,128)(2,1)S(1)} %get-tuple-element.589), channel_id=1, source_target_pairs={{0,4},{1,5},{2,6},{3,7},{4,0},{5,1},{6,2},{7,3},{8,12},{9,13},{10,... | collective-permute-start | bytes 147464 | tf_op jit(solution)/shard_map/cond/branch_1_fun/ppermute | solution.py:226
  (2 other events, 1.2 us)

commit v6 on v5

--- a/solution.py
+++ b/solution.py
@@ -250,7 +250,7 @@
             (2 * cap * chip // 16 - 2 * first, cap * device // 8 - first)
             for chip, device in ((10, 6), (11, 6), (12, 6), (13, 7), (16, 8))
         ]
-        flips = sorted(range(1, planes), key=lambda k: -k)
+        flips = sorted(range(1, planes), key=lambda k: (k == 1, k))
         half = width // 2
 
         me = lax.axis_index("own")

time: 100 us -> 99.2 us (level); the launches traced: 99.9 us -> 100 us
  starting transfers between devices: 24.7 us -> 29.3 us
  waiting for transfers between devices: 29.3 us -> 24.9 us
    ppermute x23, starting transfers between devices: 24.7 us -> 29.3 us  [flipped(): return lax.ppermute(x, axis, [(i, i ^ flip) for i in range(size)])]
    ppermute x23, waiting for transfers between devices: 29.3 us -> 24.9 us  [flipped(): return lax.ppermute(x, axis, [(i, i ^ flip) for i in range(size)])]
  transfers between devices with their start and end apart: 23 -> 23, of which waited for: 9 -> 7; matrix products, arithmetic and copies ran while one was open for 22% -> 22% of each run, Pallas kernels for 12% -> 12%
where the time goes in v6:
time: 99.2 us; the launch traced here: 100 us
  starting transfers between devices  29.3 us (30%)
  waiting for transfers between devices  24.9 us (25%)
  Pallas kernels  20.1 us (20%)
  other arithmetic  10.2 us (10%)
  local copies, waits for them, and re-layouts  8.37 us (8%)
  matrix products  5.44 us (5%)
  loops' own time  1.68 us (2%)
    ppermute x23, starting transfers between devices, flipped(): return lax.ppermute(x, axis, [(i, i ^ flip) for i in range(size)])  29.3 us
    ppermute x23, waiting for transfers between devices, flipped(): return lax.ppermute(x, axis, [(i, i ^ flip) for i in range(size)])  24.9 us
    pallas_call x3, Pallas kernels, shrink(): pl.pallas_call(functools.partial(shrink_body, len(xs), len(ws), rank, sta...  11.9 us
    pallas_call x2, Pallas kernels, pack(): pl.pallas_call(functools.partial(pack_body, flips, number, start), grid_s...  4.99 us
    dot_general x1, matrix products, branch(): base = jnp.dot(tokens, matrix, preferred_element_type=jnp.float32)  4.77 us
    dynamic_slice x2, local copies, waits for them, and re-layouts, local(): half_of = lambda x, c: lax.dynamic_slice_in_dim(x, c * half, half, axis=1)  4.67 us
    reduce_sum x8, other arithmetic, named_by(): jnp.sum(jnp.where(hot, column.reshape(1, -1) + 1, 0), 1, keepdims=True) - 1  2.11 us
  transfers between devices with their start and end apart: 23, of which 7 were waited for; matrix products, arithmetic and copies ran while one was open for 22% of the time, Pallas kernels for 12%

profile of v6, /device:TPU:0, one launch (start us, length us, event | category | flops | bytes accessed | tf_op | source)
XLA Modules:
  0.0 100.3 jit_solution(3402703922286290700)
XLA Ops:
  1.6 3.1 %collective-permute-start.55 = (s32[1,128]{1,0:T(1,128)S(1)}, s32[1,128]{1,0:T(1,128)S(1)}, u32[]{:S(2)}, u32[]{:S(2)}) collective-permute-start(s32[1,128]{1,0:T(1,128)S(1)} %get-tuple-element.1424), channel_id=1, source_target_pairs={{0,4},{1,5},{2,6},{3,7},{4,0},{5,1},{6,2},{7,3},{8,12},{9,13},{10,... | collective-permute-start | bytes 1544 | tf_op jit(solution)/shard_map/ppermute | solution.py:226
  4.7 2.4 %constant_dynamic-slice_fusion.1 = bf16[128,4096]{1,0:T(8,128)(2,1)} fusion(bf16[128,8192]{1,0:T(8,128)(2,1)} %bitcast.957, s32[]{:T(128)S(6)} %select_n.2050), kind=kLoop, calls=%fused_computation.1336 | loop fusion | bytes 2097156 | tf_op jit(solution)/shard_map/dynamic_slice | solution.py:273
  7.0 1.5 %collective-permute-start.66 = (bf16[128,4096]{1,0:T(8,128)(2,1)}, bf16[128,4096]{1,0:T(8,128)(2,1)}, u32[]{:S(2)}, u32[]{:S(2)}) collective-permute-start(bf16[128,4096]{1,0:T(8,128)(2,1)} %constant_dynamic-slice_fusion.1), channel_id=1, source_target_pairs={{0,2},{1,3},{2,0},{3,1},{4,6},{5,7},{6,4},{7,5},{8,10},{9,11},{10,... | collective-permute-start | bytes 3145736 | tf_op jit(solution)/shard_map/ppermute | solution.py:226
  9.2 2.7 %collective-permute-start.56 = (s32[2,128]{1,0:T(2,128)S(1)}, s32[2,128]{1,0:T(2,128)S(1)}, u32[]{:S(2)}, u32[]{:S(2)}) collective-permute-start(s32[2,128]{1,0:T(2,128)S(1)} %pad_add_fusion.17), channel_id=1, source_target_pairs={{0,8},{1,9},{2,10},{3,11},{4,12},{5,13},{6,14},{7,15},{8,0},{9,1},... | collective-permute-start | bytes 3080 | tf_op jit(solution)/shard_map/ppermute | solution.py:226
  11.9 1.7 %shard_map.74 = (bf16[16,8192]{1,0:T(8,128)(2,1)S(1)}, bf16[16,8192]{1,0:T(8,128)(2,1)S(1)}, bf16[16,8192]{1,0:T(8,128)(2,1)S(1)}) custom-call(s32[3]{0:T(128)S(1)} %pad_add_fusion.18.place_ref, s32[1,128]{1,0:T(1,128)S(1)} %get-tuple-element.1423.goes_ref, s32[1,128]{1,0:T(1,128)S(1)} %bitcast.949, bf16[128,8192]{1,0:T(8,128)(2,1)S(1)} %copy-done), custom_call_target="tpu_custom_call" | custom-call | flops 100663296 | bytes 2883584 | tf_op jit(solution)/shard_map/pallas_call | solution.py:90
  13.9 2.7 %collective-permute-start.63 = (bf16[16,8192]{1,0:T(8,128)(2,1)S(1)}, bf16[16,8192]{1,0:T(8,128)(2,1)S(1)}, u32[]{:S(2)}, u32[]{:S(2)}) collective-permute-start(bf16[16,8192]{1,0:T(8,128)(2,1)S(1)} %get-tuple-element.752), channel_id=1, source_target_pairs={{0,8},{1,9},{2,10},{3,11},{4,12},{5,13},{6,14},{7,15},{8,0},{9,1},... | collective-permute-start | bytes 786440 | tf_op jit(solution)/shard_map/ppermute | solution.py:226
  17.5 2.3 %constant_dynamic-slice_fusion = bf16[128,4096]{1,0:T(8,128)(2,1)} fusion(bf16[128,8192]{1,0:T(8,128)(2,1)} %collective-permute-done.58, s32[]{:T(128)S(6)} %select_n.2050), kind=kLoop, calls=%fused_computation.1335 | loop fusion | bytes 2097156 | tf_op jit(solution)/shard_map/dynamic_slice | solution.py:273
  20.3 1.4 %shard_map.75 = s32[1,128]{1,0:T(1,128)} custom-call(s32[3]{0:T(128)S(1)} %pad_add_fusion.18.place_ref, s32[4,128]{1,0:T(4,128)} %copy-done.23, s32[4,128]{1,0:T(4,128)} %copy-done.24), custom_call_target="tpu_custom_call" | custom-call | tf_op jit(solution)/shard_map/pallas_call | solution.py:43
  23.0 10.0 %collective-permute-done.61 = s32[1,128]{1,0:T(1,128)S(1)} collective-permute-done((s32[1,128]{1,0:T(1,128)}, s32[1,128]{1,0:T(1,128)S(1)}, u32[]{:S(2)}, u32[]{:S(2)}) %collective-permute-start.61) | collective-permute-done | bytes 544 | tf_op jit(solution)/shard_map/ppermute | solution.py:226
  33.6 1.5 %collective-permute-start.62 = (s32[1,128]{1,0:T(1,128)S(1)}, s32[1,128]{1,0:T(1,128)S(1)}, u32[]{:S(2)}, u32[]{:S(2)}) collective-permute-start(s32[1,128]{1,0:T(1,128)S(1)} %max.6), channel_id=1, source_target_pairs={{0,16},{16,0},{1,17},{17,1},{2,18},{18,2},{3,19},{19,3},{4,20},{20... | collective-permute-start | bytes 1544 | tf_op jit(solution)/shard_map/ppermute | solution.py:226
  35.7 1.4 %collective-permute-done.62 = s32[1,128]{1,0:T(1,128)S(1)} collective-permute-done((s32[1,128]{1,0:T(1,128)S(1)}, s32[1,128]{1,0:T(1,128)S(1)}, u32[]{:S(2)}, u32[]{:S(2)}) %collective-permute-start.62) | collective-permute-done | bytes 544 | tf_op jit(solution)/shard_map/ppermute | solution.py:226
  37.2 62.4 %conditional.3 = (bf16[128,512]{1,0:T(8,128)(2,1)S(1)}) conditional(s32[]{:T(128)} %bitcast.187, (s32[]{:T(128)}, s32[]{:T(128)}, s32[2,128]{1,0:T(2,128)S(1)}, pred[2,128]{1,0:T(4,128)(4,1)S(1)}, pred[2,128]{1,0:T(4,128)(4,1)S(1)}, /*index=5*/s32[2,128]{1,0:T(2,128)S(1)}, s32[2,128]{1,0:T(2,128)S(1)}, ...), branch_computations={%region_2.12_spmd, %region_12.22_spmd, %region_22.32_spmd, %region... | conditional | flops 4556362752 | bytes 74956320
  37.6 3.3 %branch_1_fun.6 = (bf16[56,4096]{1,0:T(8,128)(2,1)}, bf16[56,4096]{1,0:T(8,128)(2,1)}, bf16[56,4096]{1,0:T(8,128)(2,1)}) custom-call(s32[3]{0:T(128)S(1)} %pad_add_fusion.5.place_ref, s32[2,128]{1,0:T(2,128)S(1)} %get-tuple-element.1215.goes_ref, s32[2,128]{1,0:T(2,128)S(1)} %get-tuple-element.1281.within_ref, ...), custom_call_target="tpu_custom_call" | custom-call | flops 352321536 | bytes 3473408 | tf_op jit(solution)/shard_map/cond/branch_1_fun/pallas_call | solution.py:90
  40.9 4.9 %collective-permute-start.11 = (bf16[56,4096]{1,0:T(8,128)(2,1)}, bf16[56,4096]{1,0:T(8,128)(2,1)}, u32[]{:S(2)}, u32[]{:S(2)}) collective-permute-start(bf16[56,4096]{1,0:T(8,128)(2,1)} %get-tuple-element.559), channel_id=1, source_target_pairs={{0,8},{1,9},{2,10},{3,11},{4,12},{5,13},{6,14},{7,15},{8,0},{9,1},... | collective-permute-start | bytes 1376264 | tf_op jit(solution)/shard_map/cond/branch_1_fun/ppermute | solution.py:226
  45.7 1.2 %collective-permute-start.12 = (bf16[56,4096]{1,0:T(8,128)(2,1)}, bf16[56,4096]{1,0:T(8,128)(2,1)}, u32[]{:S(2)}, u32[]{:S(2)}) collective-permute-start(bf16[56,4096]{1,0:T(8,128)(2,1)} %get-tuple-element.560), channel_id=1, source_target_pairs={{0,12},{1,13},{2,14},{3,15},{4,8},{5,9},{6,10},{7,11},{8,4},{9,5},... | collective-permute-start | bytes 1376264 | tf_op jit(solution)/shard_map/cond/branch_1_fun/ppermute | solution.py:226
  47.0 1.0 constant_dynamic-update-slice_fusion.6.refs_1_
  53.7 1.3 %pad_add_fusion.3 = s32[168,1]{0,1:T(1,128)} fusion(s32[56,1]{0,1:T(1,128)} %add_bitcast_fusion.27, s32[56,1]{0,1:T(1,128)S(1)} %add_bitcast_fusion.28, s32[56,1]{0,1:T(1,128)S(1)} %add_bitcast_fusion.29), kind=kLoop, calls=%fused_computation.463 | loop fusion | flops 336 | bytes 1344 | tf_op jit(solution)/shard_map/cond/branch_1_fun/concatenate | solution.py:372
  54.9 0.9 constant_dynamic-update-slice_fusion.10
  55.9 0.9 pad_maximum_fusion.1
  56.8 1.7 %collective-permute-start.17 = (bf16[256,512]{1,0:T(8,128)(2,1)S(1)}, bf16[256,512]{1,0:T(8,128)(2,1)S(1)}, u32[]{:S(2)}, u32[]{:S(2)}) collective-permute-start(bf16[256,512]{1,0:T(8,128)(2,1)S(1)} %pad_maximum_fusion.1), channel_id=1, source_target_pairs={{0,2},{1,3},{2,0},{3,1},{4,6},{5,7},{6,4},{7,5},{8,10},{9,11},{10,... | collective-permute-start | bytes 786440 | tf_op jit(solution)/shard_map/cond/branch_1_fun/ppermute | solution.py:226
  58.5 4.7 %branch_1_fun.7 = f32[352,64]{1,0:T(8,128)S(1)} custom-call(s32[3]{0:T(128)S(1)} %get-tuple-element.567.place_ref, bf16[128,8192]{1,0:T(8,128)(2,1)} %copy-done.3, bf16[48,8192]{1,0:T(8,128)(2,1)S(1)} %constant_dynamic-update-slice_fusion.6.refs_1_, bf16[128,8192]{1,0:T(8,128)(2,1)} %get-tuple-element.550.refs_1_.refs_2_, ...), custom_call_target="tpu_custom_call" | custom-call | flops 1107296256 | bytes 6029312 | tf_op jit(solution)/shard_map/cond/branch_1_fun/pallas_call | solution.py:147
  63.1 4.8 %fusion.289 = f32[128,512]{1,0:T(8,128)S(1)} fusion(bf16[128,8192]{1,0:T(8,128)(2,1)S(1)} %copy-done.4, bf16[8192,512]{1,0:T(8,128)(2,1)} %get-tuple-element.794), kind=kOutput, calls=%fused_computation.1343 | convolution fusion | flops 1073741824 | bytes 10747904 | tf_op jit(solution)/shard_map/cond/branch_1_fun/dot_general | solution.py:381
  67.9 6.4 %collective-permute-done.15.refs_4_.refs_6_ = bf16[128,4096]{1,0:T(8,128)(2,1)S(1)} collective-permute-done((bf16[128,4096]{1,0:T(8,128)(2,1)}, bf16[128,4096]{1,0:T(8,128)(2,1)S(1)}, u32[]{:S(2)}, u32[]{:S(2)}) %collective-permute-start.15) | collective-permute-done | bytes 1048608 | tf_op jit(solution)/shard_map/cond/branch_1_fun/ppermute | solution.py:226
  74.3 3.0 %branch_1_fun.8 = f32[352,64]{1,0:T(8,128)S(1)} custom-call(s32[3]{0:T(128)S(1)} %get-tuple-element.567.place_ref, bf16[128,8192]{1,0:T(8,128)(2,1)S(1)} %copy-done.4, bf16[48,8192]{1,0:T(8,128)(2,1)S(1)} %constant_dynamic-update-slice_fusion.6.refs_1_, bf16[128,8192]{1,0:T(8,128)(2,1)} %get-tuple-element.550.refs_1_.refs_2_, ...), custom_call_target="tpu_custom_call" | custom-call | flops 369098752 | bytes 3932160 | tf_op jit(solution)/shard_map/cond/branch_1_fun/pallas_call | solution.py:147
  77.5 2.0 %collective-permute-done.17 = bf16[256,512]{1,0:T(8,128)(2,1)S(1)} collective-permute-done((bf16[256,512]{1,0:T(8,128)(2,1)S(1)}, bf16[256,512]{1,0:T(8,128)(2,1)S(1)}, u32[]{:S(2)}, u32[]{:S(2)}) %collective-permute-start.17) | collective-permute-done | bytes 262176 | tf_op jit(solution)/shard_map/cond/branch_1_fun/ppermute | solution.py:226
  79.5 0.9 branch_1_fun.9
  80.7 4.2 %branch_1_fun.10.one_ref = f32[168,64]{1,0:T(8,128)S(1)} custom-call(s32[3]{0:T(128)S(1)} %get-tuple-element.567.place_ref, bf16[56,4096]{1,0:T(8,128)(2,1)} %collective-permute-done.11.refs_0_, bf16[56,4096]{1,0:T(8,128)(2,1)} %collective-permute-done.12.refs_1_, bf16[56,4096]{1,0:T(8,128)(2,1)} %collective-permute-done.13.refs_2_, ...), custom_call_target="tpu_custom_call" | custom-call | flops 704643072 | bytes 5570560 | tf_op jit(solution)/shard_map/cond/branch_1_fun/pallas_call | solution.py:147
  85.0 1.2 %collective-permute-done.18.two_ref = f32[168,64]{1,0:T(8,128)S(1)} collective-permute-done((f32[168,64]{1,0:T(8,128)S(1)}, f32[168,64]{1,0:T(8,128)S(1)}, u32[]{:S(2)}, u32[]{:S(2)}) %collective-permute-start.18) | collective-permute-done | bytes 43040 | tf_op jit(solution)/shard_map/cond/branch_1_fun/ppermute | solution.py:226
  86.3 0.9 branch_1_fun.11
  87.1 2.7 %collective-permute-start.20 = (bf16[48,512]{1,0:T(8,128)(2,1)S(1)}, bf16[48,512]{1,0:T(8,128)(2,1)S(1)}, u32[]{:S(2)}, u32[]{:S(2)}) collective-permute-start(bf16[48,512]{1,0:T(8,128)(2,1)S(1)} %get-tuple-element.588), channel_id=1, source_target_pairs={{0,12},{1,13},{2,14},{3,15},{4,8},{5,9},{6,10},{7,11},{8,4},{9,5},... | collective-permute-start | bytes 147464 | tf_op jit(solution)/shard_map/cond/branch_1_fun/ppermute | solution.py:226
  89.8 4.8 %collective-permute-start.19 = (bf16[48,512]{1,0:T(8,128)(2,1)S(1)}, bf16[48,512]{1,0:T(8,128)(2,1)S(1)}, u32[]{:S(2)}, u32[]{:S(2)}) collective-permute-start(bf16[48,512]{1,0:T(8,128)(2,1)S(1)} %get-tuple-element.587), channel_id=1, source_target_pairs={{0,8},{1,9},{2,10},{3,11},{4,12},{5,13},{6,14},{7,15},{8,0},{9,1},... | collective-permute-start | bytes 147464 | tf_op jit(solution)/shard_map/cond/branch_1_fun/ppermute | solution.py:226
  94.9 3.7 %collective-permute-done.19 = bf16[48,512]{1,0:T(8,128)(2,1)S(1)} collective-permute-done((bf16[48,512]{1,0:T(8,128)(2,1)S(1)}, bf16[48,512]{1,0:T(8,128)(2,1)S(1)}, u32[]{:S(2)}, u32[]{:S(2)}) %collective-permute-start.19) | collective-permute-done | bytes 49184 | tf_op jit(solution)/shard_map/cond/branch_1_fun/ppermute | solution.py:226
  (111 shorter events, 13.4 us)
Async XLA Ops:
  0.0 11.9 %copy-start = (bf16[128,8192]{1,0:T(8,128)(2,1)S(1)}, bf16[128,8192]{1,0:T(8,128)(2,1)}, u32[]{:S(2)}) copy-start(bf16[128,8192]{1,0:T(8,128)(2,1)} %refs_0_.1) | copy-start | bytes 6291460
  0.0 13.8 %collective-permute-start.57 = (bf16[128,8192]{1,0:T(8,128)(2,1)}, bf16[128,8192]{1,0:T(8,128)(2,1)}, u32[]{:S(2)}, u32[]{:S(2)}) collective-permute-start(bf16[128,8192]{1,0:T(8,128)(2,1)} %refs_0_.1), channel_id=1, source_target_pairs={{0,1},{1,0},{2,3},{3,2},{4,5},{5,4},{6,7},{7,6},{8,9},{9,8},{10,11... | collective-permute-start | bytes 6291464 | tf_op jit(solution)/shard_map/ppermute | solution.py:226
  0.5 13.4 %collective-permute-start.58 = (bf16[128,8192]{1,0:T(8,128)(2,1)}, bf16[128,8192]{1,0:T(8,128)(2,1)}, u32[]{:S(2)}, u32[]{:S(2)}) collective-permute-start(bf16[128,8192]{1,0:T(8,128)(2,1)} %bitcast.956), channel_id=1, source_target_pairs={{0,1},{1,0},{2,3},{3,2},{4,5},{5,4},{6,7},{7,6},{8,9},{9,8},{10,11... | collective-permute-start | bytes 6291464 | tf_op jit(solution)/shard_map/ppermute | solution.py:226
  1.6 7.6 %collective-permute-start.55 = (s32[1,128]{1,0:T(1,128)S(1)}, s32[1,128]{1,0:T(1,128)S(1)}, u32[]{:S(2)}, u32[]{:S(2)}) collective-permute-start(s32[1,128]{1,0:T(1,128)S(1)} %get-tuple-element.1424), channel_id=1, source_target_pairs={{0,4},{1,5},{2,6},{3,7},{4,0},{5,1},{6,2},{7,3},{8,12},{9,13},{10,... | collective-permute-start | bytes 1544 | tf_op jit(solution)/shard_map/ppermute | solution.py:226
  4.7 9.1 %collective-permute-start.59 = (bf16[128,512]{1,0:T(8,128)(2,1)}, bf16[128,512]{1,0:T(8,128)(2,1)}, u32[]{:S(2)}, u32[]{:S(2)}) collective-permute-start(bf16[128,512]{1,0:T(8,128)(2,1)} %bitcast.950), channel_id=1, source_target_pairs={{0,1},{1,0},{2,3},{3,2},{4,5},{5,4},{6,7},{7,6},{8,9},{9,8},{10,11... | collective-permute-start | bytes 393224 | tf_op jit(solution)/shard_map/ppermute | solution.py:226
  7.0 30.1 %collective-permute-start.66 = (bf16[128,4096]{1,0:T(8,128)(2,1)}, bf16[128,4096]{1,0:T(8,128)(2,1)}, u32[]{:S(2)}, u32[]{:S(2)}) collective-permute-start(bf16[128,4096]{1,0:T(8,128)(2,1)} %constant_dynamic-slice_fusion.1), channel_id=1, source_target_pairs={{0,2},{1,3},{2,0},{3,1},{4,6},{5,7},{6,4},{7,5},{8,10},{9,11},{10,... | collective-permute-start | bytes 3145736 | tf_op jit(solution)/shard_map/ppermute | solution.py:226
  9.2 4.5 %collective-permute-start.56 = (s32[2,128]{1,0:T(2,128)S(1)}, s32[2,128]{1,0:T(2,128)S(1)}, u32[]{:S(2)}, u32[]{:S(2)}) collective-permute-start(s32[2,128]{1,0:T(2,128)S(1)} %pad_add_fusion.17), channel_id=1, source_target_pairs={{0,8},{1,9},{2,10},{3,11},{4,12},{5,13},{6,14},{7,15},{8,0},{9,1},... | collective-permute-start | bytes 3080 | tf_op jit(solution)/shard_map/ppermute | solution.py:226
  11.9 25.3 %copy-start.11 = (bf16[2,64,512]{2,1,0:T(8,128)(2,1)S(1)}, bf16[2,64,512]{2,1,0:T(8,128)(2,1)}, u32[]{:S(2)}) copy-start(bf16[2,64,512]{2,1,0:T(8,128)(2,1)} %param.16) | copy-start | bytes 393220
  13.8 6.0 %copy-start.23 = (s32[4,128]{1,0:T(4,128)}, s32[4,128]{1,0:T(4,128)S(1)}, u32[]{:S(2)}) copy-start(s32[4,128]{1,0:T(4,128)S(1)} %pad_add_fusion.16.mine_ref) | copy-start | bytes 6148
  13.8 5.9 %collective-permute-start.60 = (s32[4,128]{1,0:T(4,128)S(1)}, s32[4,128]{1,0:T(4,128)S(1)}, u32[]{:S(2)}, u32[]{:S(2)}) collective-permute-start(s32[4,128]{1,0:T(4,128)S(1)} %pad_add_fusion.16.mine_ref), channel_id=1, source_target_pairs={{0,1},{1,0},{2,3},{3,2},{4,5},{5,4},{6,7},{7,6},{8,9},{9,8},{10,11... | collective-permute-start | bytes 6152 | tf_op jit(solution)/shard_map/ppermute | solution.py:226
  13.9 23.3 %collective-permute-start.63 = (bf16[16,8192]{1,0:T(8,128)(2,1)S(1)}, bf16[16,8192]{1,0:T(8,128)(2,1)S(1)}, u32[]{:S(2)}, u32[]{:S(2)}) collective-permute-start(bf16[16,8192]{1,0:T(8,128)(2,1)S(1)} %get-tuple-element.752), channel_id=1, source_target_pairs={{0,8},{1,9},{2,10},{3,11},{4,12},{5,13},{6,14},{7,15},{8,0},{9,1},... | collective-permute-start | bytes 786440 | tf_op jit(solution)/shard_map/ppermute | solution.py:226
  16.6 20.6 %collective-permute-start.64 = (bf16[16,8192]{1,0:T(8,128)(2,1)S(1)}, bf16[16,8192]{1,0:T(8,128)(2,1)S(1)}, u32[]{:S(2)}, u32[]{:S(2)}) collective-permute-start(bf16[16,8192]{1,0:T(8,128)(2,1)S(1)} %get-tuple-element.753), channel_id=1, source_target_pairs={{0,12},{1,13},{2,14},{3,15},{4,8},{5,9},{6,10},{7,11},{8,4},{9,5},... | collective-permute-start | bytes 786440 | tf_op jit(solution)/shard_map/ppermute | solution.py:226
  16.8 20.4 %collective-permute-start.65 = (bf16[16,8192]{1,0:T(8,128)(2,1)S(1)}, bf16[16,8192]{1,0:T(8,128)(2,1)}, u32[]{:S(2)}, u32[]{:S(2)}) collective-permute-start(bf16[16,8192]{1,0:T(8,128)(2,1)S(1)} %get-tuple-element.754), channel_id=1, source_target_pairs={{0,4},{1,5},{2,6},{3,7},{4,0},{5,1},{6,2},{7,3},{8,12},{9,13},{10,... | collective-permute-start | bytes 786440 | tf_op jit(solution)/shard_map/ppermute | solution.py:226
  21.8 11.2 %collective-permute-start.61 = (s32[1,128]{1,0:T(1,128)}, s32[1,128]{1,0:T(1,128)S(1)}, u32[]{:S(2)}, u32[]{:S(2)}) collective-permute-start(s32[1,128]{1,0:T(1,128)} %shard_map.75), channel_id=1, source_target_pairs={{0,2},{1,3},{2,0},{3,1},{4,6},{5,7},{6,4},{7,5},{8,10},{9,11},{10,... | collective-permute-start | bytes 1544 | tf_op jit(solution)/shard_map/ppermute | solution.py:226
  33.6 3.5 %collective-permute-start.62 = (s32[1,128]{1,0:T(1,128)S(1)}, s32[1,128]{1,0:T(1,128)S(1)}, u32[]{:S(2)}, u32[]{:S(2)}) collective-permute-start(s32[1,128]{1,0:T(1,128)S(1)} %max.6), channel_id=1, source_target_pairs={{0,16},{16,0},{1,17},{17,1},{2,18},{18,2},{3,19},{19,3},{4,20},{20... | collective-permute-start | bytes 1544 | tf_op jit(solution)/shard_map/ppermute | solution.py:226
  37.4 3.5 %copy-start.3 = (bf16[128,8192]{1,0:T(8,128)(2,1)}, bf16[128,8192]{1,0:T(8,128)(2,1)S(1)}, u32[]{:S(2)}) copy-start(bf16[128,8192]{1,0:T(8,128)(2,1)S(1)} %get-tuple-element.574.refs_0_) | copy-start | bytes 6291460 | tf_op jit(solution)/shard_map/conditional.1
  37.4 3.5 %copy-start.14 = (s32[2,128]{1,0:T(2,128)}, s32[2,128]{1,0:T(2,128)S(1)}, u32[]{:S(2)}) copy-start(s32[2,128]{1,0:T(2,128)S(1)} %get-tuple-element.1193) | copy-start | bytes 3076 | tf_op jit(solution)/shard_map/conditional.1
  37.6 11.0 %copy-start.31 = (s32[2]{0:T(128)S(1)}, s32[2]{0:T(128)}, u32[]{:S(2)}) copy-start(s32[2]{0:T(128)} %get-tuple-element.563) | copy-start | bytes 28 | tf_op jit(solution)/shard_map/conditional.1
  40.9 39.6 %collective-permute-start.11 = (bf16[56,4096]{1,0:T(8,128)(2,1)}, bf16[56,4096]{1,0:T(8,128)(2,1)}, u32[]{:S(2)}, u32[]{:S(2)}) collective-permute-start(bf16[56,4096]{1,0:T(8,128)(2,1)} %get-tuple-element.559), channel_id=1, source_target_pairs={{0,8},{1,9},{2,10},{3,11},{4,12},{5,13},{6,14},{7,15},{8,0},{9,1},... | collective-permute-start | bytes 1376264 | tf_op jit(solution)/shard_map/cond/branch_1_fun/ppermute | solution.py:226
  45.7 34.8 %collective-permute-start.12 = (bf16[56,4096]{1,0:T(8,128)(2,1)}, bf16[56,4096]{1,0:T(8,128)(2,1)}, u32[]{:S(2)}, u32[]{:S(2)}) collective-permute-start(bf16[56,4096]{1,0:T(8,128)(2,1)} %get-tuple-element.560), channel_id=1, source_target_pairs={{0,12},{1,13},{2,14},{3,15},{4,8},{5,9},{6,10},{7,11},{8,4},{9,5},... | collective-permute-start | bytes 1376264 | tf_op jit(solution)/shard_map/cond/branch_1_fun/ppermute | solution.py:226
  47.0 33.6 %collective-permute-start.13 = (bf16[56,4096]{1,0:T(8,128)(2,1)}, bf16[56,4096]{1,0:T(8,128)(2,1)}, u32[]{:S(2)}, u32[]{:S(2)}) collective-permute-start(bf16[56,4096]{1,0:T(8,128)(2,1)} %get-tuple-element.561), channel_id=1, source_target_pairs={{0,4},{1,5},{2,6},{3,7},{4,0},{5,1},{6,2},{7,3},{8,12},{9,13},{10,... | collective-permute-start | bytes 1376264 | tf_op jit(solution)/shard_map/cond/branch_1_fun/ppermute | solution.py:226
  48.0 8.8 %collective-permute-start.14 = (bf16[48,8192]{1,0:T(8,128)(2,1)S(1)}, bf16[48,8192]{1,0:T(8,128)(2,1)S(1)}, u32[]{:S(2)}, u32[]{:S(2)}) collective-permute-start(bf16[48,8192]{1,0:T(8,128)(2,1)S(1)} %constant_dynamic-update-slice_fusion.6.refs_1_), channel_id=1, source_target_pairs={{0,1},{1,0},{2,3},{3,2},{4,5},{5,4},{6,7},{7,6},{8,9},{9,8},{10,11... | collective-permute-start | bytes 2359304 | tf_op jit(solution)/shard_map/cond/branch_1_fun/ppermute | solution.py:226
  48.1 26.2 %collective-permute-start.15 = (bf16[128,4096]{1,0:T(8,128)(2,1)}, bf16[128,4096]{1,0:T(8,128)(2,1)S(1)}, u32[]{:S(2)}, u32[]{:S(2)}) collective-permute-start(bf16[128,4096]{1,0:T(8,128)(2,1)} %get-tuple-element.572.refs_5_.refs_4_), channel_id=1, source_target_pairs={{0,2},{1,3},{2,0},{3,1},{4,6},{5,7},{6,4},{7,5},{8,10},{9,11},{10,... | collective-permute-start | bytes 3145736 | tf_op jit(solution)/shard_map/cond/branch_1_fun/ppermute | solution.py:226
  56.8 22.7 %collective-permute-start.17 = (bf16[256,512]{1,0:T(8,128)(2,1)S(1)}, bf16[256,512]{1,0:T(8,128)(2,1)S(1)}, u32[]{:S(2)}, u32[]{:S(2)}) collective-permute-start(bf16[256,512]{1,0:T(8,128)(2,1)S(1)} %pad_maximum_fusion.1), channel_id=1, source_target_pairs={{0,2},{1,3},{2,0},{3,1},{4,6},{5,7},{6,4},{7,5},{8,10},{9,11},{10,... | collective-permute-start | bytes 786440 | tf_op jit(solution)/shard_map/cond/branch_1_fun/ppermute | solution.py:226
  58.4 4.7 %copy-start.4 = (bf16[128,8192]{1,0:T(8,128)(2,1)S(1)}, bf16[128,8192]{1,0:T(8,128)(2,1)}, u32[]{:S(2)}) copy-start(bf16[128,8192]{1,0:T(8,128)(2,1)} %copy-done.3) | copy-start | bytes 6291460 | tf_op jit(solution)/shard_map/conditional.1
  77.4 3.2 %copy-start.27 = (s32[168,1]{0,1:T(1,128)S(1)}, s32[168,1]{0,1:T(1,128)}, u32[]{:S(2)}) copy-start(s32[168,1]{0,1:T(1,128)} %pad_add_fusion.3) | copy-start | bytes 2020 | tf_op jit(solution)/shard_map/conditional.1
  77.4 2.1 %collective-permute-start.16 = (f32[176,64]{1,0:T(8,128)S(1)}, f32[176,64]{1,0:T(8,128)S(1)}, u32[]{:S(2)}, u32[]{:S(2)}) collective-permute-start(f32[176,64]{1,0:T(8,128)S(1)} %get-tuple-element.1267), channel_id=1, source_target_pairs={{0,1},{1,0},{2,3},{3,2},{4,5},{5,4},{6,7},{7,6},{8,9},{9,8},{10,11... | collective-permute-start | bytes 135176 | tf_op jit(solution)/shard_map/cond/branch_1_fun/ppermute | solution.py:226
  80.7 4.3 %copy-start.15 = (s32[2,128]{1,0:T(2,128)S(1)}, s32[2,128]{1,0:T(2,128)}, u32[]{:S(2)}) copy-start(s32[2,128]{1,0:T(2,128)} %copy-done.14) | copy-start | bytes 3076 | tf_op jit(solution)/shard_map/conditional.1
  84.9 1.3 %collective-permute-start.18 = (f32[168,64]{1,0:T(8,128)S(1)}, f32[168,64]{1,0:T(8,128)S(1)}, u32[]{:S(2)}, u32[]{:S(2)}) collective-permute-start(f32[168,64]{1,0:T(8,128)S(1)} %branch_1_fun.10.one_ref), channel_id=1, source_target_pairs={{0,1},{1,0},{2,3},{3,2},{4,5},{5,4},{6,7},{7,6},{8,9},{9,8},{10,11... | collective-permute-start | bytes 129032 | tf_op jit(solution)/shard_map/cond/branch_1_fun/ppermute | solution.py:226
  87.1 7.5 %collective-permute-start.20 = (bf16[48,512]{1,0:T(8,128)(2,1)S(1)}, bf16[48,512]{1,0:T(8,128)(2,1)S(1)}, u32[]{:S(2)}, u32[]{:S(2)}) collective-permute-start(bf16[48,512]{1,0:T(8,128)(2,1)S(1)} %get-tuple-element.588), channel_id=1, source_target_pairs={{0,12},{1,13},{2,14},{3,15},{4,8},{5,9},{6,10},{7,11},{8,4},{9,5},... | collective-permute-start | bytes 147464 | tf_op jit(solution)/shard_map/cond/branch_1_fun/ppermute | solution.py:226
  89.8 8.8 %collective-permute-start.19 = (bf16[48,512]{1,0:T(8,128)(2,1)S(1)}, bf16[48,512]{1,0:T(8,128)(2,1)S(1)}, u32[]{:S(2)}, u32[]{:S(2)}) collective-permute-start(bf16[48,512]{1,0:T(8,128)(2,1)S(1)} %get-tuple-element.587), channel_id=1, source_target_pairs={{0,8},{1,9},{2,10},{3,11},{4,12},{5,13},{6,14},{7,15},{8,0},{9,1},... | collective-permute-start | bytes 147464 | tf_op jit(solution)/shard_map/cond/branch_1_fun/ppermute | solution.py:226
  94.6 4.2 %collective-permute-start.21 = (bf16[48,512]{1,0:T(8,128)(2,1)S(1)}, bf16[48,512]{1,0:T(8,128)(2,1)S(1)}, u32[]{:S(2)}, u32[]{:S(2)}) collective-permute-start(bf16[48,512]{1,0:T(8,128)(2,1)S(1)} %get-tuple-element.589), channel_id=1, source_target_pairs={{0,4},{1,5},{2,6},{3,7},{4,0},{5,1},{6,2},{7,3},{8,12},{9,13},{10,... | collective-permute-start | bytes 147464 | tf_op jit(solution)/shard_map/cond/branch_1_fun/ppermute | solution.py:226
  (2 other events, 1.2 us)

commit v7 on v5

--- a/solution.py
+++ b/solution.py
@@ -345,8 +345,8 @@
                 arrived = [send(x, k) for x, k in zip(packed, flips)]
                 last_down = swap(near_down, 2)
                 down = [kept_down, near_down, far_down, last_down]
-                up = jnp.concatenate([up, mate_up], axis=0)
-                up = jnp.concatenate([up, swap(up, 2)], axis=0)
+                far_up = swap(up, 2)
+                up = jnp.concatenate([up, mate_up, far_up, swap(far_up, 1)], axis=0)
                 first_mine = jnp.concatenate(first_arrived, axis=0)
                 first_mate = swap(first_mine, 1)
 

time: 100 us -> 113 us (1.13)
  waiting for transfers between devices: 29.3 us -> 41.5 us
  local copies, waits for them, and re-layouts: 8.37 us -> 12.3 us
  other arithmetic: 10.2 us -> 6.41 us
    ppermute x23 -> x24, waiting for transfers between devices: 29.3 us -> 41.5 us  [flipped(): return lax.ppermute(x, axis, [(i, i ^ flip) for i in range(size)])]
    another operation x18 -> x27, local copies, waits for them, and re-layouts: 0.99 us -> 4.34 us
    reduce_sum x8, other arithmetic: 2.11 us -> 0.91 us  [named_by(): jnp.sum(jnp.where(hot, column.reshape(1, -1) + 1, 0), 1, keepdims=True) - 1]
    sub x9, other arithmetic: 1.18 us -> 0.05 us  [named_by(): jnp.sum(jnp.where(hot, column.reshape(1, -1) + 1, 0), 1, keepdims=True) - 1]
    ppermute x23 -> x24, starting transfers between devices: 24.7 us -> 25 us  [flipped(): return lax.ppermute(x, axis, [(i, i ^ flip) for i in range(size)])]
  transfers between devices with their start and end apart: 23 -> 24, of which waited for: 9 -> 11; matrix products, arithmetic and copies ran while one was open for 22% -> 18% of each run, Pallas kernels for 12% -> 10%
where the time goes in v7:
time: 113 us
  waiting for transfers between devices  41.5 us (37%)
  starting transfers between devices  25 us (22%)
  Pallas kernels  20 us (18%)
  local copies, waits for them, and re-layouts  12.3 us (11%)
  other arithmetic  6.41 us (6%)
  matrix products  6.09 us (5%)
  loops' own time  1.29 us (1%)
    ppermute x24, waiting for transfers between devices, flipped(): return lax.ppermute(x, axis, [(i, i ^ flip) for i in range(size)])  41.5 us
    ppermute x24, starting transfers between devices, flipped(): return lax.ppermute(x, axis, [(i, i ^ flip) for i in range(size)])  25 us
    pallas_call x3, Pallas kernels, shrink(): pl.pallas_call(functools.partial(shrink_body, len(xs), len(ws), rank, sta...  11.9 us
    pallas_call x2, Pallas kernels, pack(): pl.pallas_call(functools.partial(pack_body, flips, number, start), grid_s...  4.86 us
    dot_general x1, matrix products, branch(): base = jnp.dot(tokens, matrix, preferred_element_type=jnp.float32)  4.76 us
    dynamic_slice x2, local copies, waits for them, and re-layouts, local(): half_of = lambda x, c: lax.dynamic_slice_in_dim(x, c * half, half, axis=1)  4.62 us
    another operation x27, local copies, waits for them, and re-layouts  4.34 us
  transfers between devices with their start and end apart: 24, of which 11 were waited for; matrix products, arithmetic and copies ran while one was open for 18% of the time, Pallas kernels for 10%

profile of v7, /device:TPU:0, one launch (start us, length us, event | category | flops | bytes accessed | tf_op | source)
XLA Modules:
  0.0 112.9 jit_solution(16837807700294079670)
XLA Ops:
  1.6 3.1 %collective-permute-start.60 = (s32[1,128]{1,0:T(1,128)S(1)}, s32[1,128]{1,0:T(1,128)S(1)}, u32[]{:S(2)}, u32[]{:S(2)}) collective-permute-start(s32[1,128]{1,0:T(1,128)S(1)} %get-tuple-element.1424), channel_id=1, source_target_pairs={{0,4},{1,5},{2,6},{3,7},{4,0},{5,1},{6,2},{7,3},{8,12},{9,13},{10,... | collective-permute-start | bytes 1544 | tf_op jit(solution)/shard_map/ppermute | solution.py:226
  4.7 2.3 %constant_dynamic-slice_fusion.1 = bf16[128,4096]{1,0:T(8,128)(2,1)} fusion(bf16[128,8192]{1,0:T(8,128)(2,1)} %bitcast.957, s32[]{:T(128)S(6)} %select_n.2050), kind=kLoop, calls=%fused_computation.1336 | loop fusion | bytes 2097156 | tf_op jit(solution)/shard_map/dynamic_slice | solution.py:273
  7.0 1.5 %collective-permute-start.71 = (bf16[128,4096]{1,0:T(8,128)(2,1)}, bf16[128,4096]{1,0:T(8,128)(2,1)}, u32[]{:S(2)}, u32[]{:S(2)}) collective-permute-start(bf16[128,4096]{1,0:T(8,128)(2,1)} %constant_dynamic-slice_fusion.1), channel_id=1, source_target_pairs={{0,2},{1,3},{2,0},{3,1},{4,6},{5,7},{6,4},{7,5},{8,10},{9,11},{10,... | collective-permute-start | bytes 3145736 | tf_op jit(solution)/shard_map/ppermute | solution.py:226
  9.3 2.7 %collective-permute-start.61 = (s32[2,128]{1,0:T(2,128)S(1)}, s32[2,128]{1,0:T(2,128)S(1)}, u32[]{:S(2)}, u32[]{:S(2)}) collective-permute-start(s32[2,128]{1,0:T(2,128)S(1)} %pad_add_fusion.17), channel_id=1, source_target_pairs={{0,8},{1,9},{2,10},{3,11},{4,12},{5,13},{6,14},{7,15},{8,0},{9,1},... | collective-permute-start | bytes 3080 | tf_op jit(solution)/shard_map/ppermute | solution.py:226
  11.9 1.7 %shard_map.74 = (bf16[16,8192]{1,0:T(8,128)(2,1)S(1)}, bf16[16,8192]{1,0:T(8,128)(2,1)S(1)}, bf16[16,8192]{1,0:T(8,128)(2,1)S(1)}) custom-call(s32[3]{0:T(128)S(1)} %pad_add_fusion.18.place_ref, s32[1,128]{1,0:T(1,128)S(1)} %get-tuple-element.1423.goes_ref, s32[1,128]{1,0:T(1,128)S(1)} %bitcast.949, bf16[128,8192]{1,0:T(8,128)(2,1)S(1)} %copy-done.15), custom_call_target="tpu_custom_call" | custom-call | flops 100663296 | bytes 2883584 | tf_op jit(solution)/shard_map/pallas_call | solution.py:90
  14.5 2.5 %collective-permute-start.68 = (bf16[16,8192]{1,0:T(8,128)(2,1)S(1)}, bf16[16,8192]{1,0:T(8,128)(2,1)S(1)}, u32[]{:S(2)}, u32[]{:S(2)}) collective-permute-start(bf16[16,8192]{1,0:T(8,128)(2,1)S(1)} %get-tuple-element.752), channel_id=1, source_target_pairs={{0,12},{1,13},{2,14},{3,15},{4,8},{5,9},{6,10},{7,11},{8,4},{9,5},... | collective-permute-start | bytes 786440 | tf_op jit(solution)/shard_map/ppermute | solution.py:226
  17.1 1.8 %collective-permute-start.70 = (bf16[16,8192]{1,0:T(8,128)(2,1)S(1)}, bf16[16,8192]{1,0:T(8,128)(2,1)}, u32[]{:S(2)}, u32[]{:S(2)}) collective-permute-start(bf16[16,8192]{1,0:T(8,128)(2,1)S(1)} %get-tuple-element.754), channel_id=1, source_target_pairs={{0,4},{1,5},{2,6},{3,7},{4,0},{5,1},{6,2},{7,3},{8,12},{9,13},{10,... | collective-permute-start | bytes 786440 | tf_op jit(solution)/shard_map/ppermute | solution.py:226
  18.9 2.3 %constant_dynamic-slice_fusion = bf16[128,4096]{1,0:T(8,128)(2,1)} fusion(bf16[128,8192]{1,0:T(8,128)(2,1)} %collective-permute-done.63, s32[]{:T(128)S(6)} %select_n.2050), kind=kLoop, calls=%fused_computation.1335 | loop fusion | bytes 2097156 | tf_op jit(solution)/shard_map/dynamic_slice | solution.py:273
  21.8 1.4 %shard_map.75 = s32[1,128]{1,0:T(1,128)} custom-call(s32[3]{0:T(128)S(1)} %pad_add_fusion.18.place_ref, s32[4,128]{1,0:T(4,128)} %copy-done.38, s32[4,128]{1,0:T(4,128)} %copy-done.44), custom_call_target="tpu_custom_call" | custom-call | tf_op jit(solution)/shard_map/pallas_call | solution.py:43
  24.4 8.5 %collective-permute-done.66 = s32[1,128]{1,0:T(1,128)S(1)} collective-permute-done((s32[1,128]{1,0:T(1,128)}, s32[1,128]{1,0:T(1,128)S(1)}, u32[]{:S(2)}, u32[]{:S(2)}) %collective-permute-start.66) | collective-permute-done | bytes 544 | tf_op jit(solution)/shard_map/ppermute | solution.py:226
  33.5 1.5 %collective-permute-start.67 = (s32[1,128]{1,0:T(1,128)S(1)}, s32[1,128]{1,0:T(1,128)S(1)}, u32[]{:S(2)}, u32[]{:S(2)}) collective-permute-start(s32[1,128]{1,0:T(1,128)S(1)} %max.6), channel_id=1, source_target_pairs={{0,16},{16,0},{1,17},{17,1},{2,18},{18,2},{3,19},{19,3},{4,20},{20... | collective-permute-start | bytes 1544 | tf_op jit(solution)/shard_map/ppermute | solution.py:226
  35.7 1.4 %collective-permute-done.67 = s32[1,128]{1,0:T(1,128)S(1)} collective-permute-done((s32[1,128]{1,0:T(1,128)S(1)}, s32[1,128]{1,0:T(1,128)S(1)}, u32[]{:S(2)}, u32[]{:S(2)}) %collective-permute-start.67) | collective-permute-done | bytes 544 | tf_op jit(solution)/shard_map/ppermute | solution.py:226
  37.1 3.7 %collective-permute-done.69 = bf16[16,8192]{1,0:T(8,128)(2,1)S(1)} collective-permute-done((bf16[16,8192]{1,0:T(8,128)(2,1)S(1)}, bf16[16,8192]{1,0:T(8,128)(2,1)S(1)}, u32[]{:S(2)}, u32[]{:S(2)}) %collective-permute-start.69) | collective-permute-done | bytes 262176 | tf_op jit(solution)/shard_map/ppermute | solution.py:226
  40.9 71.9 %conditional.3 = (bf16[128,512]{1,0:T(8,128)(2,1)}) conditional(s32[]{:T(128)} %bitcast.187, (s32[]{:T(128)}, s32[]{:T(128)}, s32[2,128]{1,0:T(2,128)S(1)}, pred[2,128]{1,0:T(4,128)(4,1)S(1)}, pred[2,128]{1,0:T(4,128)(4,1)S(1)}, /*index=5*/s32[2,128]{1,0:T(2,128)S(1)}, s32[2,128]{1,0:T(2,128)S(1)}, ...), branch_computations={%region_2.12_spmd, %region_12.22_spmd, %region_22.32_spmd, %region... | conditional | flops 4555838464 | bytes 83885776
  41.9 3.2 %branch_1_fun.6 = (bf16[56,4096]{1,0:T(8,128)(2,1)}, bf16[56,4096]{1,0:T(8,128)(2,1)}, bf16[56,4096]{1,0:T(8,128)(2,1)S(1)}) custom-call(s32[3]{0:T(128)S(1)} %pad_add_fusion.5.place_ref, s32[2,128]{1,0:T(2,128)S(1)} %get-tuple-element.1215.goes_ref, s32[2,128]{1,0:T(2,128)S(1)} %get-tuple-element.1281.within_ref, ...), custom_call_target="tpu_custom_call" | custom-call | flops 352321536 | bytes 3473408 | tf_op jit(solution)/shard_map/cond/branch_1_fun/pallas_call | solution.py:90
  45.1 2.7 %collective-permute-start.12 = (bf16[56,4096]{1,0:T(8,128)(2,1)}, bf16[56,4096]{1,0:T(8,128)(2,1)}, u32[]{:S(2)}, u32[]{:S(2)}) collective-permute-start(bf16[56,4096]{1,0:T(8,128)(2,1)} %get-tuple-element.559), channel_id=1, source_target_pairs={{0,12},{1,13},{2,14},{3,15},{4,8},{5,9},{6,10},{7,11},{8,4},{9,5},... | collective-permute-start | bytes 1376264 | tf_op jit(solution)/shard_map/cond/branch_1_fun/ppermute | solution.py:226
  47.8 1.0 constant_dynamic-update-slice_fusion.7.refs_1_
  49.5 1.5 %collective-permute-start.18 = (bf16[128,512]{1,0:T(8,128)(2,1)S(1)}, bf16[128,512]{1,0:T(8,128)(2,1)}, u32[]{:S(2)}, u32[]{:S(2)}) collective-permute-start(bf16[128,512]{1,0:T(8,128)(2,1)S(1)} %get-tuple-element.579), channel_id=1, source_target_pairs={{0,2},{1,3},{2,0},{3,1},{4,6},{5,7},{6,4},{7,5},{8,10},{9,11},{10,... | collective-permute-start | bytes 393224 | tf_op jit(solution)/shard_map/cond/branch_1_fun/ppermute | solution.py:226
  55.2 0.9 constant_dynamic-update-slice_fusion.12
  56.1 21.4 %collective-permute-done.18 = bf16[128,512]{1,0:T(8,128)(2,1)} collective-permute-done((bf16[128,512]{1,0:T(8,128)(2,1)S(1)}, bf16[128,512]{1,0:T(8,128)(2,1)}, u32[]{:S(2)}, u32[]{:S(2)}) %collective-permute-start.18) | collective-permute-done | bytes 131104 | tf_op jit(solution)/shard_map/cond/branch_1_fun/ppermute | solution.py:226
  77.6 1.7 %collective-permute-start.14 = (bf16[56,4096]{1,0:T(8,128)(2,1)}, bf16[56,4096]{1,0:T(8,128)(2,1)S(1)}, u32[]{:S(2)}, u32[]{:S(2)}) collective-permute-start(bf16[56,4096]{1,0:T(8,128)(2,1)} %copy-done.13), channel_id=1, source_target_pairs={{0,4},{1,5},{2,6},{3,7},{4,0},{5,1},{6,2},{7,3},{8,12},{9,13},{10,... | collective-permute-start | bytes 1376264 | tf_op jit(solution)/shard_map/cond/branch_1_fun/ppermute | solution.py:226
  80.3 4.6 %branch_1_fun.7 = f32[352,64]{1,0:T(8,128)S(1)} custom-call(s32[3]{0:T(128)S(1)} %get-tuple-element.567.place_ref, bf16[128,8192]{1,0:T(8,128)(2,1)} %copy-done.18, bf16[48,8192]{1,0:T(8,128)(2,1)S(1)} %constant_dynamic-update-slice_fusion.7.refs_1_, bf16[128,8192]{1,0:T(8,128)(2,1)} %get-tuple-element.550.refs_1_.refs_2_, ...), custom_call_target="tpu_custom_call" | custom-call | flops 1107296256 | bytes 6029312 | tf_op jit(solution)/shard_map/cond/branch_1_fun/pallas_call | solution.py:147
  85.0 4.8 %fusion.289 = f32[128,512]{1,0:T(8,128)S(1)} fusion(bf16[128,8192]{1,0:T(8,128)(2,1)S(1)} %copy-done.19, bf16[8192,512]{1,0:T(8,128)(2,1)} %get-tuple-element.794), kind=kOutput, calls=%fused_computation.1343 | convolution fusion | flops 1073741824 | bytes 10747904 | tf_op jit(solution)/shard_map/cond/branch_1_fun/dot_general | solution.py:381
  89.8 3.0 %branch_1_fun.8 = f32[352,64]{1,0:T(8,128)S(1)} custom-call(s32[3]{0:T(128)S(1)} %get-tuple-element.567.place_ref, bf16[128,8192]{1,0:T(8,128)(2,1)S(1)} %copy-done.19, bf16[48,8192]{1,0:T(8,128)(2,1)S(1)} %constant_dynamic-update-slice_fusion.7.refs_1_, bf16[128,8192]{1,0:T(8,128)(2,1)} %get-tuple-element.550.refs_1_.refs_2_, ...), custom_call_target="tpu_custom_call" | custom-call | flops 369098752 | bytes 3932160 | tf_op jit(solution)/shard_map/cond/branch_1_fun/pallas_call | solution.py:147
  93.5 0.9 collective-permute-done.17.two_ref
  94.4 0.9 branch_1_fun.9
  96.8 1.0 copy-done.7
  97.8 4.2 %branch_1_fun.10.one_ref = f32[168,64]{1,0:T(8,128)S(1)} custom-call(s32[3]{0:T(128)S(1)} %get-tuple-element.567.place_ref, bf16[56,4096]{1,0:T(8,128)(2,1)} %collective-permute-done.12.refs_0_, bf16[56,4096]{1,0:T(8,128)(2,1)} %collective-permute-done.13.refs_1_, bf16[56,4096]{1,0:T(8,128)(2,1)S(1)} %copy-done.7, ...), custom_call_target="tpu_custom_call" | custom-call | flops 704643072 | bytes 5570560 | tf_op jit(solution)/shard_map/cond/branch_1_fun/pallas_call | solution.py:147
  102.1 1.2 %collective-permute-done.20.two_ref = f32[168,64]{1,0:T(8,128)S(1)} collective-permute-done((f32[168,64]{1,0:T(8,128)S(1)}, f32[168,64]{1,0:T(8,128)S(1)}, u32[]{:S(2)}, u32[]{:S(2)}) %collective-permute-start.20) | collective-permute-done | bytes 43040 | tf_op jit(solution)/shard_map/cond/branch_1_fun/ppermute | solution.py:226
  105.0 1.5 %collective-permute-start.21 = (bf16[48,512]{1,0:T(8,128)(2,1)S(1)}, bf16[48,512]{1,0:T(8,128)(2,1)S(1)}, u32[]{:S(2)}, u32[]{:S(2)}) collective-permute-start(bf16[48,512]{1,0:T(8,128)(2,1)S(1)} %get-tuple-element.587), channel_id=1, source_target_pairs={{0,12},{1,13},{2,14},{3,15},{4,8},{5,9},{6,10},{7,11},{8,4},{9,5},... | collective-permute-start | bytes 147464 | tf_op jit(solution)/shard_map/cond/branch_1_fun/ppermute | solution.py:226
  106.6 1.2 %collective-permute-start.23 = (bf16[48,512]{1,0:T(8,128)(2,1)S(1)}, bf16[48,512]{1,0:T(8,128)(2,1)S(1)}, u32[]{:S(2)}, u32[]{:S(2)}) collective-permute-start(bf16[48,512]{1,0:T(8,128)(2,1)S(1)} %get-tuple-element.589), channel_id=1, source_target_pairs={{0,4},{1,5},{2,6},{3,7},{4,0},{5,1},{6,2},{7,3},{8,12},{9,13},{10,... | collective-permute-start | bytes 147464 | tf_op jit(solution)/shard_map/cond/branch_1_fun/ppermute | solution.py:226
  107.8 2.6 %collective-permute-done.22 = bf16[48,512]{1,0:T(8,128)(2,1)S(1)} collective-permute-done((bf16[48,512]{1,0:T(8,128)(2,1)S(1)}, bf16[48,512]{1,0:T(8,128)(2,1)S(1)}, u32[]{:S(2)}, u32[]{:S(2)}) %collective-permute-start.22) | collective-permute-done | bytes 49184 | tf_op jit(solution)/shard_map/cond/branch_1_fun/ppermute | solution.py:226
  (121 shorter events, 18.4 us)
Async XLA Ops:
  0.0 11.9 %copy-start.15 = (bf16[128,8192]{1,0:T(8,128)(2,1)S(1)}, bf16[128,8192]{1,0:T(8,128)(2,1)}, u32[]{:S(2)}) copy-start(bf16[128,8192]{1,0:T(8,128)(2,1)} %refs_0_.1) | copy-start | bytes 6291460
  0.0 13.8 %collective-permute-start.62 = (bf16[128,8192]{1,0:T(8,128)(2,1)}, bf16[128,8192]{1,0:T(8,128)(2,1)}, u32[]{:S(2)}, u32[]{:S(2)}) collective-permute-start(bf16[128,8192]{1,0:T(8,128)(2,1)} %refs_0_.1), channel_id=1, source_target_pairs={{0,1},{1,0},{2,3},{3,2},{4,5},{5,4},{6,7},{7,6},{8,9},{9,8},{10,11... | collective-permute-start | bytes 6291464 | tf_op jit(solution)/shard_map/ppermute | solution.py:226
  0.5 13.4 %collective-permute-start.63 = (bf16[128,8192]{1,0:T(8,128)(2,1)}, bf16[128,8192]{1,0:T(8,128)(2,1)}, u32[]{:S(2)}, u32[]{:S(2)}) collective-permute-start(bf16[128,8192]{1,0:T(8,128)(2,1)} %bitcast.956), channel_id=1, source_target_pairs={{0,1},{1,0},{2,3},{3,2},{4,5},{5,4},{6,7},{7,6},{8,9},{9,8},{10,11... | collective-permute-start | bytes 6291464 | tf_op jit(solution)/shard_map/ppermute | solution.py:226
  1.6 7.7 %collective-permute-start.60 = (s32[1,128]{1,0:T(1,128)S(1)}, s32[1,128]{1,0:T(1,128)S(1)}, u32[]{:S(2)}, u32[]{:S(2)}) collective-permute-start(s32[1,128]{1,0:T(1,128)S(1)} %get-tuple-element.1424), channel_id=1, source_target_pairs={{0,4},{1,5},{2,6},{3,7},{4,0},{5,1},{6,2},{7,3},{8,12},{9,13},{10,... | collective-permute-start | bytes 1544 | tf_op jit(solution)/shard_map/ppermute | solution.py:226
  4.7 9.1 %collective-permute-start.64 = (bf16[128,512]{1,0:T(8,128)(2,1)}, bf16[128,512]{1,0:T(8,128)(2,1)S(1)}, u32[]{:S(2)}, u32[]{:S(2)}) collective-permute-start(bf16[128,512]{1,0:T(8,128)(2,1)} %bitcast.950), channel_id=1, source_target_pairs={{0,1},{1,0},{2,3},{3,2},{4,5},{5,4},{6,7},{7,6},{8,9},{9,8},{10,11... | collective-permute-start | bytes 393224 | tf_op jit(solution)/shard_map/ppermute | solution.py:226
  7.0 30.1 %collective-permute-start.71 = (bf16[128,4096]{1,0:T(8,128)(2,1)}, bf16[128,4096]{1,0:T(8,128)(2,1)}, u32[]{:S(2)}, u32[]{:S(2)}) collective-permute-start(bf16[128,4096]{1,0:T(8,128)(2,1)} %constant_dynamic-slice_fusion.1), channel_id=1, source_target_pairs={{0,2},{1,3},{2,0},{3,1},{4,6},{5,7},{6,4},{7,5},{8,10},{9,11},{10,... | collective-permute-start | bytes 3145736 | tf_op jit(solution)/shard_map/ppermute | solution.py:226
  9.3 4.5 %collective-permute-start.61 = (s32[2,128]{1,0:T(2,128)S(1)}, s32[2,128]{1,0:T(2,128)S(1)}, u32[]{:S(2)}, u32[]{:S(2)}) collective-permute-start(s32[2,128]{1,0:T(2,128)S(1)} %pad_add_fusion.17), channel_id=1, source_target_pairs={{0,8},{1,9},{2,10},{3,11},{4,12},{5,13},{6,14},{7,15},{8,0},{9,1},... | collective-permute-start | bytes 3080 | tf_op jit(solution)/shard_map/ppermute | solution.py:226
  11.9 29.0 %copy-start.26 = (bf16[2,64,512]{2,1,0:T(8,128)(2,1)S(1)}, bf16[2,64,512]{2,1,0:T(8,128)(2,1)}, u32[]{:S(2)}) copy-start(bf16[2,64,512]{2,1,0:T(8,128)(2,1)} %param.16) | copy-start | bytes 393220
  13.8 7.4 %copy-start.38 = (s32[4,128]{1,0:T(4,128)}, s32[4,128]{1,0:T(4,128)S(1)}, u32[]{:S(2)}) copy-start(s32[4,128]{1,0:T(4,128)S(1)} %pad_add_fusion.16.mine_ref) | copy-start | bytes 6148
  14.5 6.7 %collective-permute-start.65 = (s32[4,128]{1,0:T(4,128)S(1)}, s32[4,128]{1,0:T(4,128)S(1)}, u32[]{:S(2)}, u32[]{:S(2)}) collective-permute-start(s32[4,128]{1,0:T(4,128)S(1)} %pad_add_fusion.16.mine_ref), channel_id=1, source_target_pairs={{0,1},{1,0},{2,3},{3,2},{4,5},{5,4},{6,7},{7,6},{8,9},{9,8},{10,11... | collective-permute-start | bytes 6152 | tf_op jit(solution)/shard_map/ppermute | solution.py:226
  14.5 22.7 %collective-permute-start.68 = (bf16[16,8192]{1,0:T(8,128)(2,1)S(1)}, bf16[16,8192]{1,0:T(8,128)(2,1)S(1)}, u32[]{:S(2)}, u32[]{:S(2)}) collective-permute-start(bf16[16,8192]{1,0:T(8,128)(2,1)S(1)} %get-tuple-element.752), channel_id=1, source_target_pairs={{0,12},{1,13},{2,14},{3,15},{4,8},{5,9},{6,10},{7,11},{8,4},{9,5},... | collective-permute-start | bytes 786440 | tf_op jit(solution)/shard_map/ppermute | solution.py:226
  17.0 23.9 %collective-permute-start.69 = (bf16[16,8192]{1,0:T(8,128)(2,1)S(1)}, bf16[16,8192]{1,0:T(8,128)(2,1)S(1)}, u32[]{:S(2)}, u32[]{:S(2)}) collective-permute-start(bf16[16,8192]{1,0:T(8,128)(2,1)S(1)} %get-tuple-element.753), channel_id=1, source_target_pairs={{0,8},{1,9},{2,10},{3,11},{4,12},{5,13},{6,14},{7,15},{8,0},{9,1},... | collective-permute-start | bytes 786440 | tf_op jit(solution)/shard_map/ppermute | solution.py:226
  17.1 23.8 %collective-permute-start.70 = (bf16[16,8192]{1,0:T(8,128)(2,1)S(1)}, bf16[16,8192]{1,0:T(8,128)(2,1)}, u32[]{:S(2)}, u32[]{:S(2)}) collective-permute-start(bf16[16,8192]{1,0:T(8,128)(2,1)S(1)} %get-tuple-element.754), channel_id=1, source_target_pairs={{0,4},{1,5},{2,6},{3,7},{4,0},{5,1},{6,2},{7,3},{8,12},{9,13},{10,... | collective-permute-start | bytes 786440 | tf_op jit(solution)/shard_map/ppermute | solution.py:226
  23.2 9.7 %collective-permute-start.66 = (s32[1,128]{1,0:T(1,128)}, s32[1,128]{1,0:T(1,128)S(1)}, u32[]{:S(2)}, u32[]{:S(2)}) collective-permute-start(s32[1,128]{1,0:T(1,128)} %shard_map.75), channel_id=1, source_target_pairs={{0,2},{1,3},{2,0},{3,1},{4,6},{5,7},{6,4},{7,5},{8,10},{9,11},{10,... | collective-permute-start | bytes 1544 | tf_op jit(solution)/shard_map/ppermute | solution.py:226
  33.5 3.5 %collective-permute-start.67 = (s32[1,128]{1,0:T(1,128)S(1)}, s32[1,128]{1,0:T(1,128)S(1)}, u32[]{:S(2)}, u32[]{:S(2)}) collective-permute-start(s32[1,128]{1,0:T(1,128)S(1)} %max.6), channel_id=1, source_target_pairs={{0,16},{16,0},{1,17},{17,1},{2,18},{18,2},{3,19},{19,3},{4,20},{20... | collective-permute-start | bytes 1544 | tf_op jit(solution)/shard_map/ppermute | solution.py:226
  41.1 8.3 %copy-start.30 = (s32[2,128]{1,0:T(2,128)}, s32[2,128]{1,0:T(2,128)S(1)}, u32[]{:S(2)}) copy-start(s32[2,128]{1,0:T(2,128)S(1)} %get-tuple-element.1193) | copy-start | bytes 3076 | tf_op jit(solution)/shard_map/conditional.1
  41.9 9.1 %copy-start.51 = (s32[2]{0:T(128)S(1)}, s32[2]{0:T(128)}, u32[]{:S(2)}) copy-start(s32[2]{0:T(128)} %get-tuple-element.563) | copy-start | bytes 28 | tf_op jit(solution)/shard_map/conditional.1
  41.9 9.1 %copy-start.40 = (s32[4,2,128]{2,1,0:T(2,128)S(1)}, s32[4,2,128]{2,1,0:T(2,128)}, u32[]{:S(2)}) copy-start(s32[4,2,128]{2,1,0:T(2,128)} %copy.153) | copy-start | bytes 12292 | tf_op jit(solution)/shard_map/conditional.1
  45.1 4.4 %copy-start.13 = (bf16[56,4096]{1,0:T(8,128)(2,1)}, bf16[56,4096]{1,0:T(8,128)(2,1)S(1)}, u32[]{:S(2)}) copy-start(bf16[56,4096]{1,0:T(8,128)(2,1)S(1)} %get-tuple-element.561) | copy-start | bytes 1376260 | tf_op jit(solution)/shard_map/conditional.1
  45.1 50.3 %collective-permute-start.12 = (bf16[56,4096]{1,0:T(8,128)(2,1)}, bf16[56,4096]{1,0:T(8,128)(2,1)}, u32[]{:S(2)}, u32[]{:S(2)}) collective-permute-start(bf16[56,4096]{1,0:T(8,128)(2,1)} %get-tuple-element.559), channel_id=1, source_target_pairs={{0,12},{1,13},{2,14},{3,15},{4,8},{5,9},{6,10},{7,11},{8,4},{9,5},... | collective-permute-start | bytes 1376264 | tf_op jit(solution)/shard_map/cond/branch_1_fun/ppermute | solution.py:226
  47.8 47.6 %collective-permute-start.13 = (bf16[56,4096]{1,0:T(8,128)(2,1)}, bf16[56,4096]{1,0:T(8,128)(2,1)}, u32[]{:S(2)}, u32[]{:S(2)}) collective-permute-start(bf16[56,4096]{1,0:T(8,128)(2,1)} %get-tuple-element.560), channel_id=1, source_target_pairs={{0,8},{1,9},{2,10},{3,11},{4,12},{5,13},{6,14},{7,15},{8,0},{9,1},... | collective-permute-start | bytes 1376264 | tf_op jit(solution)/shard_map/cond/branch_1_fun/ppermute | solution.py:226
  48.8 31.4 %collective-permute-start.15 = (bf16[48,8192]{1,0:T(8,128)(2,1)S(1)}, bf16[48,8192]{1,0:T(8,128)(2,1)S(1)}, u32[]{:S(2)}, u32[]{:S(2)}) collective-permute-start(bf16[48,8192]{1,0:T(8,128)(2,1)S(1)} %constant_dynamic-update-slice_fusion.7.refs_1_), channel_id=1, source_target_pairs={{0,1},{1,0},{2,3},{3,2},{4,5},{5,4},{6,7},{7,6},{8,9},{9,8},{10,11... | collective-permute-start | bytes 2359304 | tf_op jit(solution)/shard_map/cond/branch_1_fun/ppermute | solution.py:226
  48.9 40.9 %collective-permute-start.16 = (bf16[128,4096]{1,0:T(8,128)(2,1)}, bf16[128,4096]{1,0:T(8,128)(2,1)S(1)}, u32[]{:S(2)}, u32[]{:S(2)}) collective-permute-start(bf16[128,4096]{1,0:T(8,128)(2,1)} %get-tuple-element.572.refs_5_.refs_4_), channel_id=1, source_target_pairs={{0,2},{1,3},{2,0},{3,1},{4,6},{5,7},{6,4},{7,5},{8,10},{9,11},{10,... | collective-permute-start | bytes 3145736 | tf_op jit(solution)/shard_map/cond/branch_1_fun/ppermute | solution.py:226
  49.5 28.1 %collective-permute-start.18 = (bf16[128,512]{1,0:T(8,128)(2,1)S(1)}, bf16[128,512]{1,0:T(8,128)(2,1)}, u32[]{:S(2)}, u32[]{:S(2)}) collective-permute-start(bf16[128,512]{1,0:T(8,128)(2,1)S(1)} %get-tuple-element.579), channel_id=1, source_target_pairs={{0,2},{1,3},{2,0},{3,1},{4,6},{5,7},{6,4},{7,5},{8,10},{9,11},{10,... | collective-permute-start | bytes 393224 | tf_op jit(solution)/shard_map/cond/branch_1_fun/ppermute | solution.py:226
  77.6 18.3 %collective-permute-start.14 = (bf16[56,4096]{1,0:T(8,128)(2,1)}, bf16[56,4096]{1,0:T(8,128)(2,1)S(1)}, u32[]{:S(2)}, u32[]{:S(2)}) collective-permute-start(bf16[56,4096]{1,0:T(8,128)(2,1)} %copy-done.13), channel_id=1, source_target_pairs={{0,4},{1,5},{2,6},{3,7},{4,0},{5,1},{6,2},{7,3},{8,12},{9,13},{10,... | collective-permute-start | bytes 1376264 | tf_op jit(solution)/shard_map/cond/branch_1_fun/ppermute | solution.py:226
  80.3 13.2 %collective-permute-start.19 = (bf16[128,512]{1,0:T(8,128)(2,1)}, bf16[128,512]{1,0:T(8,128)(2,1)S(1)}, u32[]{:S(2)}, u32[]{:S(2)}) collective-permute-start(bf16[128,512]{1,0:T(8,128)(2,1)} %collective-permute-done.18), channel_id=1, source_target_pairs={{0,1},{1,0},{2,3},{3,2},{4,5},{5,4},{6,7},{7,6},{8,9},{9,8},{10,11... | collective-permute-start | bytes 393224 | tf_op jit(solution)/shard_map/cond/branch_1_fun/ppermute | solution.py:226
  80.3 4.7 %copy-start.19 = (bf16[128,8192]{1,0:T(8,128)(2,1)S(1)}, bf16[128,8192]{1,0:T(8,128)(2,1)}, u32[]{:S(2)}) copy-start(bf16[128,8192]{1,0:T(8,128)(2,1)} %copy-done.18) | copy-start | bytes 6291460 | tf_op jit(solution)/shard_map/conditional.1
  92.9 1.5 %collective-permute-start.17 = (f32[176,64]{1,0:T(8,128)S(1)}, f32[176,64]{1,0:T(8,128)S(1)}, u32[]{:S(2)}, u32[]{:S(2)}) collective-permute-start(f32[176,64]{1,0:T(8,128)S(1)} %get-tuple-element.1267), channel_id=1, source_target_pairs={{0,1},{1,0},{2,3},{3,2},{4,5},{5,4},{6,7},{7,6},{8,9},{9,8},{10,11... | collective-permute-start | bytes 135176 | tf_op jit(solution)/shard_map/cond/branch_1_fun/ppermute | solution.py:226
  102.0 1.3 %collective-permute-start.20 = (f32[168,64]{1,0:T(8,128)S(1)}, f32[168,64]{1,0:T(8,128)S(1)}, u32[]{:S(2)}, u32[]{:S(2)}) collective-permute-start(f32[168,64]{1,0:T(8,128)S(1)} %branch_1_fun.10.one_ref), channel_id=1, source_target_pairs={{0,1},{1,0},{2,3},{3,2},{4,5},{5,4},{6,7},{7,6},{8,9},{9,8},{10,11... | collective-permute-start | bytes 129032 | tf_op jit(solution)/shard_map/cond/branch_1_fun/ppermute | solution.py:226
  104.2 6.2 %collective-permute-start.22 = (bf16[48,512]{1,0:T(8,128)(2,1)S(1)}, bf16[48,512]{1,0:T(8,128)(2,1)S(1)}, u32[]{:S(2)}, u32[]{:S(2)}) collective-permute-start(bf16[48,512]{1,0:T(8,128)(2,1)S(1)} %get-tuple-element.588), channel_id=1, source_target_pairs={{0,8},{1,9},{2,10},{3,11},{4,12},{5,13},{6,14},{7,15},{8,0},{9,1},... | collective-permute-start | bytes 147464 | tf_op jit(solution)/shard_map/cond/branch_1_fun/ppermute | solution.py:226
  105.0 6.4 %collective-permute-start.21 = (bf16[48,512]{1,0:T(8,128)(2,1)S(1)}, bf16[48,512]{1,0:T(8,128)(2,1)S(1)}, u32[]{:S(2)}, u32[]{:S(2)}) collective-permute-start(bf16[48,512]{1,0:T(8,128)(2,1)S(1)} %get-tuple-element.587), channel_id=1, source_target_pairs={{0,12},{1,13},{2,14},{3,15},{4,8},{5,9},{6,10},{7,11},{8,4},{9,5},... | collective-permute-start | bytes 147464 | tf_op jit(solution)/shard_map/cond/branch_1_fun/ppermute | solution.py:226
  106.6 5.3 %collective-permute-start.23 = (bf16[48,512]{1,0:T(8,128)(2,1)S(1)}, bf16[48,512]{1,0:T(8,128)(2,1)S(1)}, u32[]{:S(2)}, u32[]{:S(2)}) collective-permute-start(bf16[48,512]{1,0:T(8,128)(2,1)S(1)} %get-tuple-element.589), channel_id=1, source_target_pairs={{0,4},{1,5},{2,6},{3,7},{4,0},{5,1},{6,2},{7,3},{8,12},{9,13},{10,... | collective-permute-start | bytes 147464 | tf_op jit(solution)/shard_map/cond/branch_1_fun/ppermute | solution.py:226
  (7 other events, 15.1 us)
